TPU v7x, 256 devices: a whole 4x4x8 slice. The times are simulated.
256 devices in a mesh: tm: 4 (over y), chan: 64 (over x, z, core).
Axes of the slice: x: 4, y: 4, z: 8, core: 2. Of those that a mesh axis runs over, the one named last changes fastest.
Arguments:
- records: bfloat16 [256, 2048, 256], P('tm', 'chan'), may hold values from -6 to 6
- pair_blocks: int32 [1024, 2], P('chan'), may hold values from 0 to 127, as said below
- pair_counts: int32 [64], P('chan'), may hold values from 1 to 16, as said below
Outputs:
- correlations: float32 [1024, 401, 256], P(('chan', 'tm'))
Inputs may be any that keep to these rules, and one draw needn't show every extreme that they name: `pair_blocks`: for owner o, every slot has 0 <= j - i < 8, j < 128, and block i among the channels of chan index o or o + 1. `pair_counts`: some owner has all its slots live in every draw.
All inputs are finite; a program needn't handle non-finite values.
Results may differ from a plain program's by a relative error of at most 0.0027.
Values may be sent and summed in bfloat16 or wider, within the bound.
No kernel may reach another device: no remote copies, remote signals or barrier semaphores. Data moves between devices by JAX's collectives and lax.ppermute only.
A program may use at most 128 MiB of HBM per device.

v0:
```python
import math

import jax
import jax.numpy as jnp
from jax import lax
from jax.sharding import PartitionSpec as P

LAGS = 401
BLK = 16


water_share = 0.1
tiny_eps = 1e-06


def shifted(block, axis, distance):
    devices = range(lax.axis_size(axis))
    route = [(i - distance, i) for i in devices if i - distance in devices]
    return lax.ppermute(block, axis, route)


def make_tables(length, lag_count, segments):
    bins = length // 2
    time_index = jnp.arange(bins, dtype=jnp.int32)[:, None]
    freq_index = jnp.arange(bins, dtype=jnp.int32)[None, :]
    radians = (time_index * freq_index % length).astype(jnp.float32) * (2.0 * math.pi / length)
    forward = jnp.concatenate([jnp.cos(radians), -jnp.sin(radians)], axis=1).astype(jnp.bfloat16)
    lag_shift = jnp.arange(lag_count, dtype=jnp.int32)[:, None] - (lag_count - 1) // 2
    lag_radians = (lag_shift * freq_index % length).astype(jnp.float32) * (2.0 * math.pi / length)
    weight = jnp.where(freq_index == 0, 1.0, 2.0).astype(jnp.float32) / math.sqrt(
        float(bins * segments)
    )
    backward = jnp.concatenate(
        [jnp.cos(lag_radians) * weight, -jnp.sin(lag_radians) * weight], axis=1
    )
    return (forward, backward)


def whiten(records, forward):
    spectra = jnp.einsum("sct,tf->scf", records, forward, preferred_element_type=jnp.float32)
    bins = spectra.shape[-1] // 2
    real_part = spectra[..., :bins]
    imag_part = spectra[..., bins:]
    energy = real_part * real_part + imag_part * imag_part
    water_level = jnp.mean(energy, axis=-1, keepdims=True)
    inverse_amp = 1.0 / jnp.sqrt(energy + water_share * water_level + tiny_eps)
    return jnp.concatenate([real_part * inverse_amp, imag_part * inverse_amp], axis=-1).astype(
        jnp.bfloat16
    )


def cross_spectrum(left_block, right_block):
    bins = left_block.shape[-1] // 2
    left_real = left_block[..., :bins]
    left_imag = left_block[..., bins:]
    right_real = right_block[..., :bins]
    right_imag = right_block[..., bins:]
    f32 = jnp.float32
    real_sum = jnp.einsum(
        "saf,sbf->fab", left_real, right_real, preferred_element_type=f32
    ) + jnp.einsum("saf,sbf->fab", left_imag, right_imag, preferred_element_type=f32)
    imag_sum = jnp.einsum(
        "saf,sbf->fab", left_imag, right_real, preferred_element_type=f32
    ) - jnp.einsum("saf,sbf->fab", left_real, right_imag, preferred_element_type=f32)
    return jnp.concatenate([real_sum.reshape(bins, -1), imag_sum.reshape(bins, -1)], axis=0)


def local(records, pair_blocks, pair_counts):
    length = 2 * records.shape[2]
    segments = records.shape[0] * lax.axis_size("tm")
    forward, backward = make_tables(length, LAGS, segments)
    owner_index = lax.axis_index("chan")
    own_spectra = whiten(records, forward)
    pieces = [own_spectra]
    for offset in range(1, 6):
        pieces.append(shifted(own_spectra, "chan", -offset))
    band_data = jnp.concatenate(pieces, axis=1)
    base_channel = owner_index * records.shape[1]
    live_count = pair_counts[0]

    def per_slot(slot_index):
        first_start = pair_blocks[slot_index, 0] * BLK - base_channel
        second_start = pair_blocks[slot_index, 1] * BLK - base_channel
        left_block = lax.dynamic_slice_in_dim(band_data, first_start, BLK, 1)
        right_block = lax.dynamic_slice_in_dim(band_data, second_start, BLK, 1)
        cross = cross_spectrum(left_block, right_block)
        return jnp.where(slot_index < live_count, cross, jnp.zeros_like(cross))

    cross_all = lax.map(per_slot, jnp.arange(pair_blocks.shape[0], dtype=jnp.int32))
    partial_value = jnp.einsum("lf,kfp->klp", backward, cross_all, precision=lax.Precision.HIGHEST)
    return lax.psum_scatter(partial_value, "tm", scatter_dimension=0, tiled=True)


def solution(mesh):
    return jax.shard_map(
        local,
        mesh=mesh,
        in_specs=(P("tm", "chan", None), P("chan", None), P("chan")),
        out_specs=P(("chan", "tm"), None, None),
        check_vma=False,
    )
```

profile of v0, /device:TPU:0, one launch (start us, length us, event | category | flops | bytes accessed | tf_op | source)
XLA Modules:
  0.0 904.5 jit_solution(11711263384755591038)
XLA Ops:
  18.1 2.7 cosine_multiply_fusion
  20.8 3.1 constant_dynamic-update-slice_fusion.4
  23.9 77.9 %collective-permute-done.1 = bf16[64,32,512]{2,0,1:T(8,128)(2,1)} collective-permute-done((bf16[64,32,512]{2,0,1:T(8,128)(2,1)S(1)}, bf16[64,32,512]{2,0,1:T(8,128)(2,1)}, u32[]{:S(2)}, u32[]{:S(2)}) %collective-permute-start.1) | collective-permute-done | bytes 2097184 | tf_op jit(solution)/shard_map/ppermute | solution.py:19
  101.8 3.1 constant_dynamic-update-slice_fusion.3
  105.6 3.1 constant_dynamic-update-slice_fusion.2
  108.7 177.5 %collective-permute-done.3 = bf16[64,32,512]{2,0,1:T(8,128)(2,1)} collective-permute-done((bf16[64,32,512]{2,0,1:T(8,128)(2,1)S(1)}, bf16[64,32,512]{2,0,1:T(8,128)(2,1)}, u32[]{:S(2)}, u32[]{:S(2)}) %collective-permute-start.3) | collective-permute-done | bytes 2097184 | tf_op jit(solution)/shard_map/ppermute | solution.py:19
  286.2 3.1 constant_dynamic-update-slice_fusion.1
  289.4 3.2 constant_dynamic-update-slice_fusion
  292.6 35.0 %copy.10 = bf16[64,192,512]{0,1,2:T(8,128)(2,1)} copy(bf16[64,192,512]{2,0,1:T(8,128)(2,1)} %constant_dynamic-update-slice_fusion) | data formatting | bytes 25165824 | tf_op jit(solution)/shard_map/while | solution.py:89
  328.1 413.7 %while.10 = (s32[]{:T(128)}, f32[16,512,256]{1,2,0:T(8,128)}, s32[16]{0:T(128)}, s32[]{:T(128)}, s32[16,2]{0,1:T(2,128)}, /*index=5*/s32[]{:T(128)}, bf16[64,192...) while((s32[]{:T(128)}, f32[16,512,256]{1,2,0:T(8,128)}, ...), condition=%wide.region_2.3_spmd, body=%wide.region_1.2_spmd.sunk | while | flops 33947664 | bytes 20448168 | solution.py:89
  335.0 3.3 fusion.96
  340.3 1.9 convolution_add_fusion.2
  345.4 1.9 fusion.93
  348.8 2.0 convolution_subtract_fusion.2
  360.9 3.3 fusion.96
  366.1 1.9 convolution_add_fusion.2
  371.2 1.9 fusion.93
  374.7 2.0 convolution_subtract_fusion.2
  386.8 3.3 fusion.96
  392.0 1.9 convolution_add_fusion.2
  400.5 2.0 convolution_subtract_fusion.2
  412.6 3.3 fusion.96
  417.8 1.9 convolution_add_fusion.2
  426.3 2.0 convolution_subtract_fusion.2
  438.4 3.3 fusion.96
  443.7 1.9 convolution_add_fusion.2
  448.8 1.9 fusion.93
  452.2 2.0 convolution_subtract_fusion.2
  464.3 3.3 fusion.96
  469.5 1.9 convolution_add_fusion.2
  478.1 2.0 convolution_subtract_fusion.2
  490.2 3.3 fusion.96
  495.4 1.9 convolution_add_fusion.2
  503.9 2.0 convolution_subtract_fusion.2
  516.0 3.3 fusion.96
  521.2 1.9 convolution_add_fusion.2
  529.7 2.0 convolution_subtract_fusion.2
  541.9 3.3 fusion.96
  547.1 1.9 convolution_add_fusion.2
  555.6 2.0 convolution_subtract_fusion.2
  567.7 3.3 fusion.96
  572.9 1.9 convolution_add_fusion.2
  581.4 2.0 convolution_subtract_fusion.2
  593.5 3.3 fusion.96
  598.8 1.9 convolution_add_fusion.2
  607.3 2.0 convolution_subtract_fusion.2
  619.4 3.3 fusion.96
  624.7 1.9 convolution_add_fusion.2
  633.2 2.0 convolution_subtract_fusion.2
  645.4 3.3 fusion.96
  650.6 1.9 convolution_add_fusion.2
  659.1 2.0 convolution_subtract_fusion.2
  671.2 3.3 fusion.96
  676.4 1.9 convolution_add_fusion.2
  685.0 2.0 convolution_subtract_fusion.2
  697.0 3.3 fusion.96
  702.3 1.9 convolution_add_fusion.2
  710.8 2.0 convolution_subtract_fusion.2
  723.0 3.3 fusion.96
  728.2 1.9 convolution_add_fusion.2
  736.7 2.0 convolution_subtract_fusion.2
  741.8 15.1 %convolution_bitcast_fusion = f32[16,401,256]{2,1,0:T(8,128)} fusion(f32[16,512,256]{1,2,0:T(8,128)} %get-tuple-element.42, f32[401,256]{1,0:T(8,128)} %get-tuple-element.78, f32[401,256]{1,0:T(8,128)} %get-tuple-element.77), kind=kOutput, calls=%fused_computation.20 | convolution fusion | flops 10091700224 | bytes 15779840 | tf_op jit(solution)/shard_map/lf,kfp->klp/dot_general | solution.py:90
  757.0 137.4 %reduce-scatter.2.cloned.1.call-done = f32[4,401,256]{2,1,0:T(8,128)} async-done(((f32[16,401,256]{2,1,0:T(8,128)}), f32[4,401,256]{2,1,0:T(8,128)}) %reduce-scatter.2.cloned.1.call-update) | async-done | bytes 1642512 | tf_op jit(solution)/shard_map/reduce_scatter | solution.py:91
  894.4 3.2 copy.12
  (245 shorter events, 236.2 us)
Async XLA Ops:
  6.5 1.2 copy-start
  6.5 887.8 %reduce-scatter.2.cloned.1.call-start = ((), (), s32[]{:S(2)}) async-start(), calls=%async_computation.1 | async-start | bytes 8355840 | tf_op jit(solution)/shard_map/reduce_scatter | solution.py:91
  11.6 9.2 %collective-permute-start = (bf16[64,32,512]{2,0,1:T(8,128)(2,1)S(1)}, bf16[64,32,512]{2,0,1:T(8,128)(2,1)}, u32[]{:S(2)}, u32[]{:S(2)}) collective-permute-start(bf16[64,32,512]{2,0,1:T(8,128)(2,1)S(1)} %get-tuple-element.75), channel_id=1, source_target_pairs={{1,0},{2,1},{3,2},{4,3},{5,4},{6,5},{7,6},{8,7},{9,8},{10,9},{11,1... | collective-permute-start | bytes 6291464 | tf_op jit(solution)/shard_map/ppermute | solution.py:19
  12.9 89.0 %collective-permute-start.1 = (bf16[64,32,512]{2,0,1:T(8,128)(2,1)S(1)}, bf16[64,32,512]{2,0,1:T(8,128)(2,1)}, u32[]{:S(2)}, u32[]{:S(2)}) collective-permute-start(bf16[64,32,512]{2,0,1:T(8,128)(2,1)S(1)} %get-tuple-element.75), channel_id=1, source_target_pairs={{2,0},{3,1},{4,2},{5,3},{6,4},{7,5},{8,6},{9,7},{10,8},{11,9},{12,... | collective-permute-start | bytes 6291464 | tf_op jit(solution)/shard_map/ppermute | solution.py:19
  14.2 91.5 %collective-permute-start.2 = (bf16[64,32,512]{2,0,1:T(8,128)(2,1)S(1)}, bf16[64,32,512]{2,0,1:T(8,128)(2,1)}, u32[]{:S(2)}, u32[]{:S(2)}) collective-permute-start(bf16[64,32,512]{2,0,1:T(8,128)(2,1)S(1)} %get-tuple-element.75), channel_id=1, source_target_pairs={{3,0},{4,1},{5,2},{6,3},{7,4},{8,5},{9,6},{10,7},{11,8},{12,9},{13... | collective-permute-start | bytes 6291464 | tf_op jit(solution)/shard_map/ppermute | solution.py:19
  15.5 270.8 %collective-permute-start.3 = (bf16[64,32,512]{2,0,1:T(8,128)(2,1)S(1)}, bf16[64,32,512]{2,0,1:T(8,128)(2,1)}, u32[]{:S(2)}, u32[]{:S(2)}) collective-permute-start(bf16[64,32,512]{2,0,1:T(8,128)(2,1)S(1)} %get-tuple-element.75), channel_id=1, source_target_pairs={{4,0},{5,1},{6,2},{7,3},{8,4},{9,5},{10,6},{11,7},{12,8},{13,9},{1... | collective-permute-start | bytes 6291464 | tf_op jit(solution)/shard_map/ppermute | solution.py:19
  16.8 272.6 %collective-permute-start.4 = (bf16[64,32,512]{2,0,1:T(8,128)(2,1)S(1)}, bf16[64,32,512]{2,0,1:T(8,128)(2,1)}, u32[]{:S(2)}, u32[]{:S(2)}) collective-permute-start(bf16[64,32,512]{2,0,1:T(8,128)(2,1)S(1)} %get-tuple-element.75), channel_id=1, source_target_pairs={{5,0},{6,1},{7,2},{8,3},{9,4},{10,5},{11,6},{12,7},{13,8},{14,9},{... | collective-permute-start | bytes 6291464 | tf_op jit(solution)/shard_map/ppermute | solution.py:19
  338.3 1.9 copy-start.3
  350.7 2.3 copy-start.2
  364.2 1.9 copy-start.3
  376.6 2.3 copy-start.2
  390.1 1.9 copy-start.3
  402.5 2.3 copy-start.2
  415.9 1.9 copy-start.3
  428.3 2.3 copy-start.2
  441.7 1.9 copy-start.3
  454.1 2.3 copy-start.2
  467.6 1.9 copy-start.3
  480.0 2.3 copy-start.2
  493.5 1.9 copy-start.3
  505.8 2.3 copy-start.2
  519.3 1.9 copy-start.3
  531.7 2.3 copy-start.2
  545.2 1.9 copy-start.3
  557.5 2.3 copy-start.2
  571.0 1.9 copy-start.3
  583.4 2.3 copy-start.2
  596.8 1.9 copy-start.3
  609.2 2.3 copy-start.2
  622.7 1.9 copy-start.3
  635.2 2.3 copy-start.2
  648.7 1.9 copy-start.3
  661.1 2.3 copy-start.2
  674.5 1.9 copy-start.3
  686.9 2.3 copy-start.2
  700.4 1.9 copy-start.3
  712.8 2.3 copy-start.2
  726.2 1.9 copy-start.3
  738.6 2.3 copy-start.2
  756.9 140.7 %copy-start.1 = (bf16[64,32,256]{2,1,0:T(8,128)(2,1)S(1)}, bf16[64,32,256]{2,1,0:T(8,128)(2,1)}, u32[]{:S(2)}) copy-start(bf16[64,32,256]{2,1,0:T(8,128)(2,1)} %param.5) | copy-start | bytes 3145732
Sparse Core Ops, SparseCore 0:
  757.1 137.2 reduce-scatter.1
where the time goes:
time: 914 us; the launch traced here: 904 us
  waiting for transfers between devices  393 us (43%)
  local copies, waits for them, and re-layouts  239 us (26%)
  matrix products  162 us (18%)
  loops' own time  69.2 us (8%)
  other arithmetic  20.8 us (2%)
  between operations  13.5 us (1%)
    ppermute x5, waiting for transfers between devices, shifted(): return lax.ppermute(block, axis, route)  256 us
    reduce_scatter x1, waiting for transfers between devices, local(): lax.psum_scatter(partial_value, 'tm', scatter_dimension=0, tiled=True)  137 us
    another operation x1, loops' own time, local(): lax.map(per_slot, jnp.arange(pair_blocks.shape[0], dtype=jnp.int32))  69.2 us
    dot_general x16, matrix products, cross_spectrum(): jnp.einsum('saf,sbf->fab', left_real, right_real, preferred_element_type=...  52.8 us
    while x1, local copies, waits for them, and re-layouts, local(): lax.map(per_slot, jnp.arange(pair_blocks.shape[0], dtype=jnp.int32))  35 us
    dot_general x16, matrix products, cross_spectrum(): jnp.einsum('saf,sbf->fab', left_real, right_imag, preferred_element_type=...  31.3 us
    dot_general x16, matrix products, cross_spectrum(): jnp.einsum('saf,sbf->fab', left_imag, right_imag, preferred_element_type=...  31 us
    dot_general x16, matrix products, cross_spectrum(): jnp.einsum('saf,sbf->fab', left_imag, right_real, preferred_element_type=...  30.8 us
  transfers between devices with their start and end apart: 6, of which 4 were waited for; matrix products, arithmetic and copies ran while one was open for 2% of the time, Pallas kernels for 0%

commit v1 on v0

v1 whole, which is shorter than its diff:
```python
import functools
import math

import jax
import jax.numpy as jnp
import ml_dtypes
import numpy as np
from jax import lax
from jax.experimental import pallas as pl
from jax.experimental.pallas import tpu as pltpu
from jax.sharding import PartitionSpec as P

LAGS = 401
ROWS = 416
BLK = 16
SLOTS = 16
BINS = 256
LEFT = 64
BAND = 176
CHUNKS = 2

water_share = 0.1
tiny_eps = 1e-06

MIB = 1024 * 1024


def make_tables(segments):
    length = 2 * BINS
    index = np.arange(BINS, dtype=np.int32)
    scale = np.float32(2.0 * math.pi / length)
    radians = (index[:, None] * index[None, :] % length).astype(np.float32) * scale
    forward = np.concatenate([np.cos(radians), -np.sin(radians)], axis=1)
    lag_shift = np.arange(LAGS, dtype=np.int32)[:, None] - (LAGS - 1) // 2
    lag_radians = (lag_shift * index[None, :] % length).astype(np.float32) * scale
    weight = np.where(index == 0, 1.0, 2.0).astype(np.float32)[None, :] / np.float32(
        math.sqrt(float(BINS * segments))
    )
    backward = np.concatenate([np.cos(lag_radians) * weight, -np.sin(lag_radians) * weight], axis=1)
    backward = np.pad(backward.astype(np.float32), ((0, ROWS - LAGS), (0, 0)))
    high = backward.astype(ml_dtypes.bfloat16)
    low = (backward - high.astype(np.float32)).astype(ml_dtypes.bfloat16)
    stacked = np.concatenate([high, high, low], axis=1)
    return (np.ascontiguousarray(forward.astype(ml_dtypes.bfloat16).T), stacked)


def front_kernel(right_ref, odd_ref, first_ref, table_ref, x0, b0, a1, b1, a2, b2, o5, out_ref,
                 band, spec_a, spec_b, bins_ref):
    segs = x0.shape[0]
    depth = 2 * segs
    odd = odd_ref[0] == 1

    @pl.loop(0, segs)
    def _(s):
        band[s, 0:32, :] = x0[s]
        band[s, 32:64, :] = jnp.where(odd, b1[s], b0[s])
        band[s, 64:96, :] = a1[s]
        band[s, 96:128, :] = jnp.where(odd, b2[s], b1[s])
        band[s, 128:160, :] = a2[s]
        band[s, 160:176, :] = o5[s]

    starts = [pl.multiple_of(right_ref[q] * BLK, BLK) for q in range(SLOTS)]

    def transform(s, spec):
        left = band[s, 0:LEFT, :]
        rows = [band[s, pl.ds(start, BLK), :] for start in starts] + [left, left]
        spec[...] = lax.dot_general(
            table_ref[...],
            jnp.concatenate(rows, axis=0),
            (((1,), (1,)), ((), ())),
            preferred_element_type=jnp.float32,
        )

    in_first = lax.broadcasted_iota(jnp.int32, (8, 128), 1) < LEFT

    def whiten(s, spec):
        for h in range(3):
            lanes = slice(h * 128, (h + 1) * 128)
            total = jnp.zeros((8, 128), jnp.float32)
            for f in range(0, BINS, 8):
                real_part = spec[f:f + 8, lanes]
                imag_part = spec[BINS + f:BINS + f + 8, lanes]
                total = total + (real_part * real_part + imag_part * imag_part)
            level = jnp.sum(total, axis=0, keepdims=True) * (1.0 / BINS)
            floor = jnp.broadcast_to(water_share * level + tiny_eps, (8, 128))
            for f in range(0, BINS, 8):
                real_part = spec[f:f + 8, lanes]
                imag_part = spec[BINS + f:BINS + f + 8, lanes]
                inverse = lax.rsqrt(real_part * real_part + imag_part * imag_part + floor)
                real_part = real_part * inverse
                imag_part = imag_part * inverse
                if h == 2:
                    real_part, imag_part = (
                        jnp.where(in_first, real_part, imag_part),
                        jnp.where(in_first, imag_part, -real_part),
                    )
                bins_ref[h, pl.ds(f * depth + s, 8, stride=depth), :] = real_part
                bins_ref[h, pl.ds(f * depth + segs + s, 8, stride=depth), :] = imag_part

    transform(0, spec_a)

    @pl.loop(0, segs // 2)
    def _(pair):
        s = 2 * pair
        transform(s + 1, spec_b)
        whiten(s, spec_a)
        transform(jnp.minimum(s + 2, segs - 1), spec_a)
        whiten(s + 1, spec_b)

    first = first_ref[...]
    chosen = [jnp.broadcast_to(first == i, (BLK, 256)) for i in range(3)]

    @pl.loop(0, BINS // 4)
    def _(group):
        for step in range(4):
            f = group * 4 + step
            rows = pl.ds(pl.multiple_of(f * depth, 8), depth)
            right = jnp.concatenate([bins_ref[0, rows, :], bins_ref[1, rows, :]], axis=1)
            left = bins_ref[2, rows, :]
            cross = lax.dot_general(
                left.astype(jnp.bfloat16),
                right.astype(jnp.bfloat16),
                (((0,), (0,)), ((), ())),
                preferred_element_type=jnp.float32,
            )
            for part in range(2):
                blocks = [cross[part * LEFT + i * BLK:part * LEFT + (i + 1) * BLK] for i in range(4)]
                own = blocks[3]
                for i in range(3):
                    own = jnp.where(chosen[i], blocks[i], own)
                for a in range(0, BLK, 8):
                    for h in range(2):
                        out_ref[h, pl.ds(a * 512 + part * BINS + f, 8, stride=512), :] = own[
                            a:a + 8, h * 128:(h + 1) * 128
                        ]


def front(right, odd, first, table, pieces):
    segs = pieces[0].shape[0]
    vmem = pl.BlockSpec(memory_space=pltpu.VMEM)
    smem = pl.BlockSpec(memory_space=pltpu.SMEM)
    return pl.pallas_call(
        front_kernel,
        out_shape=jax.ShapeDtypeStruct((2, BLK * 512, 128), jnp.float32),
        in_specs=[smem, smem] + [vmem] * (2 + len(pieces)),
        out_specs=vmem,
        scratch_shapes=[
            pltpu.VMEM((segs, BAND, BINS), jnp.bfloat16),
            pltpu.VMEM((512, 384), jnp.float32),
            pltpu.VMEM((512, 384), jnp.float32),
            pltpu.VMEM((3, BINS * 2 * segs, 128), jnp.float32),
        ],
        compiler_params=pltpu.CompilerParams(vmem_limit_bytes=56 * MIB),
        cost_estimate=pl.CostEstimate(flops=25_000_000_000, bytes_accessed=12_000_000, transcendentals=0),
        name="front",
    )(right, odd, first, table, *pieces)


def post_kernel(live_ref, table_ref, *refs):
    sums = refs[:CHUNKS]
    plus_ref, minus_ref, keep_ref, other_ref, own_ref, lags = refs[CHUNKS:]
    a = pl.program_id(0)
    halves = []
    for h in range(2):
        half = sums[0][h]
        for other in sums[1:]:
            half = half + other[h]
        halves.append(half)
    cross = jnp.concatenate(halves, axis=1)
    high = cross.astype(jnp.bfloat16)
    low = (cross - high.astype(jnp.float32)).astype(jnp.bfloat16)
    lags[a] = jnp.dot(
        table_ref[...],
        jnp.concatenate([high, low, high], axis=0),
        preferred_element_type=jnp.float32,
    )

    @pl.when(a == BLK - 1)
    def _():
        block = lax.broadcasted_iota(jnp.int32, (BLK, 128), 1) // BLK
        odd_block = {d: (block // d) % 2 == 1 for d in (4, 2, 1)}
        live = [live_ref[q] == 1 for q in range(SLOTS)]

        @pl.loop(0, ROWS // BLK)
        def _(tile):
            rows = pl.ds(pl.multiple_of(tile * BLK, BLK), BLK)
            for hq in range(2):
                for ha in range(2):
                    arrays = [lags[8 * ha + k, rows, hq * 128:(hq + 1) * 128] for k in range(8)]
                    for d in (4, 2, 1):
                        for k in range(8):
                            if k & d == 0:
                                one, two = arrays[k], arrays[k + d]
                                mask = odd_block[d]
                                arrays[k] = jnp.where(mask, pltpu.roll(two, BLK * d, 1), one)
                                arrays[k + d] = jnp.where(mask, two, pltpu.roll(one, 128 - BLK * d, 1))
                    lanes = slice(ha * 128, (ha + 1) * 128)
                    for k in range(8):
                        q = 8 * hq + k
                        value = jnp.where(live[q], arrays[k], 0.0)
                        if q < 4:
                            plus_ref[q, rows, lanes] = value.astype(jnp.bfloat16)
                        elif q < 8:
                            minus_ref[q - 4, rows, lanes] = value.astype(jnp.bfloat16)
                        elif q < 10:
                            keep_ref[q - 8, rows, lanes] = value
                        elif q < 12:
                            other_ref[q - 10, rows, lanes] = value
                        else:
                            own_ref[q - 12, rows, lanes] = value


def post(live, table, sums):
    def whole(shape):
        return pl.BlockSpec(shape, lambda a: (0,) * len(shape))

    shapes = [((4, ROWS, 256), jnp.bfloat16)] * 2 + [((2, ROWS, 256), jnp.float32)] * 2
    shapes.append(((4, ROWS, 256), jnp.float32))
    return pl.pallas_call(
        post_kernel,
        grid=(BLK,),
        out_shape=[jax.ShapeDtypeStruct(s, d) for s, d in shapes],
        in_specs=[pl.BlockSpec(memory_space=pltpu.SMEM), whole(table.shape)]
        + [pl.BlockSpec((2, 512, 128), lambda a: (0, a, 0))] * len(sums),
        out_specs=[whole(s) for s, _ in shapes],
        scratch_shapes=[pltpu.VMEM((BLK, ROWS, 256), jnp.float32)],
        compiler_params=pltpu.CompilerParams(vmem_limit_bytes=48 * MIB),
        cost_estimate=pl.CostEstimate(flops=12_000_000_000, bytes_accessed=24_000_000, transcendentals=0),
        name="post",
    )(live, table, *sums)


def moved(block, axis, to):
    size = lax.axis_size(axis)
    return lax.ppermute(block, axis, [(i, to(i) % size) for i in range(size)])


def gather_band(own):
    one_chip = functools.partial(moved, axis="chan", to=lambda i: i - 2)
    swap = functools.partial(moved, axis="chan", to=lambda i: i ^ 1)
    b0 = swap(own)
    a1 = one_chip(own)
    a2 = one_chip(a1)
    b1 = swap(a1)
    b2 = swap(a2)
    o5 = moved(a2[:, :BLK], "chan", lambda i: i - 1)
    return [own, b0, a1, b1, a2, b2, o5]


def local(records, pair_blocks, pair_counts):
    segs = records.shape[0]
    table, backward = make_tables(segs * lax.axis_size("tm"))
    owner = lax.axis_index("chan")
    row = lax.axis_index("tm")

    group = np.array([2, 2, 1, 1, 2, 2, 3, 3, 1, 1, 3, 3, 0, 0, 0, 0], np.int32)
    inside = np.array([0, 1, 2, 3, 2, 3, 0, 1, 0, 1, 2, 3, 0, 1, 2, 3], np.int32)
    order = (row + group) % 4 * 4 + inside
    relative = pair_blocks[order] - 2 * owner
    first = jnp.clip(relative[:, 0], 0, 3)
    right = jnp.clip(relative[:, 1], 0, 10)
    live = (order < pair_counts[0]).astype(jnp.int32)
    odd = (owner % 2).astype(jnp.int32)[None]
    first_lanes = jnp.repeat(first, BLK)[None, :]

    step = segs // CHUNKS
    sums = []
    for chunk in range(CHUNKS):
        pieces = gather_band(records[chunk * step:(chunk + 1) * step])
        sums.append(front(right, odd, first_lanes, table, pieces))
    plus, minus, keep, other, own = post(live, backward, sums)

    from_below = moved(plus, "tm", lambda i: i + 1)
    from_above = moved(minus, "tm", lambda i: i - 1)
    up = (keep + from_below[:2].astype(jnp.float32)).astype(jnp.bfloat16)
    down = (other + from_above[:2].astype(jnp.float32)).astype(jnp.bfloat16)
    two_below = moved(up, "tm", lambda i: i + 1)
    two_above = moved(down, "tm", lambda i: i - 1)
    f32 = jnp.float32
    low = own[:2] + from_above[2:].astype(f32) + two_below.astype(f32)
    high = own[2:] + from_below[2:].astype(f32) + two_above.astype(f32)
    return jnp.concatenate([low, high], axis=0)[:, :LAGS]


def solution(mesh):
    return jax.shard_map(
        local,
        mesh=mesh,
        in_specs=(P("tm", "chan", None), P("chan", None), P("chan")),
        out_specs=P(("chan", "tm"), None, None),
        check_vma=False,
    )
```

time: 914 us -> 246 us (0.27)
  waiting for transfers between devices: 393 us -> 54.1 us
  local copies, waits for them, and re-layouts: 239 us -> 6.34 us
  matrix products: 162 us -> 0 us
  Pallas kernels: 0 us -> 143 us
  loops' own time: 69.2 us -> 0 us
  starting transfers between devices: 6.45 us -> 38.6 us
  other arithmetic: 20.8 us -> 1.42 us
  between operations: 13.5 us -> 0.85 us
    ppermute x5 -> x16, waiting for transfers between devices: 256 us -> 54.1 us  [moved(): return lax.ppermute(block, axis, [(i, to(i) % size) for i in range(size)])]
    dot_general x66 -> x0, matrix products: 162 us -> none  [the longest x16 52.8 us: cross_spectrum(): jnp.einsum('saf,sbf->fab', left_real, right_real, preferred_element_type=...]
    pallas_call x0 -> x3, Pallas kernels: none -> 143 us  [the longest x2 120 us: front(): pl.pallas_call(front_kernel, out_shape=jax.ShapeDtypeStruct((2, BLK * 512...]
    reduce_scatter x1 -> x0, waiting for transfers between devices: 137 us -> none  [local(): lax.psum_scatter(partial_value, 'tm', scatter_dimension=0, tiled=True)]
    dot_general x64 -> x0, local copies, waits for them, and re-layouts: 95 us -> none  [the longest x16 25.4 us: cross_spectrum(): jnp.einsum('saf,sbf->fab', left_imag, right_imag, preferred_element_type=...]
    another operation x1 -> x0, loops' own time: 69.2 us -> none  [local(): lax.map(per_slot, jnp.arange(pair_blocks.shape[0], dtype=jnp.int32))]
    while x65 -> x0, local copies, waits for them, and re-layouts: 40.4 us -> none  [the longest x1 35 us: local(): lax.map(per_slot, jnp.arange(pair_blocks.shape[0], dtype=jnp.int32))]
    dynamic_slice x32 -> x0, local copies, waits for them, and re-layouts: 40.2 us -> none  [the longest x16 21.5 us: per_slot(): second_start = pair_blocks[slot_index, 1] * BLK - base_channel]
  transfers between devices with their start and end apart: 6 -> 16, of which waited for: 4 -> 7; matrix products, arithmetic and copies ran while one was open for 2% -> 1% of each run, Pallas kernels for 0% -> 25%
where the time goes in v1:
time: 246 us; the launch traced here: 245 us
  Pallas kernels  143 us (58%)
  waiting for transfers between devices  54.1 us (22%)
  starting transfers between devices  38.6 us (16%)
  local copies, waits for them, and re-layouts  6.34 us (3%)
    pallas_call x2, Pallas kernels, front(): pl.pallas_call(front_kernel, out_shape=jax.ShapeDtypeStruct((2, BLK * 512...  120 us
    ppermute x16, waiting for transfers between devices, moved(): return lax.ppermute(block, axis, [(i, to(i) % size) for i in range(size)])  54.1 us
    ppermute x16, starting transfers between devices, moved(): return lax.ppermute(block, axis, [(i, to(i) % size) for i in range(size)])  38.6 us
    pallas_call x1, Pallas kernels, post(): pl.pallas_call(post_kernel, grid=(BLK,), out_shape=[jax.ShapeDtypeStruct(...  23.3 us
  transfers between devices with their start and end apart: 16, of which 7 were waited for; matrix products, arithmetic and copies ran while one was open for 1% of the time, Pallas kernels for 25%

profile of v1, /device:TPU:0, one launch (start us, length us, event | category | flops | bytes accessed | tf_op | source)
XLA Modules:
  0.0 244.6 jit_solution(18274476909661269443)
XLA Ops:
  0.0 1.3 fusion.6
  1.3 0.0 copy-start.3
  1.3 0.0 copy-start.2
  1.3 6.4 %collective-permute-start.1 = (bf16[32,32,256]{2,1,0:T(8,128)(2,1)S(1)}, bf16[32,32,256]{2,1,0:T(8,128)(2,1)S(1)}, u32[]{:S(2)}, u32[]{:S(2)}) collective-permute-start(bf16[32,32,256]{2,1,0:T(8,128)(2,1)S(1)} %get-tuple-element.22.x0), channel_id=1, source_target_pairs={{0,62},{1,63},{2,0},{3,1},{4,2},{5,3},{6,4},{7,5},{8,6},{9,7},{10,... | collective-permute-start | bytes 1572872 | tf_op jit(solution)/shard_map/ppermute | solution.py:235
  7.7 1.0 collective-permute-start.7
  8.7 11.3 %collective-permute-done.1.a1 = bf16[32,32,256]{2,1,0:T(8,128)(2,1)S(1)} collective-permute-done((bf16[32,32,256]{2,1,0:T(8,128)(2,1)S(1)}, bf16[32,32,256]{2,1,0:T(8,128)(2,1)S(1)}, u32[]{:S(2)}, u32[]{:S(2)}) %collective-permute-start.1) | collective-permute-done | bytes 524320 | tf_op jit(solution)/shard_map/ppermute | solution.py:235
  20.0 5.8 %collective-permute-start.3 = (bf16[32,32,256]{2,1,0:T(8,128)(2,1)S(1)}, bf16[32,32,256]{2,1,0:T(8,128)(2,1)S(1)}, u32[]{:S(2)}, u32[]{:S(2)}) collective-permute-start(bf16[32,32,256]{2,1,0:T(8,128)(2,1)S(1)} %collective-permute-done.1.a1), channel_id=1, source_target_pairs={{0,62},{1,63},{2,0},{3,1},{4,2},{5,3},{6,4},{7,5},{8,6},{9,7},{10,... | collective-permute-start | bytes 1572872 | tf_op jit(solution)/shard_map/ppermute | solution.py:235
  25.8 0.0 collective-permute-start
  25.8 0.0 copy-done.6
  25.9 0.1 copy.10
  25.9 0.0 copy-done.7
  25.9 0.0 copy-done.8
  26.0 0.6 gather_fusion
  26.5 0.6 collective-permute-start.2
  27.1 4.2 %collective-permute-done.7.a1 = bf16[32,32,256]{2,1,0:T(8,128)(2,1)S(1)} collective-permute-done((bf16[32,32,256]{2,1,0:T(8,128)(2,1)S(1)}, bf16[32,32,256]{2,1,0:T(8,128)(2,1)S(1)}, u32[]{:S(2)}, u32[]{:S(2)}) %collective-permute-start.7) | collective-permute-done | bytes 524320 | tf_op jit(solution)/shard_map/ppermute | solution.py:235
  31.3 5.8 %collective-permute-start.9 = (bf16[32,32,256]{2,1,0:T(8,128)(2,1)S(1)}, bf16[32,32,256]{2,1,0:T(8,128)(2,1)S(1)}, u32[]{:S(2)}, u32[]{:S(2)}) collective-permute-start(bf16[32,32,256]{2,1,0:T(8,128)(2,1)S(1)} %collective-permute-done.7.a1), channel_id=1, source_target_pairs={{0,62},{1,63},{2,0},{3,1},{4,2},{5,3},{6,4},{7,5},{8,6},{9,7},{10,... | collective-permute-start | bytes 1572872 | tf_op jit(solution)/shard_map/ppermute | solution.py:235
  37.1 5.4 %collective-permute-done.3.a2 = bf16[32,32,256]{2,1,0:T(8,128)(2,1)S(1)} collective-permute-done((bf16[32,32,256]{2,1,0:T(8,128)(2,1)S(1)}, bf16[32,32,256]{2,1,0:T(8,128)(2,1)S(1)}, u32[]{:S(2)}, u32[]{:S(2)}) %collective-permute-start.3) | collective-permute-done | bytes 524320 | tf_op jit(solution)/shard_map/ppermute | solution.py:235
  42.5 0.0 collective-permute-start.4
  42.5 6.0 %collective-permute-start.5 = (bf16[32,16,256]{2,1,0:T(8,128)(2,1)S(1)}, bf16[32,16,256]{2,1,0:T(8,128)(2,1)}, u32[]{:S(2)}, u32[]{:S(2)}) collective-permute-start(bf16[32,16,256]{2,1,0:T(8,128)(2,1)S(1)} %slice.56), channel_id=1, source_target_pairs={{0,63},{1,0},{2,1},{3,2},{4,3},{5,4},{6,5},{7,6},{8,7},{9,8},{10,9... | collective-permute-start | bytes 786440 | tf_op jit(solution)/shard_map/ppermute | solution.py:235
  48.5 0.8 fusion
  50.0 0.1 broadcast_in_dim.11
  50.0 0.6 broadcast_in_dim_reshape.3.first_ref
  50.7 1.9 collective-permute-done.9.a2
  52.6 0.0 collective-permute-start.6
  52.6 0.0 collective-permute-done.b0
  52.6 0.6 collective-permute-start.8
  53.2 0.0 collective-permute-done.2.b1
  53.2 5.5 %collective-permute-start.11 = (bf16[32,16,256]{2,1,0:T(8,128)(2,1)S(1)}, bf16[32,16,256]{2,1,0:T(8,128)(2,1)S(1)}, u32[]{:S(2)}, u32[]{:S(2)}) collective-permute-start(bf16[32,16,256]{2,1,0:T(8,128)(2,1)S(1)} %slice.57), channel_id=1, source_target_pairs={{0,63},{1,0},{2,1},{3,2},{4,3},{5,4},{6,5},{7,6},{8,7},{9,8},{10,9... | collective-permute-start | bytes 786440 | tf_op jit(solution)/shard_map/ppermute | solution.py:235
  58.7 0.0 collective-permute-done.5.o5
  58.7 0.0 collective-permute-start.10
  58.7 0.0 collective-permute-done.4.b2
  58.8 0.0 copy-done.3
  58.8 0.0 copy-done.10
  58.8 0.0 copy-done.4
  58.8 60.1 %front.2.refs_0_ = f32[2,8192,128]{2,1,0:T(8,128)} custom-call(s32[16]{0:T(128)} %get-tuple-element.16.right_ref, s32[1]{0:T(128)} %bitcast.1.odd_ref, s32[1,256]{1,0:T(1,128)} %broadcast_in_dim_reshape.3.first_ref, bf16[512,256]{1,0:T(8,128)(2,1)} %constant.54.clone.table_ref, bf16[32,32,256]{2,1,0:T(8,128)(2,1)} %copy-done.3, ...), custom_call_target="tpu_custom_call" | custom-call | flops 24999999488 | bytes 12000000 | tf_op jit(solution)/shard_map/front/pallas_call | solution.py:142
  118.8 0.0 copy-done.2
  118.9 0.0 copy-done.9
  118.9 0.0 copy-done.5
  118.9 0.0 copy-start
  118.9 0.0 collective-permute-done.6.b0
  118.9 0.0 copy-start.11
  118.9 0.0 collective-permute-done.8.b1
  118.9 0.0 copy-start.12
  118.9 0.0 collective-permute-done.11.o5
  118.9 0.0 collective-permute-done.10.b2
  119.0 0.7 copy-done.11
  119.7 0.2 copy-done.12
  119.9 0.1 copy-done.14
  120.0 0.8 copy-done.13
  120.8 60.0 %front.3.refs_1_ = f32[2,8192,128]{2,1,0:T(8,128)} custom-call(s32[16]{0:T(128)} %get-tuple-element.16.right_ref, s32[1]{0:T(128)} %bitcast.1.odd_ref, s32[1,256]{1,0:T(1,128)} %broadcast_in_dim_reshape.3.first_ref, bf16[512,256]{1,0:T(8,128)(2,1)} %constant.54.clone.table_ref, bf16[32,32,256]{2,1,0:T(8,128)(2,1)} %copy-done.2, ...), custom_call_target="tpu_custom_call" | custom-call | flops 24999999488 | bytes 12000000 | tf_op jit(solution)/shard_map/front/pallas_call | solution.py:142
  180.8 23.3 %post.1 = (bf16[4,416,256]{2,1,0:T(8,128)(2,1)S(1)}, bf16[4,416,256]{2,1,0:T(8,128)(2,1)S(1)}, f32[2,416,256]{2,1,0:T(8,128)S(1)}, f32[2,416,256]{2,1,0:T(8,128)S(1)}, f32[4,416,256]{2,1,0:T(8,128)}) custom-call(s32[16]{0:T(128)S(1)} %compare_convert_fusion.live_ref, bf16[416,1536]{1,0:T(8,128)(2,1)S(1)} %copy-done, f32[2,8192,128]{2,1,0:T(8,128)} %front.2.refs_0_, ...), custom_call_target="tpu_custom_call" | custom-call | flops 12000000000 | bytes 24000000 | tf_op jit(solution)/shard_map/post/pallas_call | solution.py:219
  204.1 3.0 %collective-permute-start.12 = (bf16[4,416,256]{2,1,0:T(8,128)(2,1)S(1)}, bf16[4,416,256]{2,1,0:T(8,128)(2,1)S(1)}, u32[]{:S(2)}, u32[]{:S(2)}) collective-permute-start(bf16[4,416,256]{2,1,0:T(8,128)(2,1)S(1)} %get-tuple-element.11), channel_id=1, source_target_pairs={{0,192},{64,0},{128,64},{192,128},{1,193},{65,1},{129,65},{193,129... | collective-permute-start | bytes 2555912 | tf_op jit(solution)/shard_map/ppermute | solution.py:235
  207.1 0.0 collective-permute-start.13
  207.1 18.9 %collective-permute-done.12 = bf16[4,416,256]{2,1,0:T(8,128)(2,1)S(1)} collective-permute-done((bf16[4,416,256]{2,1,0:T(8,128)(2,1)S(1)}, bf16[4,416,256]{2,1,0:T(8,128)(2,1)S(1)}, u32[]{:S(2)}, u32[]{:S(2)}) %collective-permute-start.12) | collective-permute-done | bytes 852000 | tf_op jit(solution)/shard_map/ppermute | solution.py:235
  225.9 0.1 add_convert_fusion
  226.1 3.8 %collective-permute-start.15 = (bf16[2,416,256]{2,1,0:T(8,128)(2,1)S(1)}, bf16[2,416,256]{2,1,0:T(8,128)(2,1)S(1)}, u32[]{:S(2)}, u32[]{:S(2)}) collective-permute-start(bf16[2,416,256]{2,1,0:T(8,128)(2,1)S(1)} %add_convert_fusion), channel_id=1, source_target_pairs={{0,192},{64,0},{128,64},{192,128},{1,193},{65,1},{129,65},{193,129... | collective-permute-start | bytes 1277960 | tf_op jit(solution)/shard_map/ppermute | solution.py:235
  229.8 0.0 collective-permute-done.13
  229.8 0.1 add_convert_fusion.1
  230.0 0.1 collective-permute-start.14
  230.0 8.7 %collective-permute-done.15 = bf16[2,416,256]{2,1,0:T(8,128)(2,1)S(1)} collective-permute-done((bf16[2,416,256]{2,1,0:T(8,128)(2,1)S(1)}, bf16[2,416,256]{2,1,0:T(8,128)(2,1)S(1)}, u32[]{:S(2)}, u32[]{:S(2)}) %collective-permute-start.15) | collective-permute-done | bytes 426016 | tf_op jit(solution)/shard_map/ppermute | solution.py:235
  238.8 3.6 %collective-permute-done.14 = bf16[2,416,256]{2,1,0:T(8,128)(2,1)S(1)} collective-permute-done((bf16[2,416,256]{2,1,0:T(8,128)(2,1)S(1)}, bf16[2,416,256]{2,1,0:T(8,128)(2,1)S(1)}, u32[]{:S(2)}, u32[]{:S(2)}) %collective-permute-start.14) | collective-permute-done | bytes 426016 | tf_op jit(solution)/shard_map/ppermute | solution.py:235
  242.4 0.2 convert_add_fusion.1
  242.6 0.2 pad_maximum_fusion
  242.8 1.8 copy.11
  (18 shorter events, 0.1 us)
Async XLA Ops:
  0.0 25.9 %copy-start.7 = (s32[16]{0:T(128)S(1)}, s32[16]{0:T(128)}, u32[]{:S(2)}) copy-start(s32[16]{0:T(128)} %constant.53.clone) | copy-start | bytes 196
  0.0 25.9 %copy-start.8 = (s32[16]{0:T(128)S(1)}, s32[16]{0:T(128)}, u32[]{:S(2)}) copy-start(s32[16]{0:T(128)} %constant.52.clone) | copy-start | bytes 196
  0.0 25.8 %copy-start.6 = (s32[16,2]{0,1:T(2,128)S(1)}, s32[16,2]{0,1:T(2,128)}, u32[]{:S(2)}) copy-start(s32[16,2]{0,1:T(2,128)} %param.8) | copy-start | bytes 388
  1.3 57.5 %copy-start.3 = (bf16[32,32,256]{2,1,0:T(8,128)(2,1)}, bf16[32,32,256]{2,1,0:T(8,128)(2,1)S(1)}, u32[]{:S(2)}) copy-start(bf16[32,32,256]{2,1,0:T(8,128)(2,1)S(1)} %get-tuple-element.22.x0) | copy-start | bytes 1572868
  1.3 117.5 %copy-start.2 = (bf16[32,32,256]{2,1,0:T(8,128)(2,1)}, bf16[32,32,256]{2,1,0:T(8,128)(2,1)S(1)}, u32[]{:S(2)}) copy-start(bf16[32,32,256]{2,1,0:T(8,128)(2,1)S(1)} %get-tuple-element.21.x0) | copy-start | bytes 1572868
  1.3 18.7 %collective-permute-start.1 = (bf16[32,32,256]{2,1,0:T(8,128)(2,1)S(1)}, bf16[32,32,256]{2,1,0:T(8,128)(2,1)S(1)}, u32[]{:S(2)}, u32[]{:S(2)}) collective-permute-start(bf16[32,32,256]{2,1,0:T(8,128)(2,1)S(1)} %get-tuple-element.22.x0), channel_id=1, source_target_pairs={{0,62},{1,63},{2,0},{3,1},{4,2},{5,3},{6,4},{7,5},{8,6},{9,7},{10,... | collective-permute-start | bytes 1572872 | tf_op jit(solution)/shard_map/ppermute | solution.py:235
  7.7 23.6 %collective-permute-start.7 = (bf16[32,32,256]{2,1,0:T(8,128)(2,1)S(1)}, bf16[32,32,256]{2,1,0:T(8,128)(2,1)S(1)}, u32[]{:S(2)}, u32[]{:S(2)}) collective-permute-start(bf16[32,32,256]{2,1,0:T(8,128)(2,1)S(1)} %get-tuple-element.21.x0), channel_id=1, source_target_pairs={{0,62},{1,63},{2,0},{3,1},{4,2},{5,3},{6,4},{7,5},{8,6},{9,7},{10,... | collective-permute-start | bytes 1572872 | tf_op jit(solution)/shard_map/ppermute | solution.py:235
  20.0 38.7 %copy-start.10 = (bf16[32,32,256]{2,1,0:T(8,128)(2,1)}, bf16[32,32,256]{2,1,0:T(8,128)(2,1)S(1)}, u32[]{:S(2)}) copy-start(bf16[32,32,256]{2,1,0:T(8,128)(2,1)S(1)} %collective-permute-done.1.a1) | copy-start | bytes 1572868
  20.0 22.5 %collective-permute-start.3 = (bf16[32,32,256]{2,1,0:T(8,128)(2,1)S(1)}, bf16[32,32,256]{2,1,0:T(8,128)(2,1)S(1)}, u32[]{:S(2)}, u32[]{:S(2)}) collective-permute-start(bf16[32,32,256]{2,1,0:T(8,128)(2,1)S(1)} %collective-permute-done.1.a1), channel_id=1, source_target_pairs={{0,62},{1,63},{2,0},{3,1},{4,2},{5,3},{6,4},{7,5},{8,6},{9,7},{10,... | collective-permute-start | bytes 1572872 | tf_op jit(solution)/shard_map/ppermute | solution.py:235
  25.8 26.8 %collective-permute-start = (bf16[32,32,256]{2,1,0:T(8,128)(2,1)S(1)}, bf16[32,32,256]{2,1,0:T(8,128)(2,1)}, u32[]{:S(2)}, u32[]{:S(2)}) collective-permute-start(bf16[32,32,256]{2,1,0:T(8,128)(2,1)S(1)} %get-tuple-element.22.x0), channel_id=1, source_target_pairs={{0,1},{1,0},{2,3},{3,2},{4,5},{5,4},{6,7},{7,6},{8,9},{9,8},{10,11... | collective-permute-start | bytes 1572872 | tf_op jit(solution)/shard_map/ppermute | solution.py:235
  26.5 26.7 %collective-permute-start.2 = (bf16[32,32,256]{2,1,0:T(8,128)(2,1)S(1)}, bf16[32,32,256]{2,1,0:T(8,128)(2,1)}, u32[]{:S(2)}, u32[]{:S(2)}) collective-permute-start(bf16[32,32,256]{2,1,0:T(8,128)(2,1)S(1)} %collective-permute-done.1.a1), channel_id=1, source_target_pairs={{0,1},{1,0},{2,3},{3,2},{4,5},{5,4},{6,7},{7,6},{8,9},{9,8},{10,11... | collective-permute-start | bytes 1572872 | tf_op jit(solution)/shard_map/ppermute | solution.py:235
  31.3 87.6 %copy-start.9 = (bf16[32,32,256]{2,1,0:T(8,128)(2,1)}, bf16[32,32,256]{2,1,0:T(8,128)(2,1)S(1)}, u32[]{:S(2)}) copy-start(bf16[32,32,256]{2,1,0:T(8,128)(2,1)S(1)} %collective-permute-done.7.a1) | copy-start | bytes 1572868
  31.3 21.3 %collective-permute-start.9 = (bf16[32,32,256]{2,1,0:T(8,128)(2,1)S(1)}, bf16[32,32,256]{2,1,0:T(8,128)(2,1)S(1)}, u32[]{:S(2)}, u32[]{:S(2)}) collective-permute-start(bf16[32,32,256]{2,1,0:T(8,128)(2,1)S(1)} %collective-permute-done.7.a1), channel_id=1, source_target_pairs={{0,62},{1,63},{2,0},{3,1},{4,2},{5,3},{6,4},{7,5},{8,6},{9,7},{10,... | collective-permute-start | bytes 1572872 | tf_op jit(solution)/shard_map/ppermute | solution.py:235
  42.5 16.3 %copy-start.4 = (bf16[32,32,256]{2,1,0:T(8,128)(2,1)}, bf16[32,32,256]{2,1,0:T(8,128)(2,1)S(1)}, u32[]{:S(2)}) copy-start(bf16[32,32,256]{2,1,0:T(8,128)(2,1)S(1)} %collective-permute-done.3.a2) | copy-start | bytes 1572868
  42.5 16.2 %collective-permute-start.4 = (bf16[32,32,256]{2,1,0:T(8,128)(2,1)S(1)}, bf16[32,32,256]{2,1,0:T(8,128)(2,1)}, u32[]{:S(2)}, u32[]{:S(2)}) collective-permute-start(bf16[32,32,256]{2,1,0:T(8,128)(2,1)S(1)} %collective-permute-done.3.a2), channel_id=1, source_target_pairs={{0,1},{1,0},{2,3},{3,2},{4,5},{5,4},{6,7},{7,6},{8,9},{9,8},{10,11... | collective-permute-start | bytes 1572872 | tf_op jit(solution)/shard_map/ppermute | solution.py:235
  42.5 16.2 %collective-permute-start.5 = (bf16[32,16,256]{2,1,0:T(8,128)(2,1)S(1)}, bf16[32,16,256]{2,1,0:T(8,128)(2,1)}, u32[]{:S(2)}, u32[]{:S(2)}) collective-permute-start(bf16[32,16,256]{2,1,0:T(8,128)(2,1)S(1)} %slice.56), channel_id=1, source_target_pairs={{0,63},{1,0},{2,1},{3,2},{4,3},{5,4},{6,5},{7,6},{8,7},{9,8},{10,9... | collective-permute-start | bytes 786440 | tf_op jit(solution)/shard_map/ppermute | solution.py:235
  52.6 66.3 %copy-start.5 = (bf16[32,32,256]{2,1,0:T(8,128)(2,1)}, bf16[32,32,256]{2,1,0:T(8,128)(2,1)S(1)}, u32[]{:S(2)}) copy-start(bf16[32,32,256]{2,1,0:T(8,128)(2,1)S(1)} %collective-permute-done.9.a2) | copy-start | bytes 1572868
  52.6 66.3 %collective-permute-start.6 = (bf16[32,32,256]{2,1,0:T(8,128)(2,1)S(1)}, bf16[32,32,256]{2,1,0:T(8,128)(2,1)S(1)}, u32[]{:S(2)}, u32[]{:S(2)}) collective-permute-start(bf16[32,32,256]{2,1,0:T(8,128)(2,1)S(1)} %get-tuple-element.21.x0), channel_id=1, source_target_pairs={{0,1},{1,0},{2,3},{3,2},{4,5},{5,4},{6,7},{7,6},{8,9},{9,8},{10,11... | collective-permute-start | bytes 1572872 | tf_op jit(solution)/shard_map/ppermute | solution.py:235
  52.6 66.3 %collective-permute-start.8 = (bf16[32,32,256]{2,1,0:T(8,128)(2,1)S(1)}, bf16[32,32,256]{2,1,0:T(8,128)(2,1)S(1)}, u32[]{:S(2)}, u32[]{:S(2)}) collective-permute-start(bf16[32,32,256]{2,1,0:T(8,128)(2,1)S(1)} %collective-permute-done.7.a1), channel_id=1, source_target_pairs={{0,1},{1,0},{2,3},{3,2},{4,5},{5,4},{6,7},{7,6},{8,9},{9,8},{10,11... | collective-permute-start | bytes 1572872 | tf_op jit(solution)/shard_map/ppermute | solution.py:235
  53.2 65.7 %collective-permute-start.11 = (bf16[32,16,256]{2,1,0:T(8,128)(2,1)S(1)}, bf16[32,16,256]{2,1,0:T(8,128)(2,1)S(1)}, u32[]{:S(2)}, u32[]{:S(2)}) collective-permute-start(bf16[32,16,256]{2,1,0:T(8,128)(2,1)S(1)} %slice.57), channel_id=1, source_target_pairs={{0,63},{1,0},{2,1},{3,2},{4,3},{5,4},{6,5},{7,6},{8,7},{9,8},{10,9... | collective-permute-start | bytes 786440 | tf_op jit(solution)/shard_map/ppermute | solution.py:235
  58.7 60.2 %collective-permute-start.10 = (bf16[32,32,256]{2,1,0:T(8,128)(2,1)S(1)}, bf16[32,32,256]{2,1,0:T(8,128)(2,1)S(1)}, u32[]{:S(2)}, u32[]{:S(2)}) collective-permute-start(bf16[32,32,256]{2,1,0:T(8,128)(2,1)S(1)} %collective-permute-done.9.a2), channel_id=1, source_target_pairs={{0,1},{1,0},{2,3},{3,2},{4,5},{5,4},{6,7},{7,6},{8,9},{9,8},{10,11... | collective-permute-start | bytes 1572872 | tf_op jit(solution)/shard_map/ppermute | solution.py:235
  118.9 61.9 %copy-start = (bf16[416,1536]{1,0:T(8,128)(2,1)S(1)}, bf16[416,1536]{1,0:T(8,128)(2,1)}, u32[]{:S(2)}) copy-start(bf16[416,1536]{1,0:T(8,128)(2,1)} %constant.55.clone.table_ref) | copy-start | bytes 3833860
  118.9 0.8 copy-start.11
  118.9 0.9 copy-start.12
  118.9 1.0 copy-start.14
  120.0 0.8 copy-start.13
  204.1 21.9 %collective-permute-start.12 = (bf16[4,416,256]{2,1,0:T(8,128)(2,1)S(1)}, bf16[4,416,256]{2,1,0:T(8,128)(2,1)S(1)}, u32[]{:S(2)}, u32[]{:S(2)}) collective-permute-start(bf16[4,416,256]{2,1,0:T(8,128)(2,1)S(1)} %get-tuple-element.11), channel_id=1, source_target_pairs={{0,192},{64,0},{128,64},{192,128},{1,193},{65,1},{129,65},{193,129... | collective-permute-start | bytes 2555912 | tf_op jit(solution)/shard_map/ppermute | solution.py:235
  207.1 22.8 %collective-permute-start.13 = (bf16[4,416,256]{2,1,0:T(8,128)(2,1)S(1)}, bf16[4,416,256]{2,1,0:T(8,128)(2,1)S(1)}, u32[]{:S(2)}, u32[]{:S(2)}) collective-permute-start(bf16[4,416,256]{2,1,0:T(8,128)(2,1)S(1)} %get-tuple-element.13), channel_id=1, source_target_pairs={{0,64},{64,128},{128,192},{192,0},{1,65},{65,129},{129,193},{193,1... | collective-permute-start | bytes 2555912 | tf_op jit(solution)/shard_map/ppermute | solution.py:235
  225.9 16.5 %copy-start.1 = (f32[4,416,256]{2,1,0:T(8,128)S(1)}, f32[4,416,256]{2,1,0:T(8,128)}, u32[]{:S(2)}) copy-start(f32[4,416,256]{2,1,0:T(8,128)} %get-tuple-element.10) | copy-start | bytes 5111812
  226.1 12.7 %collective-permute-start.15 = (bf16[2,416,256]{2,1,0:T(8,128)(2,1)S(1)}, bf16[2,416,256]{2,1,0:T(8,128)(2,1)S(1)}, u32[]{:S(2)}, u32[]{:S(2)}) collective-permute-start(bf16[2,416,256]{2,1,0:T(8,128)(2,1)S(1)} %add_convert_fusion), channel_id=1, source_target_pairs={{0,192},{64,0},{128,64},{192,128},{1,193},{65,1},{129,65},{193,129... | collective-permute-start | bytes 1277960 | tf_op jit(solution)/shard_map/ppermute | solution.py:235
  230.0 12.4 %collective-permute-start.14 = (bf16[2,416,256]{2,1,0:T(8,128)(2,1)S(1)}, bf16[2,416,256]{2,1,0:T(8,128)(2,1)S(1)}, u32[]{:S(2)}, u32[]{:S(2)}) collective-permute-start(bf16[2,416,256]{2,1,0:T(8,128)(2,1)S(1)} %add_convert_fusion.1), channel_id=1, source_target_pairs={{0,64},{64,128},{128,192},{192,0},{1,65},{65,129},{129,193},{193,1... | collective-permute-start | bytes 1277960 | tf_op jit(solution)/shard_map/ppermute | solution.py:235

commit v2 on v0

v2 whole, which is shorter than its diff:
```python
import functools
import math

import jax
import jax.numpy as jnp
import ml_dtypes
import numpy as np
from jax import lax
from jax.experimental import pallas as pl
from jax.experimental.pallas import tpu as pltpu
from jax.sharding import PartitionSpec as P

LAGS = 401
ROWS = 416
BLK = 16
SLOTS = 16
BINS = 256
LEFT = 64
BAND = 176
CHUNKS = (32, 16, 16)
PITCH = 513

water_share = 0.1
tiny_eps = 1e-06

MIB = 1024 * 1024


def make_tables(segments):
    length = 2 * BINS
    index = np.arange(BINS, dtype=np.int32)
    scale = np.float32(2.0 * math.pi / length)
    radians = (index[:, None] * index[None, :] % length).astype(np.float32) * scale
    forward = np.concatenate([np.cos(radians), -np.sin(radians)], axis=1)
    lag_shift = np.arange(LAGS, dtype=np.int32)[:, None] - (LAGS - 1) // 2
    lag_radians = (lag_shift * index[None, :] % length).astype(np.float32) * scale
    weight = np.where(index == 0, 1.0, 2.0).astype(np.float32)[None, :] / np.float32(
        math.sqrt(float(BINS * segments))
    )
    backward = np.concatenate([np.cos(lag_radians) * weight, -np.sin(lag_radians) * weight], axis=1)
    backward = np.pad(backward.astype(np.float32), ((0, ROWS - LAGS), (0, 0)))
    high = backward.astype(ml_dtypes.bfloat16)
    low = (backward - high.astype(np.float32)).astype(ml_dtypes.bfloat16)
    stacked = np.concatenate([high, low], axis=0)
    return (np.ascontiguousarray(forward.astype(ml_dtypes.bfloat16).T), stacked)


def whiten_tile(spec, lanes, put):
    total = jnp.zeros((8, 128), jnp.float32)
    for f in range(0, BINS, 8):
        real_part = spec[f:f + 8, lanes]
        imag_part = spec[BINS + f:BINS + f + 8, lanes]
        total = total + (real_part * real_part + imag_part * imag_part)
    level = jnp.sum(total, axis=0, keepdims=True) * (1.0 / BINS)
    floor = jnp.broadcast_to(water_share * level + tiny_eps, (8, 128))
    for f in range(0, BINS, 8):
        real_part = spec[f:f + 8, lanes]
        imag_part = spec[BINS + f:BINS + f + 8, lanes]
        inverse = lax.rsqrt(real_part * real_part + imag_part * imag_part + floor)
        put(f, real_part * inverse, imag_part * inverse)


def in_turns(count, transform, whiten, spec_a, spec_b):
    transform(0, spec_a)

    @pl.loop(0, count // 2)
    def _(pair):
        i = 2 * pair
        transform(i + 1, spec_b)
        whiten(i, spec_a)
        transform(jnp.minimum(i + 2, count - 1), spec_a)
        whiten(i + 1, spec_b)


def whiten_kernel(right_ref, odd_ref, table_ref, x0, b0, a1, b1, a2, b2, o5, out_ref,
                  band, spec_a, spec_b, bins_ref):
    segs = x0.shape[0]
    depth = 2 * segs
    pitch = depth + 1
    odd = odd_ref[0] == 1

    @pl.loop(0, segs)
    def _(s):
        band[s, 0:32, :] = x0[s]
        band[s, 32:64, :] = jnp.where(odd, b1[s], b0[s])
        band[s, 64:96, :] = a1[s]
        band[s, 96:128, :] = jnp.where(odd, b2[s], b1[s])
        band[s, 128:160, :] = a2[s]
        band[s, 160:176, :] = o5[s]

    starts = [pl.multiple_of(right_ref[q] * BLK, BLK) for q in range(SLOTS)]

    def transform(s, spec):
        rows = [band[s, pl.ds(start, BLK), :] for start in starts]
        spec[...] = lax.dot_general(
            table_ref[...],
            jnp.concatenate(rows, axis=0),
            (((1,), (1,)), ((), ())),
            preferred_element_type=jnp.float32,
        )

    def whiten(s, spec):
        for h in range(2):
            def put(f, real_part, imag_part):
                bins_ref[h, pl.ds(f * pitch + s, 8, stride=pitch), :] = real_part
                bins_ref[h, pl.ds(f * pitch + segs + s, 8, stride=pitch), :] = imag_part

            whiten_tile(spec, slice(h * 128, (h + 1) * 128), put)

    in_turns(segs, transform, whiten, spec_a, spec_b)

    @pl.loop(0, BINS // 4)
    def _(group):
        for step in range(4):
            f = group * 4 + step
            for h in range(2):
                out_ref[h, f] = bins_ref[h, pl.ds(f * pitch, depth), :].astype(jnp.bfloat16)


def whole(shape):
    return pl.BlockSpec(shape, lambda *_: (0,) * len(shape))


def whiten_bins(right, odd, table, whole_pieces, pieces, segs, offset):
    smem = pl.BlockSpec(memory_space=pltpu.SMEM)
    share = pl.BlockSpec((segs, 32, BINS), lambda _: (offset // segs, 0, 0))
    shape = (2, BINS, 2 * segs, 128)
    return pl.pallas_call(
        whiten_kernel,
        grid=(1,),
        out_shape=jax.ShapeDtypeStruct(shape, jnp.bfloat16),
        in_specs=[smem, smem, whole(table.shape), share, share] + [whole(p.shape) for p in pieces],
        out_specs=whole(shape),
        scratch_shapes=[
            pltpu.VMEM((segs, BAND, BINS), jnp.bfloat16),
            pltpu.VMEM((512, 256), jnp.float32),
            pltpu.VMEM((512, 256), jnp.float32),
            pltpu.VMEM((2, BINS * (2 * segs + 1), 128), jnp.float32),
        ],
        compiler_params=pltpu.CompilerParams(vmem_limit_bytes=(52 if segs > 16 else 32) * MIB),
        cost_estimate=pl.CostEstimate(flops=240_000_000 * segs, bytes_accessed=8_000_000, transcendentals=0),
        name="whiten",
    )(right, odd, table, *whole_pieces, *pieces)


def left_kernel(odd_ref, table_ref, x0, b0, *refs):
    pieces = refs[:len(CHUNKS)]
    out_ref, records, spec_a, spec_b, bins_ref = refs[len(CHUNKS):]
    odd = odd_ref[0] == 1
    segs = x0.shape[0]
    spread = LEFT + 1
    pitch = 2 * LEFT + 1
    offset = 0
    for piece in pieces:
        @pl.loop(0, piece.shape[0])
        def _(i, piece=piece, offset=offset):
            s = offset + i
            both = jnp.concatenate([x0[s], jnp.where(odd, piece[i], b0[s])], axis=0).astype(jnp.float32)
            for h in range(2):
                records[h, pl.ds(s * spread, LEFT), :] = both[:, h * 128:(h + 1) * 128]

        offset += piece.shape[0]

    def transform(quad, spec):
        rows = [
            jnp.concatenate([records[h, pl.ds(quad * 4 + k, segs, stride=spread), :] for h in range(2)], axis=1)
            for k in range(4)
        ]
        spec[...] = lax.dot_general(
            table_ref[...],
            jnp.concatenate(rows, axis=0).astype(jnp.bfloat16),
            (((1,), (1,)), ((), ())),
            preferred_element_type=jnp.float32,
        )

    in_first = lax.broadcasted_iota(jnp.int32, (8, 128), 1) < LEFT

    def whiten(quad, spec):
        for h in range(2):
            a = quad * 4 + 2 * h

            def put(f, real_part, imag_part):
                real_other = pltpu.roll(real_part, LEFT, 1)
                imag_other = pltpu.roll(imag_part, LEFT, 1)
                rows = [
                    (a, jnp.where(in_first, real_part, imag_other)),
                    (LEFT + a, jnp.where(in_first, imag_part, -real_other)),
                    (a + 1, jnp.where(in_first, real_other, imag_part)),
                    (LEFT + a + 1, jnp.where(in_first, imag_other, -real_part)),
                ]
                for row, value in rows:
                    bins_ref[pl.ds(f * pitch + row, 8, stride=pitch), :] = value

            whiten_tile(spec, slice(h * 128, (h + 1) * 128), put)

    in_turns(LEFT // 4, transform, whiten, spec_a, spec_b)

    @pl.loop(0, BINS // 4)
    def _(group):
        for step in range(4):
            f = group * 4 + step
            out_ref[f] = bins_ref[pl.ds(f * pitch, 2 * LEFT), :].astype(jnp.bfloat16)


def left_bins(odd, table, x0, b0, pieces):
    vmem = pl.BlockSpec(memory_space=pltpu.VMEM)
    smem = pl.BlockSpec(memory_space=pltpu.SMEM)
    return pl.pallas_call(
        left_kernel,
        out_shape=jax.ShapeDtypeStruct((BINS, 2 * LEFT, 128), jnp.bfloat16),
        in_specs=[smem] + [vmem] * (3 + len(pieces)),
        out_specs=vmem,
        scratch_shapes=[
            pltpu.VMEM((2, x0.shape[0] * (LEFT + 1), 128), jnp.float32),
            pltpu.VMEM((512, 256), jnp.float32),
            pltpu.VMEM((512, 256), jnp.float32),
            pltpu.VMEM((BINS * (2 * LEFT + 1), 128), jnp.float32),
        ],
        compiler_params=pltpu.CompilerParams(vmem_limit_bytes=48 * MIB),
        cost_estimate=pl.CostEstimate(flops=6_000_000_000, bytes_accessed=14_000_000, transcendentals=0),
        name="left",
    )(odd, table, x0, b0, *pieces)


def lag_sums(table_ref, cross_ref, lags):
    @pl.loop(0, BLK // 2)
    def _(pair):
        a = 2 * pair
        cross = jnp.concatenate(
            [cross_ref[pl.ds((a + k) * PITCH, 512), :].astype(jnp.bfloat16) for k in range(2)], axis=1
        )
        both = jnp.dot(table_ref[...], cross, preferred_element_type=jnp.float32)
        both = both[:ROWS] + both[ROWS:]
        lags[a] = both[:, :128]
        lags[a + 1] = both[:, 128:]


def by_slot(lags, put):
    block = lax.broadcasted_iota(jnp.int32, (BLK, 128), 1) // BLK
    odd_block = {d: (block // d) % 2 == 1 for d in (4, 2, 1)}

    @pl.loop(0, ROWS // BLK)
    def _(tile):
        rows = pl.ds(pl.multiple_of(tile * BLK, BLK), BLK)
        for ha in range(2):
            arrays = [lags[8 * ha + k, rows, :] for k in range(8)]
            for d in (4, 2, 1):
                for k in range(8):
                    if k & d == 0:
                        one, two = arrays[k], arrays[k + d]
                        arrays[k] = jnp.where(odd_block[d], pltpu.roll(two, BLK * d, 1), one)
                        arrays[k + d] = jnp.where(odd_block[d], two, pltpu.roll(one, 128 - BLK * d, 1))
            for k in range(8):
                put(k, rows, slice(ha * 128, (ha + 1) * 128), arrays[k])


def gram_kernel(tile, live_ref, first_ref, table_ref, left_ref, *refs):
    parts = refs[:len(CHUNKS)]
    outs = refs[len(CHUNKS):-2]
    sums, lags = refs[-2:]
    block = pl.program_id(0)
    bins = left_ref.shape[0]
    first = first_ref[...]
    chosen = [jnp.broadcast_to(first == i, (BLK, 128)) for i in range(3)]

    @pl.loop(0, bins // 4)
    def _(group):
        for step in range(4):
            local_bin = group * 4 + step
            f = block * bins + local_bin
            right = jnp.concatenate(
                [p[0, local_bin, part * n:(part + 1) * n, :] for part in range(2) for p, n in zip(parts, CHUNKS)],
                axis=0,
            )
            cross = jnp.dot(left_ref[local_bin], right, preferred_element_type=jnp.float32)
            for part in range(2):
                blocks = [cross[part * LEFT + i * BLK:part * LEFT + (i + 1) * BLK] for i in range(4)]
                own = blocks[3]
                for i in range(3):
                    own = jnp.where(chosen[i], blocks[i], own)
                for a in range(0, BLK, 8):
                    sums[pl.ds(a * PITCH + part * BINS + f, 8, stride=PITCH), :] = own[a:a + 8]

    @pl.when(block == pl.num_programs(0) - 1)
    def _():
        lag_sums(table_ref, sums, lags)
        live = [live_ref[8 * tile + q] == 1 for q in range(8)]

        def put(q, rows, lanes, value):
            value = jnp.where(live[q], value, 0.0)
            for out in outs:
                if q < out.shape[0]:
                    out[q, rows, lanes] = value.astype(out.dtype)
                    return
                q -= out.shape[0]

        by_slot(lags, put)


def gram(tile, live, first, table, left, parts, counts, dtype):
    step = 32
    shapes = [(n, ROWS, 256) for n in counts]
    return pl.pallas_call(
        functools.partial(gram_kernel, tile),
        grid=(BINS // step,),
        out_shape=[jax.ShapeDtypeStruct(s, dtype) for s in shapes],
        in_specs=[
            pl.BlockSpec(memory_space=pltpu.SMEM),
            pl.BlockSpec((1, 128), lambda k: (0, tile)),
            whole(table.shape),
            pl.BlockSpec((step,) + left.shape[1:], lambda k: (k, 0, 0)),
        ]
        + [pl.BlockSpec((1, step) + p.shape[2:], lambda k: (tile, k, 0, 0)) for p in parts],
        out_specs=[whole(s) for s in shapes],
        scratch_shapes=[
            pltpu.VMEM((BLK * PITCH, 128), jnp.float32),
            pltpu.VMEM((BLK, ROWS, 128), jnp.float32),
        ],
        compiler_params=pltpu.CompilerParams(vmem_limit_bytes=32 * MIB),
        cost_estimate=pl.CostEstimate(flops=16_000_000_000, bytes_accessed=20_000_000, transcendentals=0),
        name="gram",
    )(live, first, table, left, *parts)


def moved(block, axis, to):
    size = lax.axis_size(axis)
    return lax.ppermute(block, axis, [(i, to(i) % size) for i in range(size)])


def one_chip(block):
    return moved(block, "chan", lambda i: i - 2)


def swap(block):
    return moved(block, "chan", lambda i: i ^ 1)


def first_half(block, distance):
    return moved(block[:, :BLK], "chan", lambda i: i - distance)


def local(records, pair_blocks, pair_counts):
    segs = records.shape[0]
    table, backward = make_tables(segs * lax.axis_size("tm"))
    owner = lax.axis_index("chan")
    row = lax.axis_index("tm")

    group = np.array([2, 2, 1, 1, 2, 2, 3, 3, 1, 1, 3, 3, 0, 0, 0, 0], np.int32)
    inside = np.array([0, 1, 2, 3, 2, 3, 0, 1, 0, 1, 2, 3, 0, 1, 2, 3], np.int32)
    order = (row + group) % 4 * 4 + inside
    relative = pair_blocks[order] - 2 * owner
    first = jnp.clip(relative[:, 0], 0, 3)
    right = jnp.clip(relative[:, 1], 0, 10)
    live = (order < pair_counts[0]).astype(jnp.int32)
    odd = (owner % 2).astype(jnp.int32)[None]
    first_lanes = jnp.repeat(first, BLK)[None, :]

    barrier = lax.optimization_barrier
    starts = np.cumsum((0,) + CHUNKS)
    x = [records[starts[c]:starts[c + 1]] for c in range(len(CHUNKS))]

    def whitened(c, *pieces):
        return whiten_bins(right, odd, table, [records, b0], pieces, CHUNKS[c], int(starts[c]))

    a1_0, b0 = one_chip(x[0]), swap(records)
    x[1], a1_0 = barrier((x[1], a1_0))
    a2_0, b1_0, a1_1 = one_chip(a1_0), swap(a1_0), one_chip(x[1])
    x[2], a1_1 = barrier((x[2], a1_1))
    b2_0, o5_0, a2_1, b1_1, a1_2 = swap(a2_0), first_half(a2_0, 1), one_chip(a1_1), swap(a1_1), one_chip(x[2])
    part_0 = whitened(0, a1_0, b1_0, a2_0, b2_0, o5_0)
    a2_1, a1_2, part_0 = barrier((a2_1, a1_2, part_0))
    b2_1, o5_1 = swap(a2_1), first_half(a2_1, 1)
    a2_2, b1_2, o5_2 = one_chip(a1_2), swap(a1_2), first_half(a1_2, 3)
    left = left_bins(odd, table, records, b0, [b1_0, b1_1, b1_2])
    part_1 = whitened(1, a1_1, b1_1, a2_1, b2_1, o5_1)
    a2_2, o5_2, left, part_1 = barrier((a2_2, o5_2, left, part_1))
    b2_2 = swap(a2_2)
    part_2 = whitened(2, a1_2, b1_2, a2_2, b2_2, o5_2)

    parts = [part_0, part_1, part_2]
    plus, minus = gram(0, live, first_lanes, backward, left, parts, (4, 4), jnp.bfloat16)
    keep, other, own = gram(1, live, first_lanes, backward, left, parts, (2, 2, 4), jnp.float32)

    from_below = moved(plus, "tm", lambda i: i + 1)
    from_above = moved(minus, "tm", lambda i: i - 1)
    up = (keep + from_below[:2].astype(jnp.float32)).astype(jnp.bfloat16)
    down = (other + from_above[:2].astype(jnp.float32)).astype(jnp.bfloat16)
    two_below = moved(up, "tm", lambda i: i + 1)
    two_above = moved(down, "tm", lambda i: i - 1)
    f32 = jnp.float32
    low = own[:2] + from_above[2:].astype(f32) + two_below.astype(f32)
    high = own[2:] + from_below[2:].astype(f32) + two_above.astype(f32)
    return jnp.concatenate([low, high], axis=0)[:, :LAGS]


def solution(mesh):
    return jax.shard_map(
        local,
        mesh=mesh,
        in_specs=(P("tm", "chan", None), P("chan", None), P("chan")),
        out_specs=P(("chan", "tm"), None, None),
        check_vma=False,
    )
```

time: 914 us -> 169 us (0.18)
  waiting for transfers between devices: 393 us -> 36.7 us
  local copies, waits for them, and re-layouts: 239 us -> 15 us
  matrix products: 162 us -> 0 us
  Pallas kernels: 0 us -> 78.2 us
  loops' own time: 69.2 us -> 0 us
  starting transfers between devices: 6.45 us -> 34.4 us
  other arithmetic: 20.8 us -> 1.94 us
  between operations: 13.5 us -> 0.83 us
    ppermute x5 -> x20, waiting for transfers between devices: 256 us -> 36.7 us  [moved(): return lax.ppermute(block, axis, [(i, to(i) % size) for i in range(size)])]
    dot_general x66 -> x0, matrix products: 162 us -> none  [the longest x16 52.8 us: cross_spectrum(): jnp.einsum('saf,sbf->fab', left_real, right_real, preferred_element_type=...]
    reduce_scatter x1 -> x0, waiting for transfers between devices: 137 us -> none  [local(): lax.psum_scatter(partial_value, 'tm', scatter_dimension=0, tiled=True)]
    dot_general x64 -> x0, local copies, waits for them, and re-layouts: 95 us -> none  [the longest x16 25.4 us: cross_spectrum(): jnp.einsum('saf,sbf->fab', left_imag, right_imag, preferred_element_type=...]
    pallas_call x0 -> x6, Pallas kernels: none -> 78.2 us  [the longest x2 44.3 us: gram(): pl.pallas_call(functools.partial(gram_kernel, tile), grid=(BINS // step,)...]
    another operation x1 -> x0, loops' own time: 69.2 us -> none  [local(): lax.map(per_slot, jnp.arange(pair_blocks.shape[0], dtype=jnp.int32))]
    while x65 -> x0, local copies, waits for them, and re-layouts: 40.4 us -> none  [the longest x1 35 us: local(): lax.map(per_slot, jnp.arange(pair_blocks.shape[0], dtype=jnp.int32))]
    dynamic_slice x32 -> x0, local copies, waits for them, and re-layouts: 40.2 us -> none  [the longest x16 21.5 us: per_slot(): second_start = pair_blocks[slot_index, 1] * BLK - base_channel]
  transfers between devices with their start and end apart: 6 -> 20, of which waited for: 4 -> 6; matrix products, arithmetic and copies ran while one was open for 2% -> 3% of each run, Pallas kernels for 0% -> 31%
where the time goes in v2:
time: 169 us; the launch traced here: 167 us
  Pallas kernels  78.2 us (46%)
  waiting for transfers between devices  36.7 us (22%)
  starting transfers between devices  34.4 us (20%)
  local copies, waits for them, and re-layouts  15 us (9%)
  other arithmetic  1.94 us (1%)
    pallas_call x2, Pallas kernels, gram(): pl.pallas_call(functools.partial(gram_kernel, tile), grid=(BINS // step,)...  44.3 us
    ppermute x20, waiting for transfers between devices, moved(): return lax.ppermute(block, axis, [(i, to(i) % size) for i in range(size)])  36.7 us
    ppermute x20, starting transfers between devices, moved(): return lax.ppermute(block, axis, [(i, to(i) % size) for i in range(size)])  34.4 us
    pallas_call x3, Pallas kernels, whiten_bins(): pl.pallas_call(whiten_kernel, grid=(1,), out_shape=jax.ShapeDtypeStruct(s...  23.9 us
    pallas_call x1, Pallas kernels, left_bins(): pl.pallas_call(left_kernel, out_shape=jax.ShapeDtypeStruct((BINS, 2 * LEF...  9.97 us
    unnamed x29, local copies, waits for them, and re-layouts  8.48 us
  transfers between devices with their start and end apart: 20, of which 6 were waited for; matrix products, arithmetic and copies ran while one was open for 3% of the time, Pallas kernels for 31%

profile of v2, /device:TPU:0, one launch (start us, length us, event | category | flops | bytes accessed | tf_op | source)
XLA Modules:
  0.0 167.1 jit_solution(10444736076150456174)
XLA Ops:
  0.0 1.2 slice.48
  1.2 6.4 %collective-permute-start = (bf16[32,32,256]{2,1,0:T(8,128)(2,1)S(1)}, bf16[32,32,256]{2,1,0:T(8,128)(2,1)S(1)}, u32[]{:S(2)}, u32[]{:S(2)}) collective-permute-start(bf16[32,32,256]{2,1,0:T(8,128)(2,1)S(1)} %slice.48), channel_id=1, source_target_pairs={{0,62},{1,63},{2,0},{3,1},{4,2},{5,3},{6,4},{7,5},{8,6},{9,7},{10,... | collective-permute-start | bytes 1572872 | tf_op jit(solution)/shard_map/ppermute | solution.py:327
  7.6 1.9 %fusion.6 = (bf16[16,32,256]{2,1,0:T(8,128)(2,1)}, bf16[16,32,256]{2,1,0:T(8,128)(2,1)}) fusion(bf16[64,32,256]{2,1,0:T(8,128)(2,1)} %x0.7), kind=kLoop, calls=%fused_computation.20 | loop fusion | bytes 1048576 | tf_op jit(solution)/shard_map/slice | solution.py:360
  9.4 9.3 %collective-permute-done.a1 = bf16[32,32,256]{2,1,0:T(8,128)(2,1)S(1)} collective-permute-done((bf16[32,32,256]{2,1,0:T(8,128)(2,1)S(1)}, bf16[32,32,256]{2,1,0:T(8,128)(2,1)S(1)}, u32[]{:S(2)}, u32[]{:S(2)}) %collective-permute-start) | collective-permute-done | bytes 524320 | tf_op jit(solution)/shard_map/ppermute | solution.py:327
  18.8 5.8 %collective-permute-start.6 = (bf16[32,32,256]{2,1,0:T(8,128)(2,1)S(1)}, bf16[32,32,256]{2,1,0:T(8,128)(2,1)}, u32[]{:S(2)}, u32[]{:S(2)}) collective-permute-start(bf16[32,32,256]{2,1,0:T(8,128)(2,1)S(1)} %collective-permute-done.a1), channel_id=1, source_target_pairs={{0,62},{1,63},{2,0},{3,1},{4,2},{5,3},{6,4},{7,5},{8,6},{9,7},{10,... | collective-permute-start | bytes 1572872 | tf_op jit(solution)/shard_map/ppermute | solution.py:327
  24.6 0.0 collective-permute-start.4
  24.6 0.5 collective-permute-start.5
  25.1 9.8 %collective-permute-done.6.a2 = bf16[32,32,256]{2,1,0:T(8,128)(2,1)} collective-permute-done((bf16[32,32,256]{2,1,0:T(8,128)(2,1)S(1)}, bf16[32,32,256]{2,1,0:T(8,128)(2,1)}, u32[]{:S(2)}, u32[]{:S(2)}) %collective-permute-start.6) | collective-permute-done | bytes 524320 | tf_op jit(solution)/shard_map/ppermute | solution.py:327
  34.9 0.0 collective-permute-start.7
  34.9 0.5 compare_select_fusion
  35.4 0.1 copy.10
  35.5 0.6 gather_fusion
  36.1 6.0 %collective-permute-start.1 = (bf16[16,32,256]{2,1,0:T(8,128)(2,1)}, bf16[16,32,256]{2,1,0:T(8,128)(2,1)S(1)}, u32[]{:S(2)}, u32[]{:S(2)}) collective-permute-start(bf16[16,32,256]{2,1,0:T(8,128)(2,1)} %get-tuple-element.21), channel_id=1, source_target_pairs={{0,62},{1,63},{2,0},{3,1},{4,2},{5,3},{6,4},{7,5},{8,6},{9,7},{10,... | collective-permute-start | bytes 786440 | tf_op jit(solution)/shard_map/ppermute | solution.py:327
  42.1 1.0 slice.64
  43.0 0.2 collective-permute-start.8
  43.2 0.2 fusion
  43.4 5.2 %collective-permute-done.1.a1 = bf16[16,32,256]{2,1,0:T(8,128)(2,1)S(1)} collective-permute-done((bf16[16,32,256]{2,1,0:T(8,128)(2,1)}, bf16[16,32,256]{2,1,0:T(8,128)(2,1)S(1)}, u32[]{:S(2)}, u32[]{:S(2)}) %collective-permute-start.1) | collective-permute-done | bytes 262176 | tf_op jit(solution)/shard_map/ppermute | solution.py:327
  48.6 0.0 collective-permute-start.11
  48.6 0.0 collective-permute-done.5.b1.refs_0_
  48.6 5.7 %collective-permute-start.2 = (bf16[16,32,256]{2,1,0:T(8,128)(2,1)S(1)}, bf16[16,32,256]{2,1,0:T(8,128)(2,1)S(1)}, u32[]{:S(2)}, u32[]{:S(2)}) collective-permute-start(bf16[16,32,256]{2,1,0:T(8,128)(2,1)S(1)} %collective-permute-done.1.a1), channel_id=1, source_target_pairs={{0,62},{1,63},{2,0},{3,1},{4,2},{5,3},{6,4},{7,5},{8,6},{9,7},{10,... | collective-permute-start | bytes 786440 | tf_op jit(solution)/shard_map/ppermute | solution.py:327
  54.3 0.0 collective-permute-done.4.b0
  54.3 0.1 collective-permute-start.3
  54.4 0.0 collective-permute-done.8.o5
  54.4 0.0 collective-permute-done.7.b2
  54.4 0.9 copy-done.2
  55.3 0.9 copy-done.6
  56.2 13.6 %whiten.3.refs_0_ = bf16[2,256,64,128]{3,2,1,0:T(8,128)(2,1)} custom-call(s32[16]{0:T(128)S(1)} %get-tuple-element.37.right_ref, s32[1]{0:T(128)} %bitcast.1.odd_ref, bf16[512,256]{1,0:T(8,128)(2,1)S(1)} %copy-done.6, bf16[64,32,256]{2,1,0:T(8,128)(2,1)} %x0.7, bf16[64,32,256]{2,1,0:T(8,128)(2,1)} %copy-done.2, ...), custom_call_target="tpu_custom_call" | custom-call | flops 7680000000 | bytes 8000000 | tf_op jit(solution)/shard_map/whiten/pallas_call | solution.py:128
  69.8 0.0 collective-permute-done.3.a1
  69.8 0.0 collective-permute-done.2.a2
  69.8 0.4 collective-permute-start.12
  70.2 0.3 collective-permute-start.13
  70.6 2.1 %collective-permute-start.9 = (bf16[16,32,256]{2,1,0:T(8,128)(2,1)S(1)}, bf16[16,32,256]{2,1,0:T(8,128)(2,1)S(1)}, u32[]{:S(2)}, u32[]{:S(2)}) collective-permute-start(bf16[16,32,256]{2,1,0:T(8,128)(2,1)S(1)} %collective-permute-done.3.a1), channel_id=1, source_target_pairs={{0,62},{1,63},{2,0},{3,1},{4,2},{5,3},{6,4},{7,5},{8,6},{9,7},{10,... | collective-permute-start | bytes 786440 | tf_op jit(solution)/shard_map/ppermute | solution.py:327
  72.6 0.0 collective-permute-start.10
  72.6 0.0 collective-permute-done.11.refs_1_.b1
  72.6 0.1 collective-permute-start.14
  72.7 0.0 collective-permute-done.12.refs_2_.b1
  72.7 1.2 copy-done.3
  73.9 10.0 %left.1.left_ref = bf16[256,128,128]{2,1,0:T(8,128)(2,1)} custom-call(s32[1]{0:T(128)} %bitcast.1.odd_ref, bf16[512,256]{1,0:T(8,128)(2,1)S(1)} %copy-done.6, bf16[64,32,256]{2,1,0:T(8,128)(2,1)S(1)} %copy-done.1, bf16[64,32,256]{2,1,0:T(8,128)(2,1)S(1)} %copy-done.3, bf16[32,32,256]{2,1,0:T(8,128)(2,1)S(1)} %collective-permute-done.5.b1.refs_0_, ...), custom_call_target="tpu_custom_call" | custom-call | flops 6000000000 | bytes 14000000 | tf_op jit(solution)/shard_map/left/pallas_call | solution.py:208
  83.9 0.2 collective-permute-done.14.o5
  84.1 0.0 collective-permute-done.13.b2
  84.1 5.2 %whiten.4.refs_1_ = bf16[2,256,32,128]{3,2,1,0:T(8,128)(2,1)S(1)} custom-call(s32[16]{0:T(128)S(1)} %get-tuple-element.37.right_ref, s32[1]{0:T(128)} %bitcast.1.odd_ref, bf16[512,256]{1,0:T(8,128)(2,1)S(1)} %copy-done.6, bf16[64,32,256]{2,1,0:T(8,128)(2,1)S(1)} %copy-done.1, bf16[64,32,256]{2,1,0:T(8,128)(2,1)S(1)} %copy-done.3, ...), custom_call_target="tpu_custom_call" | custom-call | flops 3840000000 | bytes 8000000 | tf_op jit(solution)/shard_map/whiten/pallas_call | solution.py:128
  89.2 1.9 %copy-done.8 = bf16[2,256,32,128]{3,2,1,0:T(8,128)(2,1)} copy-done((bf16[2,256,32,128]{3,2,1,0:T(8,128)(2,1)}, bf16[2,256,32,128]{3,2,1,0:T(8,128)(2,1)S(1)}, u32[]{:S(2)}) %copy-start.8) | copy-done | bytes 4194328
  91.2 0.0 collective-permute-done.10.o5
  91.2 0.0 collective-permute-done.9.a2
  91.2 0.4 collective-permute-start.15
  92.3 0.1 broadcast_in_dim.10
  92.3 0.1 broadcast_in_dim_reshape.3.first_ref
  92.4 0.6 compare_convert_fusion.live_ref
  93.0 0.0 collective-permute-done.15.b2
  93.1 5.2 %whiten.5.refs_2_ = bf16[2,256,32,128]{3,2,1,0:T(8,128)(2,1)S(1)} custom-call(s32[16]{0:T(128)S(1)} %get-tuple-element.37.right_ref, s32[1]{0:T(128)} %bitcast.1.odd_ref, bf16[512,256]{1,0:T(8,128)(2,1)S(1)} %copy-done.7, bf16[64,32,256]{2,1,0:T(8,128)(2,1)S(1)} %copy-done.1, bf16[64,32,256]{2,1,0:T(8,128)(2,1)S(1)} %copy-done.4, ...), custom_call_target="tpu_custom_call" | custom-call | flops 3840000000 | bytes 8000000 | tf_op jit(solution)/shard_map/whiten/pallas_call | solution.py:128
  98.3 3.4 %copy-done.10 = bf16[256,128,128]{2,1,0:T(8,128)(2,1)S(1)} copy-done((bf16[256,128,128]{2,1,0:T(8,128)(2,1)S(1)}, bf16[256,128,128]{2,1,0:T(8,128)(2,1)}, u32[]{:S(2)}) %copy-start.10) | copy-done | bytes 8388632
  101.6 22.0 %gram.3 = (bf16[4,416,256]{2,1,0:T(8,128)(2,1)S(1)}, bf16[4,416,256]{2,1,0:T(8,128)(2,1)S(1)}) custom-call(s32[16]{0:T(128)S(1)} %compare_convert_fusion.live_ref, s32[1,256]{1,0:T(1,128)S(1)} %broadcast_in_dim_reshape.3.first_ref, bf16[832,512]{1,0:T(8,128)(2,1)S(1)} %copy-done.5, bf16[256,128,128]{2,1,0:T(8,128)(2,1)S(1)} %copy-done.10, ...), custom_call_target="tpu_custom_call" | custom-call | flops 16000000000 | bytes 20000000 | tf_op jit(solution)/shard_map/gram/pallas_call | solution.py:303
  123.6 3.1 %collective-permute-start.16 = (bf16[4,416,256]{2,1,0:T(8,128)(2,1)S(1)}, bf16[4,416,256]{2,1,0:T(8,128)(2,1)S(1)}, u32[]{:S(2)}, u32[]{:S(2)}) collective-permute-start(bf16[4,416,256]{2,1,0:T(8,128)(2,1)S(1)} %get-tuple-element.33), channel_id=1, source_target_pairs={{0,192},{64,0},{128,64},{192,128},{1,193},{65,1},{129,65},{193,129... | collective-permute-start | bytes 2555912 | tf_op jit(solution)/shard_map/ppermute | solution.py:327
  126.7 22.4 %gram.2 = (f32[2,416,256]{2,1,0:T(8,128)S(1)}, f32[2,416,256]{2,1,0:T(8,128)S(1)}, f32[4,416,256]{2,1,0:T(8,128)S(1)}) custom-call(s32[16]{0:T(128)S(1)} %compare_convert_fusion.live_ref, s32[1,256]{1,0:T(1,128)S(1)} %broadcast_in_dim_reshape.3.first_ref, bf16[832,512]{1,0:T(8,128)(2,1)S(1)} %copy-done.5, bf16[256,128,128]{2,1,0:T(8,128)(2,1)S(1)} %copy-done.10, ...), custom_call_target="tpu_custom_call" | custom-call | flops 16000000000 | bytes 20000000 | tf_op jit(solution)/shard_map/gram/pallas_call | solution.py:303
  149.1 0.0 collective-permute-done.16
  149.1 0.1 add_convert_fusion
  149.2 3.3 %collective-permute-start.19 = (bf16[2,416,256]{2,1,0:T(8,128)(2,1)S(1)}, bf16[2,416,256]{2,1,0:T(8,128)(2,1)S(1)}, u32[]{:S(2)}, u32[]{:S(2)}) collective-permute-start(bf16[2,416,256]{2,1,0:T(8,128)(2,1)S(1)} %add_convert_fusion), channel_id=1, source_target_pairs={{0,192},{64,0},{128,64},{192,128},{1,193},{65,1},{129,65},{193,129... | collective-permute-start | bytes 1277960 | tf_op jit(solution)/shard_map/ppermute | solution.py:327
  152.5 0.1 add_convert_fusion.1
  152.6 0.1 collective-permute-start.18
  152.7 8.6 %collective-permute-done.19 = bf16[2,416,256]{2,1,0:T(8,128)(2,1)S(1)} collective-permute-done((bf16[2,416,256]{2,1,0:T(8,128)(2,1)S(1)}, bf16[2,416,256]{2,1,0:T(8,128)(2,1)S(1)}, u32[]{:S(2)}, u32[]{:S(2)}) %collective-permute-start.19) | collective-permute-done | bytes 426016 | tf_op jit(solution)/shard_map/ppermute | solution.py:327
  161.3 3.6 %collective-permute-done.18 = bf16[2,416,256]{2,1,0:T(8,128)(2,1)S(1)} collective-permute-done((bf16[2,416,256]{2,1,0:T(8,128)(2,1)S(1)}, bf16[2,416,256]{2,1,0:T(8,128)(2,1)S(1)}, u32[]{:S(2)}, u32[]{:S(2)}) %collective-permute-start.18) | collective-permute-done | bytes 426016 | tf_op jit(solution)/shard_map/ppermute | solution.py:327
  164.9 0.2 convert_add_fusion.1
  165.2 0.2 pad_maximum_fusion
  165.3 1.8 %copy.11 = f32[4,401,256]{2,0,1:T(4,128)} copy(f32[4,401,256]{2,1,0:T(8,128)S(1)} %pad_maximum_fusion) | data formatting | bytes 3284992 | tf_op jit(solution)/shard_map/slice | solution.py:393
  (29 shorter events, 0.1 us)
Async XLA Ops:
  0.0 34.9 %copy-start.12 = (s32[16]{0:T(128)S(1)}, s32[16]{0:T(128)}, u32[]{:S(2)}) copy-start(s32[16]{0:T(128)} %constant.53.clone) | copy-start | bytes 196
  0.0 34.9 %copy-start.13 = (s32[16]{0:T(128)S(1)}, s32[16]{0:T(128)}, u32[]{:S(2)}) copy-start(s32[16]{0:T(128)} %constant.52.clone) | copy-start | bytes 196
  0.0 24.6 %copy-start = (bf16[64,32,256]{2,1,0:T(8,128)(2,1)S(1)}, bf16[64,32,256]{2,1,0:T(8,128)(2,1)}, u32[]{:S(2)}) copy-start(bf16[64,32,256]{2,1,0:T(8,128)(2,1)} %x0.7) | copy-start | bytes 3145732
  0.0 35.4 %copy-start.11 = (s32[16,2]{0,1:T(2,128)S(1)}, s32[16,2]{0,1:T(2,128)}, u32[]{:S(2)}) copy-start(s32[16,2]{0,1:T(2,128)} %param.8) | copy-start | bytes 388
  1.2 17.6 %collective-permute-start = (bf16[32,32,256]{2,1,0:T(8,128)(2,1)S(1)}, bf16[32,32,256]{2,1,0:T(8,128)(2,1)S(1)}, u32[]{:S(2)}, u32[]{:S(2)}) collective-permute-start(bf16[32,32,256]{2,1,0:T(8,128)(2,1)S(1)} %slice.48), channel_id=1, source_target_pairs={{0,62},{1,63},{2,0},{3,1},{4,2},{5,3},{6,4},{7,5},{8,6},{9,7},{10,... | collective-permute-start | bytes 1572872 | tf_op jit(solution)/shard_map/ppermute | solution.py:327
  18.8 16.1 %collective-permute-start.6 = (bf16[32,32,256]{2,1,0:T(8,128)(2,1)S(1)}, bf16[32,32,256]{2,1,0:T(8,128)(2,1)}, u32[]{:S(2)}, u32[]{:S(2)}) collective-permute-start(bf16[32,32,256]{2,1,0:T(8,128)(2,1)S(1)} %collective-permute-done.a1), channel_id=1, source_target_pairs={{0,62},{1,63},{2,0},{3,1},{4,2},{5,3},{6,4},{7,5},{8,6},{9,7},{10,... | collective-permute-start | bytes 1572872 | tf_op jit(solution)/shard_map/ppermute | solution.py:327
  24.6 29.7 %collective-permute-start.4 = (bf16[64,32,256]{2,1,0:T(8,128)(2,1)S(1)}, bf16[64,32,256]{2,1,0:T(8,128)(2,1)S(1)}, u32[]{:S(2)}, u32[]{:S(2)}) collective-permute-start(bf16[64,32,256]{2,1,0:T(8,128)(2,1)S(1)} %copy-done), channel_id=1, source_target_pairs={{0,1},{1,0},{2,3},{3,2},{4,5},{5,4},{6,7},{7,6},{8,9},{9,8},{10,11... | collective-permute-start | bytes 3145736 | tf_op jit(solution)/shard_map/ppermute | solution.py:327
  24.6 24.0 %collective-permute-start.5 = (bf16[32,32,256]{2,1,0:T(8,128)(2,1)S(1)}, bf16[32,32,256]{2,1,0:T(8,128)(2,1)S(1)}, u32[]{:S(2)}, u32[]{:S(2)}) collective-permute-start(bf16[32,32,256]{2,1,0:T(8,128)(2,1)S(1)} %collective-permute-done.a1), channel_id=1, source_target_pairs={{0,1},{1,0},{2,3},{3,2},{4,5},{5,4},{6,7},{7,6},{8,9},{9,8},{10,11... | collective-permute-start | bytes 1572872 | tf_op jit(solution)/shard_map/ppermute | solution.py:327
  34.9 19.6 %collective-permute-start.7 = (bf16[32,32,256]{2,1,0:T(8,128)(2,1)}, bf16[32,32,256]{2,1,0:T(8,128)(2,1)}, u32[]{:S(2)}, u32[]{:S(2)}) collective-permute-start(bf16[32,32,256]{2,1,0:T(8,128)(2,1)} %collective-permute-done.6.a2), channel_id=1, source_target_pairs={{0,1},{1,0},{2,3},{3,2},{4,5},{5,4},{6,7},{7,6},{8,9},{9,8},{10,11... | collective-permute-start | bytes 1572872 | tf_op jit(solution)/shard_map/ppermute | solution.py:327
  36.1 12.5 %collective-permute-start.1 = (bf16[16,32,256]{2,1,0:T(8,128)(2,1)}, bf16[16,32,256]{2,1,0:T(8,128)(2,1)S(1)}, u32[]{:S(2)}, u32[]{:S(2)}) collective-permute-start(bf16[16,32,256]{2,1,0:T(8,128)(2,1)} %get-tuple-element.21), channel_id=1, source_target_pairs={{0,62},{1,63},{2,0},{3,1},{4,2},{5,3},{6,4},{7,5},{8,6},{9,7},{10,... | collective-permute-start | bytes 786440 | tf_op jit(solution)/shard_map/ppermute | solution.py:327
  43.0 11.4 %collective-permute-start.8 = (bf16[32,16,256]{2,1,0:T(8,128)(2,1)S(1)}, bf16[32,16,256]{2,1,0:T(8,128)(2,1)S(1)}, u32[]{:S(2)}, u32[]{:S(2)}) collective-permute-start(bf16[32,16,256]{2,1,0:T(8,128)(2,1)S(1)} %slice.64), channel_id=1, source_target_pairs={{0,63},{1,0},{2,1},{3,2},{4,3},{5,4},{6,5},{7,6},{8,7},{9,8},{10,9... | collective-permute-start | bytes 786440 | tf_op jit(solution)/shard_map/ppermute | solution.py:327
  48.6 24.0 %collective-permute-start.11 = (bf16[16,32,256]{2,1,0:T(8,128)(2,1)S(1)}, bf16[16,32,256]{2,1,0:T(8,128)(2,1)S(1)}, u32[]{:S(2)}, u32[]{:S(2)}) collective-permute-start(bf16[16,32,256]{2,1,0:T(8,128)(2,1)S(1)} %collective-permute-done.1.a1), channel_id=1, source_target_pairs={{0,1},{1,0},{2,3},{3,2},{4,5},{5,4},{6,7},{7,6},{8,9},{9,8},{10,11... | collective-permute-start | bytes 786440 | tf_op jit(solution)/shard_map/ppermute | solution.py:327
  48.6 21.2 %collective-permute-start.2 = (bf16[16,32,256]{2,1,0:T(8,128)(2,1)S(1)}, bf16[16,32,256]{2,1,0:T(8,128)(2,1)S(1)}, u32[]{:S(2)}, u32[]{:S(2)}) collective-permute-start(bf16[16,32,256]{2,1,0:T(8,128)(2,1)S(1)} %collective-permute-done.1.a1), channel_id=1, source_target_pairs={{0,62},{1,63},{2,0},{3,1},{4,2},{5,3},{6,4},{7,5},{8,6},{9,7},{10,... | collective-permute-start | bytes 786440 | tf_op jit(solution)/shard_map/ppermute | solution.py:327
  54.3 1.0 copy-start.2
  54.3 15.5 %collective-permute-start.3 = (bf16[16,32,256]{2,1,0:T(8,128)(2,1)}, bf16[16,32,256]{2,1,0:T(8,128)(2,1)S(1)}, u32[]{:S(2)}, u32[]{:S(2)}) collective-permute-start(bf16[16,32,256]{2,1,0:T(8,128)(2,1)} %get-tuple-element.23), channel_id=1, source_target_pairs={{0,62},{1,63},{2,0},{3,1},{4,2},{5,3},{6,4},{7,5},{8,6},{9,7},{10,... | collective-permute-start | bytes 786440 | tf_op jit(solution)/shard_map/ppermute | solution.py:327
  55.3 0.9 copy-start.6
  56.2 16.5 %copy-start.1 = (bf16[64,32,256]{2,1,0:T(8,128)(2,1)S(1)}, bf16[64,32,256]{2,1,0:T(8,128)(2,1)}, u32[]{:S(2)}) copy-start(bf16[64,32,256]{2,1,0:T(8,128)(2,1)} %x0.7) | copy-start | bytes 3145732
  69.8 2.9 %collective-permute-start.12 = (bf16[16,32,256]{2,1,0:T(8,128)(2,1)S(1)}, bf16[16,32,256]{2,1,0:T(8,128)(2,1)S(1)}, u32[]{:S(2)}, u32[]{:S(2)}) collective-permute-start(bf16[16,32,256]{2,1,0:T(8,128)(2,1)S(1)} %collective-permute-done.3.a1), channel_id=1, source_target_pairs={{0,1},{1,0},{2,3},{3,2},{4,5},{5,4},{6,7},{7,6},{8,9},{9,8},{10,11... | collective-permute-start | bytes 786440 | tf_op jit(solution)/shard_map/ppermute | solution.py:327
  70.2 13.8 %collective-permute-start.13 = (bf16[16,32,256]{2,1,0:T(8,128)(2,1)S(1)}, bf16[16,32,256]{2,1,0:T(8,128)(2,1)S(1)}, u32[]{:S(2)}, u32[]{:S(2)}) collective-permute-start(bf16[16,32,256]{2,1,0:T(8,128)(2,1)S(1)} %collective-permute-done.2.a2), channel_id=1, source_target_pairs={{0,1},{1,0},{2,3},{3,2},{4,5},{5,4},{6,7},{7,6},{8,9},{9,8},{10,11... | collective-permute-start | bytes 786440 | tf_op jit(solution)/shard_map/ppermute | solution.py:327
  70.6 20.6 %collective-permute-start.9 = (bf16[16,32,256]{2,1,0:T(8,128)(2,1)S(1)}, bf16[16,32,256]{2,1,0:T(8,128)(2,1)S(1)}, u32[]{:S(2)}, u32[]{:S(2)}) collective-permute-start(bf16[16,32,256]{2,1,0:T(8,128)(2,1)S(1)} %collective-permute-done.3.a1), channel_id=1, source_target_pairs={{0,62},{1,63},{2,0},{3,1},{4,2},{5,3},{6,4},{7,5},{8,6},{9,7},{10,... | collective-permute-start | bytes 786440 | tf_op jit(solution)/shard_map/ppermute | solution.py:327
  72.6 18.6 %collective-permute-start.10 = (bf16[16,16,256]{2,1,0:T(8,128)(2,1)S(1)}, bf16[16,16,256]{2,1,0:T(8,128)(2,1)S(1)}, u32[]{:S(2)}, u32[]{:S(2)}) collective-permute-start(bf16[16,16,256]{2,1,0:T(8,128)(2,1)S(1)} %slice.51), channel_id=1, source_target_pairs={{0,61},{1,62},{2,63},{3,0},{4,1},{5,2},{6,3},{7,4},{8,5},{9,6},{10... | collective-permute-start | bytes 393224 | tf_op jit(solution)/shard_map/ppermute | solution.py:327
  72.6 11.4 %collective-permute-start.14 = (bf16[16,16,256]{2,1,0:T(8,128)(2,1)S(1)}, bf16[16,16,256]{2,1,0:T(8,128)(2,1)S(1)}, u32[]{:S(2)}, u32[]{:S(2)}) collective-permute-start(bf16[16,16,256]{2,1,0:T(8,128)(2,1)S(1)} %slice.52), channel_id=1, source_target_pairs={{0,63},{1,0},{2,1},{3,2},{4,3},{5,4},{6,5},{7,6},{8,7},{9,8},{10,9... | collective-permute-start | bytes 393224 | tf_op jit(solution)/shard_map/ppermute | solution.py:327
  72.7 1.2 copy-start.3
  83.9 9.1 %copy-start.4 = (bf16[64,32,256]{2,1,0:T(8,128)(2,1)S(1)}, bf16[64,32,256]{2,1,0:T(8,128)(2,1)}, u32[]{:S(2)}) copy-start(bf16[64,32,256]{2,1,0:T(8,128)(2,1)} %copy-done.2) | copy-start | bytes 3145732
  83.9 9.1 %copy-start.7 = (bf16[512,256]{1,0:T(8,128)(2,1)S(1)}, bf16[512,256]{1,0:T(8,128)(2,1)}, u32[]{:S(2)}) copy-start(bf16[512,256]{1,0:T(8,128)(2,1)} %constant.54.clone.table_ref) | copy-start | bytes 786436
  89.2 2.0 %copy-start.8 = (bf16[2,256,32,128]{3,2,1,0:T(8,128)(2,1)}, bf16[2,256,32,128]{3,2,1,0:T(8,128)(2,1)S(1)}, u32[]{:S(2)}) copy-start(bf16[2,256,32,128]{3,2,1,0:T(8,128)(2,1)S(1)} %whiten.4.refs_1_) | copy-start | bytes 12582916
  91.2 1.8 %collective-permute-start.15 = (bf16[16,32,256]{2,1,0:T(8,128)(2,1)S(1)}, bf16[16,32,256]{2,1,0:T(8,128)(2,1)S(1)}, u32[]{:S(2)}, u32[]{:S(2)}) collective-permute-start(bf16[16,32,256]{2,1,0:T(8,128)(2,1)S(1)} %collective-permute-done.9.a2), channel_id=1, source_target_pairs={{0,1},{1,0},{2,3},{3,2},{4,5},{5,4},{6,7},{7,6},{8,9},{9,8},{10,11... | collective-permute-start | bytes 786440 | tf_op jit(solution)/shard_map/ppermute | solution.py:327
  93.0 5.2 %copy-start.5 = (bf16[832,512]{1,0:T(8,128)(2,1)S(1)}, bf16[832,512]{1,0:T(8,128)(2,1)}, u32[]{:S(2)}) copy-start(bf16[832,512]{1,0:T(8,128)(2,1)} %constant.55.clone.table_ref) | copy-start | bytes 2555908
  93.0 5.2 %copy-start.9 = (bf16[2,256,32,128]{3,2,1,0:T(8,128)(2,1)S(1)}, bf16[2,256,32,128]{3,2,1,0:T(8,128)(2,1)}, u32[]{:S(2)}) copy-start(bf16[2,256,32,128]{3,2,1,0:T(8,128)(2,1)} %copy-done.8) | copy-start | bytes 12582916
  98.2 3.4 %copy-start.10 = (bf16[256,128,128]{2,1,0:T(8,128)(2,1)S(1)}, bf16[256,128,128]{2,1,0:T(8,128)(2,1)}, u32[]{:S(2)}) copy-start(bf16[256,128,128]{2,1,0:T(8,128)(2,1)} %left.1.left_ref) | copy-start | bytes 25165828
  123.6 25.5 %collective-permute-start.16 = (bf16[4,416,256]{2,1,0:T(8,128)(2,1)S(1)}, bf16[4,416,256]{2,1,0:T(8,128)(2,1)S(1)}, u32[]{:S(2)}, u32[]{:S(2)}) collective-permute-start(bf16[4,416,256]{2,1,0:T(8,128)(2,1)S(1)} %get-tuple-element.33), channel_id=1, source_target_pairs={{0,192},{64,0},{128,64},{192,128},{1,193},{65,1},{129,65},{193,129... | collective-permute-start | bytes 2555912 | tf_op jit(solution)/shard_map/ppermute | solution.py:327
  126.7 25.8 %collective-permute-start.17 = (bf16[4,416,256]{2,1,0:T(8,128)(2,1)S(1)}, bf16[4,416,256]{2,1,0:T(8,128)(2,1)S(1)}, u32[]{:S(2)}, u32[]{:S(2)}) collective-permute-start(bf16[4,416,256]{2,1,0:T(8,128)(2,1)S(1)} %get-tuple-element.35), channel_id=1, source_target_pairs={{0,64},{64,128},{128,192},{192,0},{1,65},{65,129},{129,193},{193,1... | collective-permute-start | bytes 2555912 | tf_op jit(solution)/shard_map/ppermute | solution.py:327
  149.2 12.1 %collective-permute-start.19 = (bf16[2,416,256]{2,1,0:T(8,128)(2,1)S(1)}, bf16[2,416,256]{2,1,0:T(8,128)(2,1)S(1)}, u32[]{:S(2)}, u32[]{:S(2)}) collective-permute-start(bf16[2,416,256]{2,1,0:T(8,128)(2,1)S(1)} %add_convert_fusion), channel_id=1, source_target_pairs={{0,192},{64,0},{128,64},{192,128},{1,193},{65,1},{129,65},{193,129... | collective-permute-start | bytes 1277960 | tf_op jit(solution)/shard_map/ppermute | solution.py:327
  152.6 12.3 %collective-permute-start.18 = (bf16[2,416,256]{2,1,0:T(8,128)(2,1)S(1)}, bf16[2,416,256]{2,1,0:T(8,128)(2,1)S(1)}, u32[]{:S(2)}, u32[]{:S(2)}) collective-permute-start(bf16[2,416,256]{2,1,0:T(8,128)(2,1)S(1)} %add_convert_fusion.1), channel_id=1, source_target_pairs={{0,64},{64,128},{128,192},{192,0},{1,65},{65,129},{129,193},{193,1... | collective-permute-start | bytes 1277960 | tf_op jit(solution)/shard_map/ppermute | solution.py:327

commit v3 on v2

--- a/solution.py
+++ b/solution.py
@@ -11,14 +11,16 @@
 from jax.sharding import PartitionSpec as P
 
 LAGS = 401
-ROWS = 416
+HALF = 208
+ROWS = 2 * HALF
 BLK = 16
 SLOTS = 16
 BINS = 256
 LEFT = 64
 BAND = 176
-CHUNKS = (32, 16, 16)
+CHUNKS = (32, 32)
 PITCH = 513
+GROUP = 16
 
 water_share = 0.1
 tiny_eps = 1e-06
@@ -32,17 +34,16 @@
     scale = np.float32(2.0 * math.pi / length)
     radians = (index[:, None] * index[None, :] % length).astype(np.float32) * scale
     forward = np.concatenate([np.cos(radians), -np.sin(radians)], axis=1)
-    lag_shift = np.arange(LAGS, dtype=np.int32)[:, None] - (LAGS - 1) // 2
-    lag_radians = (lag_shift * index[None, :] % length).astype(np.float32) * scale
+    shift = np.arange(HALF, dtype=np.int32)[:, None]
+    lag_radians = (shift * index[None, :] % length).astype(np.float32) * scale
     weight = np.where(index == 0, 1.0, 2.0).astype(np.float32)[None, :] / np.float32(
         math.sqrt(float(BINS * segments))
     )
-    backward = np.concatenate([np.cos(lag_radians) * weight, -np.sin(lag_radians) * weight], axis=1)
-    backward = np.pad(backward.astype(np.float32), ((0, ROWS - LAGS), (0, 0)))
-    high = backward.astype(ml_dtypes.bfloat16)
-    low = (backward - high.astype(np.float32)).astype(ml_dtypes.bfloat16)
-    stacked = np.concatenate([high, low], axis=0)
-    return (np.ascontiguousarray(forward.astype(ml_dtypes.bfloat16).T), stacked)
+    waves = np.stack([np.cos(lag_radians) * weight, -np.sin(lag_radians) * weight]).astype(np.float32)
+    waves[:, LAGS // 2 + 1:] = 0.0
+    high = waves.astype(ml_dtypes.bfloat16)
+    low = (waves - high.astype(np.float32)).astype(ml_dtypes.bfloat16)
+    return (np.ascontiguousarray(forward.astype(ml_dtypes.bfloat16).T), np.concatenate([high, low], axis=1))
 
 
 def whiten_tile(spec, lanes, put):
@@ -73,7 +74,7 @@
 
 
 def whiten_kernel(right_ref, odd_ref, table_ref, x0, b0, a1, b1, a2, b2, o5, out_ref,
-                  band, spec_a, spec_b, bins_ref):
+                  band, spec_a, spec_b, bins_ref, packed, sems):
     segs = x0.shape[0]
     depth = 2 * segs
     pitch = depth + 1
@@ -109,12 +110,21 @@
 
     in_turns(segs, transform, whiten, spec_a, spec_b)
 
-    @pl.loop(0, BINS // 4)
+    def copy(group):
+        some = pl.ds(group * GROUP, GROUP)
+        return pltpu.make_async_copy(packed.at[:, some], out_ref.at[:, some], sems.at[group])
+
+    @pl.loop(0, BINS // GROUP)
     def _(group):
-        for step in range(4):
-            f = group * 4 + step
+        for step in range(GROUP):
+            f = group * GROUP + step
             for h in range(2):
-                out_ref[h, f] = bins_ref[h, pl.ds(f * pitch, depth), :].astype(jnp.bfloat16)
+                packed[h, f] = bins_ref[h, pl.ds(f * pitch, depth), :].astype(jnp.bfloat16)
+        copy(group).start()
+
+    @pl.loop(0, BINS // GROUP)
+    def _(group):
+        copy(group).wait()
 
 
 def whole(shape):
@@ -130,14 +140,16 @@
         grid=(1,),
         out_shape=jax.ShapeDtypeStruct(shape, jnp.bfloat16),
         in_specs=[smem, smem, whole(table.shape), share, share] + [whole(p.shape) for p in pieces],
-        out_specs=whole(shape),
+        out_specs=pl.BlockSpec(memory_space=pl.ANY),
         scratch_shapes=[
             pltpu.VMEM((segs, BAND, BINS), jnp.bfloat16),
             pltpu.VMEM((512, 256), jnp.float32),
             pltpu.VMEM((512, 256), jnp.float32),
             pltpu.VMEM((2, BINS * (2 * segs + 1), 128), jnp.float32),
+            pltpu.VMEM(shape, jnp.bfloat16),
+            pltpu.SemaphoreType.DMA((BINS // GROUP,)),
         ],
-        compiler_params=pltpu.CompilerParams(vmem_limit_bytes=(52 if segs > 16 else 32) * MIB),
+        compiler_params=pltpu.CompilerParams(vmem_limit_bytes=52 * MIB),
         cost_estimate=pl.CostEstimate(flops=240_000_000 * segs, bytes_accessed=8_000_000, transcendentals=0),
         name="whiten",
     )(right, odd, table, *whole_pieces, *pieces)
@@ -145,7 +157,7 @@
 
 def left_kernel(odd_ref, table_ref, x0, b0, *refs):
     pieces = refs[:len(CHUNKS)]
-    out_ref, records, spec_a, spec_b, bins_ref = refs[len(CHUNKS):]
+    out_ref, records, spec_a, spec_b, bins_ref, packed, sems = refs[len(CHUNKS):]
     odd = odd_ref[0] == 1
     segs = x0.shape[0]
     spread = LEFT + 1
@@ -195,11 +207,20 @@
 
     in_turns(LEFT // 4, transform, whiten, spec_a, spec_b)
 
-    @pl.loop(0, BINS // 4)
+    def copy(group):
+        some = pl.ds(group * GROUP, GROUP)
+        return pltpu.make_async_copy(packed.at[some], out_ref.at[some], sems.at[group])
+
+    @pl.loop(0, BINS // GROUP)
     def _(group):
-        for step in range(4):
-            f = group * 4 + step
-            out_ref[f] = bins_ref[pl.ds(f * pitch, 2 * LEFT), :].astype(jnp.bfloat16)
+        for step in range(GROUP):
+            f = group * GROUP + step
+            packed[f] = bins_ref[pl.ds(f * pitch, 2 * LEFT), :].astype(jnp.bfloat16)
+        copy(group).start()
+
+    @pl.loop(0, BINS // GROUP)
+    def _(group):
+        copy(group).wait()
 
 
 def left_bins(odd, table, x0, b0, pieces):
@@ -209,49 +230,57 @@
         left_kernel,
         out_shape=jax.ShapeDtypeStruct((BINS, 2 * LEFT, 128), jnp.bfloat16),
         in_specs=[smem] + [vmem] * (3 + len(pieces)),
-        out_specs=vmem,
+        out_specs=pl.BlockSpec(memory_space=pl.ANY),
         scratch_shapes=[
             pltpu.VMEM((2, x0.shape[0] * (LEFT + 1), 128), jnp.float32),
             pltpu.VMEM((512, 256), jnp.float32),
             pltpu.VMEM((512, 256), jnp.float32),
             pltpu.VMEM((BINS * (2 * LEFT + 1), 128), jnp.float32),
+            pltpu.VMEM((BINS, 2 * LEFT, 128), jnp.bfloat16),
+            pltpu.SemaphoreType.DMA((BINS // GROUP,)),
         ],
-        compiler_params=pltpu.CompilerParams(vmem_limit_bytes=48 * MIB),
+        compiler_params=pltpu.CompilerParams(vmem_limit_bytes=52 * MIB),
         cost_estimate=pl.CostEstimate(flops=6_000_000_000, bytes_accessed=14_000_000, transcendentals=0),
         name="left",
     )(odd, table, x0, b0, *pieces)
 
 
 def lag_sums(table_ref, cross_ref, lags):
-    @pl.loop(0, BLK // 2)
-    def _(pair):
-        a = 2 * pair
-        cross = jnp.concatenate(
-            [cross_ref[pl.ds((a + k) * PITCH, 512), :].astype(jnp.bfloat16) for k in range(2)], axis=1
-        )
-        both = jnp.dot(table_ref[...], cross, preferred_element_type=jnp.float32)
-        both = both[:ROWS] + both[ROWS:]
-        lags[a] = both[:, :128]
-        lags[a + 1] = both[:, 128:]
+    @pl.loop(0, BLK // 4)
+    def _(four):
+        for a in (4 * four, 4 * four + 2):
+            for part in range(2):
+                cross = jnp.concatenate(
+                    [
+                        cross_ref[pl.ds((a + k) * PITCH + part * BINS, BINS), :].astype(jnp.bfloat16)
+                        for k in range(2)
+                    ],
+                    axis=1,
+                )
+                both = jnp.dot(table_ref[part], cross, preferred_element_type=jnp.float32)
+                both = both[:HALF] + both[HALF:]
+                lags[a, part * HALF:(part + 1) * HALF, :] = both[:, :128]
+                lags[a + 1, part * HALF:(part + 1) * HALF, :] = both[:, 128:]
 
 
 def by_slot(lags, put):
     block = lax.broadcasted_iota(jnp.int32, (BLK, 128), 1) // BLK
     odd_block = {d: (block // d) % 2 == 1 for d in (4, 2, 1)}
 
-    @pl.loop(0, ROWS // BLK)
+    @pl.loop(0, ROWS // (2 * BLK))
     def _(tile):
-        rows = pl.ds(pl.multiple_of(tile * BLK, BLK), BLK)
-        for ha in range(2):
-            arrays = [lags[8 * ha + k, rows, :] for k in range(8)]
-            for d in (4, 2, 1):
+        for sub in range(2):
+            rows = pl.ds(pl.multiple_of((2 * tile + sub) * BLK, BLK), BLK)
+            for ha in range(2):
+                arrays = [lags[8 * ha + k, rows, :] for k in range(8)]
+                for d in (4, 2, 1):
+                    for k in range(8):
+                        if k & d == 0:
+                            one, two = arrays[k], arrays[k + d]
+                            arrays[k] = jnp.where(odd_block[d], pltpu.roll(two, BLK * d, 1), one)
+                            arrays[k + d] = jnp.where(odd_block[d], two, pltpu.roll(one, 128 - BLK * d, 1))
                 for k in range(8):
-                    if k & d == 0:
-                        one, two = arrays[k], arrays[k + d]
-                        arrays[k] = jnp.where(odd_block[d], pltpu.roll(two, BLK * d, 1), one)
-                        arrays[k + d] = jnp.where(odd_block[d], two, pltpu.roll(one, 128 - BLK * d, 1))
-            for k in range(8):
-                put(k, rows, slice(ha * 128, (ha + 1) * 128), arrays[k])
+                    put(k, rows, slice(ha * 128, (ha + 1) * 128), arrays[k])
 
 
 def gram_kernel(tile, live_ref, first_ref, table_ref, left_ref, *refs):
@@ -263,10 +292,10 @@
     first = first_ref[...]
     chosen = [jnp.broadcast_to(first == i, (BLK, 128)) for i in range(3)]
 
-    @pl.loop(0, bins // 4)
+    @pl.loop(0, bins // GROUP)
     def _(group):
-        for step in range(4):
-            local_bin = group * 4 + step
+        for step in range(GROUP):
+            local_bin = group * GROUP + step
             f = block * bins + local_bin
             right = jnp.concatenate(
                 [p[0, local_bin, part * n:(part + 1) * n, :] for part in range(2) for p, n in zip(parts, CHUNKS)],
@@ -316,10 +345,49 @@
             pltpu.VMEM((BLK * PITCH, 128), jnp.float32),
             pltpu.VMEM((BLK, ROWS, 128), jnp.float32),
         ],
-        compiler_params=pltpu.CompilerParams(vmem_limit_bytes=32 * MIB),
+        compiler_params=pltpu.CompilerParams(vmem_limit_bytes=48 * MIB),
         cost_estimate=pl.CostEstimate(flops=16_000_000_000, bytes_accessed=20_000_000, transcendentals=0),
         name="gram",
     )(live, first, table, left, *parts)
+
+
+def final_kernel(own, below, above, two_below, two_above, out):
+    row = lax.broadcasted_iota(jnp.int32, (8, 256), 0)
+
+    def reversed_rows(x):
+        x = pltpu.roll(x, 4, 0)
+        x = jnp.where((row & 2) == 2, pltpu.roll(x, 2, 0), pltpu.roll(x, 6, 0))
+        return jnp.where((row & 1) == 1, pltpu.roll(x, 1, 0), pltpu.roll(x, 7, 0))
+
+    middle = LAGS // 2
+    for pair, (near, far) in enumerate(((above, two_below), (below, two_above))):
+        @pl.loop(0, 2)
+        def _(k, pair=pair, near=near, far=far):
+            q = 2 * pair + k
+            for start in range(0, HALF, BLK):
+                even, odd = (
+                    own[q, rows, :] + near[2 + k, rows, :].astype(jnp.float32) + far[k, rows, :].astype(jnp.float32)
+                    for rows in (slice(start, start + BLK), slice(HALF + start, HALF + start + BLK))
+                )
+                later, earlier = even + odd, even - odd
+                for u in range(start, start + BLK, 8):
+                    n = min(8, middle + 1 - u)
+                    if n > 0:
+                        out[q, middle + u:middle + u + n, :] = later[u - start:u - start + n]
+                        turned = reversed_rows(earlier[u - start:u - start + 8])
+                        out[q, middle - u - n + 1:middle - u + 1, :] = turned[8 - n:]
+
+
+def final(own, below, above, two_below, two_above):
+    vmem = pl.BlockSpec(memory_space=pltpu.VMEM)
+    return pl.pallas_call(
+        final_kernel,
+        out_shape=jax.ShapeDtypeStruct((4, LAGS, 256), jnp.float32),
+        in_specs=[vmem] * 5,
+        out_specs=vmem,
+        cost_estimate=pl.CostEstimate(flops=10_000_000, bytes_accessed=7_000_000, transcendentals=0),
+        name="final",
+    )(own, below, above, two_below, two_above)
 
 
 def moved(block, axis, to):
@@ -356,28 +424,23 @@
     first_lanes = jnp.repeat(first, BLK)[None, :]
 
     barrier = lax.optimization_barrier
-    starts = np.cumsum((0,) + CHUNKS)
-    x = [records[starts[c]:starts[c + 1]] for c in range(len(CHUNKS))]
+    step = CHUNKS[0]
+    x_0, x_1 = records[:step], records[step:]
 
     def whitened(c, *pieces):
-        return whiten_bins(right, odd, table, [records, b0], pieces, CHUNKS[c], int(starts[c]))
-
-    a1_0, b0 = one_chip(x[0]), swap(records)
-    x[1], a1_0 = barrier((x[1], a1_0))
-    a2_0, b1_0, a1_1 = one_chip(a1_0), swap(a1_0), one_chip(x[1])
-    x[2], a1_1 = barrier((x[2], a1_1))
-    b2_0, o5_0, a2_1, b1_1, a1_2 = swap(a2_0), first_half(a2_0, 1), one_chip(a1_1), swap(a1_1), one_chip(x[2])
+        return whiten_bins(right, odd, table, [records, b0], pieces, step, c * step)
+
+    a1_0, a1_1, b0 = one_chip(x_0), one_chip(x_1), swap(records)
+    a2_0, b1_0 = one_chip(a1_0), swap(a1_0)
+    a2_1, b1_1 = one_chip(a1_1), swap(a1_1)
+    b2_0, o5_0 = swap(a2_0), first_half(a2_0, 1)
     part_0 = whitened(0, a1_0, b1_0, a2_0, b2_0, o5_0)
-    a2_1, a1_2, part_0 = barrier((a2_1, a1_2, part_0))
+    a2_1, b1_1, part_0 = barrier((a2_1, b1_1, part_0))
     b2_1, o5_1 = swap(a2_1), first_half(a2_1, 1)
-    a2_2, b1_2, o5_2 = one_chip(a1_2), swap(a1_2), first_half(a1_2, 3)
-    left = left_bins(odd, table, records, b0, [b1_0, b1_1, b1_2])
+    left = left_bins(odd, table, records, b0, [b1_0, b1_1])
     part_1 = whitened(1, a1_1, b1_1, a2_1, b2_1, o5_1)
-    a2_2, o5_2, left, part_1 = barrier((a2_2, o5_2, left, part_1))
-    b2_2 = swap(a2_2)
-    part_2 = whitened(2, a1_2, b1_2, a2_2, b2_2, o5_2)
-
-    parts = [part_0, part_1, part_2]
+
+    parts = [part_0, part_1]
     plus, minus = gram(0, live, first_lanes, backward, left, parts, (4, 4), jnp.bfloat16)
     keep, other, own = gram(1, live, first_lanes, backward, left, parts, (2, 2, 4), jnp.float32)
 
@@ -387,10 +450,7 @@
     down = (other + from_above[:2].astype(jnp.float32)).astype(jnp.bfloat16)
     two_below = moved(up, "tm", lambda i: i + 1)
     two_above = moved(down, "tm", lambda i: i - 1)
-    f32 = jnp.float32
-    low = own[:2] + from_above[2:].astype(f32) + two_below.astype(f32)
-    high = own[2:] + from_below[2:].astype(f32) + two_above.astype(f32)
-    return jnp.concatenate([low, high], axis=0)[:, :LAGS]
+    return final(own, from_below, from_above, two_below, two_above)
 
 
 def solution(mesh):

time: 169 us -> 149 us (0.88)
  Pallas kernels: 78.2 us -> 70.4 us
  waiting for transfers between devices: 36.7 us -> 29 us
  local copies, waits for them, and re-layouts: 15 us -> 9.89 us
    pallas_call x2, Pallas kernels: 44.3 us -> 30.9 us  [gram(): pl.pallas_call(functools.partial(gram_kernel, tile), grid=(BINS // step,)...]
    ppermute x20 -> x15, waiting for transfers between devices: 36.7 us -> 29 us  [moved(): return lax.ppermute(block, axis, [(i, to(i) % size) for i in range(size)])]
    pallas_call x0 -> x1, Pallas kernels: none -> 3.88 us  [final(): pl.pallas_call(final_kernel, out_shape=jax.ShapeDtypeStruct((4, LAGS, 256...]
    unnamed x29 -> x21, local copies, waits for them, and re-layouts: 8.48 us -> 4.63 us
    slice x3 -> x1, local copies, waits for them, and re-layouts: 4.83 us -> 1.27 us  [local(): x_0, x_1 = (records[:step], records[step:])]
    pallas_call x0 -> x1, local copies, waits for them, and re-layouts: none -> 3.24 us  [final(): pl.pallas_call(final_kernel, out_shape=jax.ShapeDtypeStruct((4, LAGS, 256...]
    pallas_call x3 -> x2, Pallas kernels: 23.9 us -> 25.1 us  [whiten_bins(): pl.pallas_call(whiten_kernel, grid=(1,), out_shape=jax.ShapeDtypeStruct(s...]
    ppermute x20 -> x15, starting transfers between devices: 34.4 us -> 35.6 us  [moved(): return lax.ppermute(block, axis, [(i, to(i) % size) for i in range(size)])]
  transfers between devices with their start and end apart: 20 -> 15, of which waited for: 6 -> 4; matrix products, arithmetic and copies ran while one was open for 3% -> 2% of each run, Pallas kernels for 31% -> 27%
where the time goes in v3:
time: 149 us; the launch traced here: 147 us
  Pallas kernels  70.4 us (47%)
  starting transfers between devices  35.6 us (24%)
  waiting for transfers between devices  29 us (19%)
  local copies, waits for them, and re-layouts  9.89 us (7%)
    ppermute x15, starting transfers between devices, moved(): return lax.ppermute(block, axis, [(i, to(i) % size) for i in range(size)])  35.6 us
    pallas_call x2, Pallas kernels, gram(): pl.pallas_call(functools.partial(gram_kernel, tile), grid=(BINS // step,)...  30.9 us
    ppermute x15, waiting for transfers between devices, moved(): return lax.ppermute(block, axis, [(i, to(i) % size) for i in range(size)])  29 us
    pallas_call x2, Pallas kernels, whiten_bins(): pl.pallas_call(whiten_kernel, grid=(1,), out_shape=jax.ShapeDtypeStruct(s...  25.1 us
    pallas_call x1, Pallas kernels, left_bins(): pl.pallas_call(left_kernel, out_shape=jax.ShapeDtypeStruct((BINS, 2 * LEF...  10.5 us
    unnamed x21, local copies, waits for them, and re-layouts  4.63 us
    pallas_call x1, Pallas kernels, final(): pl.pallas_call(final_kernel, out_shape=jax.ShapeDtypeStruct((4, LAGS, 256...  3.88 us
    pallas_call x1, local copies, waits for them, and re-layouts, final(): pl.pallas_call(final_kernel, out_shape=jax.ShapeDtypeStruct((4, LAGS, 256...  3.24 us
  transfers between devices with their start and end apart: 15, of which 4 were waited for; matrix products, arithmetic and copies ran while one was open for 2% of the time, Pallas kernels for 27%

profile of v3, /device:TPU:0, one launch (start us, length us, event | category | flops | bytes accessed | tf_op | source)
XLA Modules:
  0.0 146.9 jit_solution(1213853440597903182)
XLA Ops:
  0.0 1.3 fusion.6
  1.3 6.4 %collective-permute-start.1 = (bf16[32,32,256]{2,1,0:T(8,128)(2,1)S(1)}, bf16[32,32,256]{2,1,0:T(8,128)(2,1)S(1)}, u32[]{:S(2)}, u32[]{:S(2)}) collective-permute-start(bf16[32,32,256]{2,1,0:T(8,128)(2,1)S(1)} %get-tuple-element.26), channel_id=1, source_target_pairs={{0,62},{1,63},{2,0},{3,1},{4,2},{5,3},{6,4},{7,5},{8,6},{9,7},{10,... | collective-permute-start | bytes 1572872 | tf_op jit(solution)/shard_map/ppermute | solution.py:395
  7.7 11.2 %collective-permute-done.1.a1 = bf16[32,32,256]{2,1,0:T(8,128)(2,1)S(1)} collective-permute-done((bf16[32,32,256]{2,1,0:T(8,128)(2,1)S(1)}, bf16[32,32,256]{2,1,0:T(8,128)(2,1)S(1)}, u32[]{:S(2)}, u32[]{:S(2)}) %collective-permute-start.1) | collective-permute-done | bytes 524320 | tf_op jit(solution)/shard_map/ppermute | solution.py:395
  18.8 5.8 %collective-permute-start.6 = (bf16[32,32,256]{2,1,0:T(8,128)(2,1)S(1)}, bf16[32,32,256]{2,1,0:T(8,128)(2,1)S(1)}, u32[]{:S(2)}, u32[]{:S(2)}) collective-permute-start(bf16[32,32,256]{2,1,0:T(8,128)(2,1)S(1)} %collective-permute-done.1.a1), channel_id=1, source_target_pairs={{0,62},{1,63},{2,0},{3,1},{4,2},{5,3},{6,4},{7,5},{8,6},{9,7},{10,... | collective-permute-start | bytes 1572872 | tf_op jit(solution)/shard_map/ppermute | solution.py:395
  24.6 0.0 collective-permute-start
  24.7 0.0 collective-permute-start.3
  24.7 0.8 copy.10
  25.4 0.7 compare_select_fusion
  26.1 0.6 gather_fusion
  26.7 0.6 collective-permute-start.2
  27.3 9.8 %collective-permute-done.6.a2 = bf16[32,32,256]{2,1,0:T(8,128)(2,1)S(1)} collective-permute-done((bf16[32,32,256]{2,1,0:T(8,128)(2,1)S(1)}, bf16[32,32,256]{2,1,0:T(8,128)(2,1)S(1)}, u32[]{:S(2)}, u32[]{:S(2)}) %collective-permute-start.6) | collective-permute-done | bytes 524320 | tf_op jit(solution)/shard_map/ppermute | solution.py:395
  37.0 0.0 copy-start.7
  37.0 0.0 collective-permute-start.7
  37.1 6.0 %collective-permute-start.8 = (bf16[32,16,256]{2,1,0:T(8,128)(2,1)S(1)}, bf16[32,16,256]{2,1,0:T(8,128)(2,1)S(1)}, u32[]{:S(2)}, u32[]{:S(2)}) collective-permute-start(bf16[32,16,256]{2,1,0:T(8,128)(2,1)S(1)} %slice.36), channel_id=1, source_target_pairs={{0,63},{1,0},{2,1},{3,2},{4,3},{5,4},{6,5},{7,6},{8,7},{9,8},{10,9... | collective-permute-start | bytes 786440 | tf_op jit(solution)/shard_map/ppermute | solution.py:395
  43.0 0.2 fusion
  43.9 0.1 broadcast_in_dim.10
  44.0 0.1 broadcast_in_dim_reshape.3.first_ref
  44.0 2.1 %collective-permute-done.3.a1 = bf16[32,32,256]{2,1,0:T(8,128)(2,1)S(1)} collective-permute-done((bf16[32,32,256]{2,1,0:T(8,128)(2,1)S(1)}, bf16[32,32,256]{2,1,0:T(8,128)(2,1)S(1)}, u32[]{:S(2)}, u32[]{:S(2)}) %collective-permute-start.3) | collective-permute-done | bytes 524320 | tf_op jit(solution)/shard_map/ppermute | solution.py:395
  46.2 0.0 collective-permute-start.5
  46.2 0.0 collective-permute-done.2.b1.refs_0_
  46.2 5.8 %collective-permute-start.4 = (bf16[32,32,256]{2,1,0:T(8,128)(2,1)S(1)}, bf16[32,32,256]{2,1,0:T(8,128)(2,1)S(1)}, u32[]{:S(2)}, u32[]{:S(2)}) collective-permute-start(bf16[32,32,256]{2,1,0:T(8,128)(2,1)S(1)} %collective-permute-done.3.a1), channel_id=1, source_target_pairs={{0,62},{1,63},{2,0},{3,1},{4,2},{5,3},{6,4},{7,5},{8,6},{9,7},{10,... | collective-permute-start | bytes 1572872 | tf_op jit(solution)/shard_map/ppermute | solution.py:395
  52.0 0.0 collective-permute-done.b0
  52.0 0.0 collective-permute-done.8.o5
  52.0 0.0 collective-permute-done.7.b2
  52.0 0.0 copy-done.7
  52.0 0.0 copy-start.2
  52.0 0.9 copy-done.2
  53.0 12.6 %whiten.2.refs_0_ = bf16[2,256,64,128]{3,2,1,0:T(8,128)(2,1)} custom-call(s32[16]{0:T(128)S(1)} %get-tuple-element.21.right_ref, s32[1]{0:T(128)} %bitcast.1.odd_ref, bf16[512,256]{1,0:T(8,128)(2,1)S(1)} %copy-done.2, bf16[64,32,256]{2,1,0:T(8,128)(2,1)} %x0.5, bf16[64,32,256]{2,1,0:T(8,128)(2,1)} %collective-permute-done.b0, ...), custom_call_target="tpu_custom_call" | custom-call | flops 7680000000 | bytes 8000000 | tf_op jit(solution)/shard_map/whiten/pallas_call | solution.py:138
  65.5 0.0 collective-permute-done.5.refs_1_.b1
  65.6 0.0 collective-permute-done.4.a2
  65.6 0.0 copy-start.8
  65.6 0.3 collective-permute-start.9
  65.9 4.0 %collective-permute-start.10 = (bf16[32,16,256]{2,1,0:T(8,128)(2,1)S(1)}, bf16[32,16,256]{2,1,0:T(8,128)(2,1)S(1)}, u32[]{:S(2)}, u32[]{:S(2)}) collective-permute-start(bf16[32,16,256]{2,1,0:T(8,128)(2,1)S(1)} %slice.29), channel_id=1, source_target_pairs={{0,63},{1,0},{2,1},{3,2},{4,3},{5,4},{6,5},{7,6},{8,7},{9,8},{10,9... | collective-permute-start | bytes 786440 | tf_op jit(solution)/shard_map/ppermute | solution.py:395
  69.9 10.5 %left.1.left_ref = bf16[256,128,128]{2,1,0:T(8,128)(2,1)} custom-call(s32[1]{0:T(128)} %bitcast.1.odd_ref, bf16[512,256]{1,0:T(8,128)(2,1)S(1)} %copy-done.2, bf16[64,32,256]{2,1,0:T(8,128)(2,1)} %x0.5, bf16[64,32,256]{2,1,0:T(8,128)(2,1)} %collective-permute-done.b0, bf16[32,32,256]{2,1,0:T(8,128)(2,1)S(1)} %collective-permute-done.2.b1.refs_0_, ...), custom_call_target="tpu_custom_call" | custom-call | flops 6000000000 | bytes 14000000 | tf_op jit(solution)/shard_map/left/pallas_call | solution.py:229
  80.4 0.0 copy-done.8
  80.4 0.0 copy-start.1
  80.4 0.0 collective-permute-done.10.o5
  80.5 0.0 collective-permute-done.9.b2
  80.5 0.0 copy-start.9
  80.5 0.8 copy-done.9
  81.3 12.6 %whiten.3.refs_1_ = bf16[2,256,64,128]{3,2,1,0:T(8,128)(2,1)} custom-call(s32[16]{0:T(128)S(1)} %get-tuple-element.21.right_ref, s32[1]{0:T(128)} %bitcast.1.odd_ref, bf16[512,256]{1,0:T(8,128)(2,1)S(1)} %copy-done.2, bf16[64,32,256]{2,1,0:T(8,128)(2,1)} %x0.5, bf16[64,32,256]{2,1,0:T(8,128)(2,1)} %collective-permute-done.b0, ...), custom_call_target="tpu_custom_call" | custom-call | flops 7680000000 | bytes 8000000 | tf_op jit(solution)/shard_map/whiten/pallas_call | solution.py:138
  93.8 0.0 copy-done.1
  93.8 14.5 %gram.3 = (bf16[4,416,256]{2,1,0:T(8,128)(2,1)S(1)}, bf16[4,416,256]{2,1,0:T(8,128)(2,1)S(1)}) custom-call(s32[16]{0:T(128)S(1)} %compare_convert_fusion.live_ref, s32[1,256]{1,0:T(1,128)S(1)} %broadcast_in_dim_reshape.3.first_ref, bf16[2,416,256]{2,1,0:T(8,128)(2,1)S(1)} %copy-done.1, bf16[256,128,128]{2,1,0:T(8,128)(2,1)} %left.1.left_ref, ...), custom_call_target="tpu_custom_call" | custom-call | flops 16000000000 | bytes 20000000 | tf_op jit(solution)/shard_map/gram/pallas_call | solution.py:332
  108.3 1.7 %collective-permute-start.11 = (bf16[4,416,256]{2,1,0:T(8,128)(2,1)S(1)}, bf16[4,416,256]{2,1,0:T(8,128)(2,1)S(1)}, u32[]{:S(2)}, u32[]{:S(2)}) collective-permute-start(bf16[4,416,256]{2,1,0:T(8,128)(2,1)S(1)} %get-tuple-element.17), channel_id=1, source_target_pairs={{0,64},{64,128},{128,192},{192,0},{1,65},{65,129},{129,193},{193,1... | collective-permute-start | bytes 2555912 | tf_op jit(solution)/shard_map/ppermute | solution.py:395
  110.0 1.7 %collective-permute-start.12 = (bf16[4,416,256]{2,1,0:T(8,128)(2,1)S(1)}, bf16[4,416,256]{2,1,0:T(8,128)(2,1)S(1)}, u32[]{:S(2)}, u32[]{:S(2)}) collective-permute-start(bf16[4,416,256]{2,1,0:T(8,128)(2,1)S(1)} %get-tuple-element.18), channel_id=1, source_target_pairs={{0,192},{64,0},{128,64},{192,128},{1,193},{65,1},{129,65},{193,129... | collective-permute-start | bytes 2555912 | tf_op jit(solution)/shard_map/ppermute | solution.py:395
  111.7 16.4 %gram.2 = (f32[2,416,256]{2,1,0:T(8,128)S(1)}, f32[2,416,256]{2,1,0:T(8,128)S(1)}, f32[4,416,256]{2,1,0:T(8,128)S(1)}) custom-call(s32[16]{0:T(128)S(1)} %compare_convert_fusion.live_ref, s32[1,256]{1,0:T(1,128)S(1)} %broadcast_in_dim_reshape.3.first_ref, bf16[2,416,256]{2,1,0:T(8,128)(2,1)S(1)} %copy-done.1, bf16[256,128,128]{2,1,0:T(8,128)(2,1)} %left.1.left_ref, ...), custom_call_target="tpu_custom_call" | custom-call | flops 16000000000 | bytes 20000000 | tf_op jit(solution)/shard_map/gram/pallas_call | solution.py:332
  128.1 0.0 copy-start
  128.1 1.2 copy-done
  129.3 0.0 collective-permute-done.11.below
  129.3 0.0 copy-start.3
  129.3 0.1 add_convert_fusion.1
  129.5 0.4 collective-permute-start.13
  129.9 0.0 collective-permute-done.12.above
  129.9 0.0 copy-start.4
  129.9 0.1 add_convert_fusion
  130.0 3.0 %collective-permute-start.14 = (bf16[2,416,256]{2,1,0:T(8,128)(2,1)S(1)}, bf16[2,416,256]{2,1,0:T(8,128)(2,1)S(1)}, u32[]{:S(2)}, u32[]{:S(2)}) collective-permute-start(bf16[2,416,256]{2,1,0:T(8,128)(2,1)S(1)} %add_convert_fusion), channel_id=1, source_target_pairs={{0,192},{64,0},{128,64},{192,128},{1,193},{65,1},{129,65},{193,129... | collective-permute-start | bytes 1277960 | tf_op jit(solution)/shard_map/ppermute | solution.py:395
  133.0 5.9 %collective-permute-done.13.two_below = bf16[2,416,256]{2,1,0:T(8,128)(2,1)S(1)} collective-permute-done((bf16[2,416,256]{2,1,0:T(8,128)(2,1)S(1)}, bf16[2,416,256]{2,1,0:T(8,128)(2,1)S(1)}, u32[]{:S(2)}, u32[]{:S(2)}) %collective-permute-start.13) | collective-permute-done | bytes 426016 | tf_op jit(solution)/shard_map/ppermute | solution.py:395
  138.9 0.0 collective-permute-done.14.two_above
  138.9 0.0 copy-done.3
  138.9 0.0 copy-done.4
  138.9 0.7 copy-done.5
  139.7 0.1 copy-done.6
  139.8 3.9 %final.1 = f32[4,401,256]{2,1,0:T(8,128)} custom-call(f32[4,416,256]{2,1,0:T(8,128)} %copy-done, bf16[4,416,256]{2,1,0:T(8,128)(2,1)} %copy-done.3, bf16[4,416,256]{2,1,0:T(8,128)(2,1)} %copy-done.4, bf16[2,416,256]{2,1,0:T(8,128)(2,1)} %copy-done.5, bf16[2,416,256]{2,1,0:T(8,128)(2,1)} %copy-done.6), custom_call_target="tpu_custom_call" | custom-call | flops 10000000 | bytes 7000000 | tf_op jit(solution)/shard_map/final/pallas_call | solution.py:383
  143.7 3.2 %copy.11 = f32[4,401,256]{2,0,1:T(4,128)} copy(f32[4,401,256]{2,1,0:T(8,128)} %final.1) | data formatting | bytes 3284992 | tf_op jit(solution)/shard_map/final/pallas_call | solution.py:383
  (7 shorter events, 0.1 us)
Async XLA Ops:
  1.3 17.6 %collective-permute-start.1 = (bf16[32,32,256]{2,1,0:T(8,128)(2,1)S(1)}, bf16[32,32,256]{2,1,0:T(8,128)(2,1)S(1)}, u32[]{:S(2)}, u32[]{:S(2)}) collective-permute-start(bf16[32,32,256]{2,1,0:T(8,128)(2,1)S(1)} %get-tuple-element.26), channel_id=1, source_target_pairs={{0,62},{1,63},{2,0},{3,1},{4,2},{5,3},{6,4},{7,5},{8,6},{9,7},{10,... | collective-permute-start | bytes 1572872 | tf_op jit(solution)/shard_map/ppermute | solution.py:395
  18.8 18.2 %collective-permute-start.6 = (bf16[32,32,256]{2,1,0:T(8,128)(2,1)S(1)}, bf16[32,32,256]{2,1,0:T(8,128)(2,1)S(1)}, u32[]{:S(2)}, u32[]{:S(2)}) collective-permute-start(bf16[32,32,256]{2,1,0:T(8,128)(2,1)S(1)} %collective-permute-done.1.a1), channel_id=1, source_target_pairs={{0,62},{1,63},{2,0},{3,1},{4,2},{5,3},{6,4},{7,5},{8,6},{9,7},{10,... | collective-permute-start | bytes 1572872 | tf_op jit(solution)/shard_map/ppermute | solution.py:395
  24.6 27.4 %collective-permute-start = (bf16[64,32,256]{2,1,0:T(8,128)(2,1)}, bf16[64,32,256]{2,1,0:T(8,128)(2,1)}, u32[]{:S(2)}, u32[]{:S(2)}) collective-permute-start(bf16[64,32,256]{2,1,0:T(8,128)(2,1)} %x0.5), channel_id=1, source_target_pairs={{0,1},{1,0},{2,3},{3,2},{4,5},{5,4},{6,7},{7,6},{8,9},{9,8},{10,11... | collective-permute-start | bytes 3145736 | tf_op jit(solution)/shard_map/ppermute | solution.py:395
  24.7 21.5 %collective-permute-start.3 = (bf16[32,32,256]{2,1,0:T(8,128)(2,1)S(1)}, bf16[32,32,256]{2,1,0:T(8,128)(2,1)S(1)}, u32[]{:S(2)}, u32[]{:S(2)}) collective-permute-start(bf16[32,32,256]{2,1,0:T(8,128)(2,1)S(1)} %get-tuple-element.25), channel_id=1, source_target_pairs={{0,62},{1,63},{2,0},{3,1},{4,2},{5,3},{6,4},{7,5},{8,6},{9,7},{10,... | collective-permute-start | bytes 1572872 | tf_op jit(solution)/shard_map/ppermute | solution.py:395
  26.7 19.5 %collective-permute-start.2 = (bf16[32,32,256]{2,1,0:T(8,128)(2,1)S(1)}, bf16[32,32,256]{2,1,0:T(8,128)(2,1)S(1)}, u32[]{:S(2)}, u32[]{:S(2)}) collective-permute-start(bf16[32,32,256]{2,1,0:T(8,128)(2,1)S(1)} %collective-permute-done.1.a1), channel_id=1, source_target_pairs={{0,1},{1,0},{2,3},{3,2},{4,5},{5,4},{6,7},{7,6},{8,9},{9,8},{10,11... | collective-permute-start | bytes 1572872 | tf_op jit(solution)/shard_map/ppermute | solution.py:395
  37.0 15.0 %copy-start.7 = (bf16[32,32,256]{2,1,0:T(8,128)(2,1)}, bf16[32,32,256]{2,1,0:T(8,128)(2,1)S(1)}, u32[]{:S(2)}) copy-start(bf16[32,32,256]{2,1,0:T(8,128)(2,1)S(1)} %collective-permute-done.6.a2) | copy-start | bytes 1572868
  37.0 15.0 %collective-permute-start.7 = (bf16[32,32,256]{2,1,0:T(8,128)(2,1)S(1)}, bf16[32,32,256]{2,1,0:T(8,128)(2,1)}, u32[]{:S(2)}, u32[]{:S(2)}) collective-permute-start(bf16[32,32,256]{2,1,0:T(8,128)(2,1)S(1)} %collective-permute-done.6.a2), channel_id=1, source_target_pairs={{0,1},{1,0},{2,3},{3,2},{4,5},{5,4},{6,7},{7,6},{8,9},{9,8},{10,11... | collective-permute-start | bytes 1572872 | tf_op jit(solution)/shard_map/ppermute | solution.py:395
  37.1 15.0 %collective-permute-start.8 = (bf16[32,16,256]{2,1,0:T(8,128)(2,1)S(1)}, bf16[32,16,256]{2,1,0:T(8,128)(2,1)S(1)}, u32[]{:S(2)}, u32[]{:S(2)}) collective-permute-start(bf16[32,16,256]{2,1,0:T(8,128)(2,1)S(1)} %slice.36), channel_id=1, source_target_pairs={{0,63},{1,0},{2,1},{3,2},{4,3},{5,4},{6,5},{7,6},{8,7},{9,8},{10,9... | collective-permute-start | bytes 786440 | tf_op jit(solution)/shard_map/ppermute | solution.py:395
  46.2 19.4 %collective-permute-start.5 = (bf16[32,32,256]{2,1,0:T(8,128)(2,1)S(1)}, bf16[32,32,256]{2,1,0:T(8,128)(2,1)S(1)}, u32[]{:S(2)}, u32[]{:S(2)}) collective-permute-start(bf16[32,32,256]{2,1,0:T(8,128)(2,1)S(1)} %collective-permute-done.3.a1), channel_id=1, source_target_pairs={{0,1},{1,0},{2,3},{3,2},{4,5},{5,4},{6,7},{7,6},{8,9},{9,8},{10,11... | collective-permute-start | bytes 1572872 | tf_op jit(solution)/shard_map/ppermute | solution.py:395
  46.2 19.4 %collective-permute-start.4 = (bf16[32,32,256]{2,1,0:T(8,128)(2,1)S(1)}, bf16[32,32,256]{2,1,0:T(8,128)(2,1)S(1)}, u32[]{:S(2)}, u32[]{:S(2)}) collective-permute-start(bf16[32,32,256]{2,1,0:T(8,128)(2,1)S(1)} %collective-permute-done.3.a1), channel_id=1, source_target_pairs={{0,62},{1,63},{2,0},{3,1},{4,2},{5,3},{6,4},{7,5},{8,6},{9,7},{10,... | collective-permute-start | bytes 1572872 | tf_op jit(solution)/shard_map/ppermute | solution.py:395
  52.0 1.0 copy-start.2
  65.6 14.9 %copy-start.8 = (bf16[32,32,256]{2,1,0:T(8,128)(2,1)}, bf16[32,32,256]{2,1,0:T(8,128)(2,1)S(1)}, u32[]{:S(2)}) copy-start(bf16[32,32,256]{2,1,0:T(8,128)(2,1)S(1)} %collective-permute-done.4.a2) | copy-start | bytes 1572868
  65.6 14.9 %collective-permute-start.9 = (bf16[32,32,256]{2,1,0:T(8,128)(2,1)S(1)}, bf16[32,32,256]{2,1,0:T(8,128)(2,1)S(1)}, u32[]{:S(2)}, u32[]{:S(2)}) collective-permute-start(bf16[32,32,256]{2,1,0:T(8,128)(2,1)S(1)} %collective-permute-done.4.a2), channel_id=1, source_target_pairs={{0,1},{1,0},{2,3},{3,2},{4,5},{5,4},{6,7},{7,6},{8,9},{9,8},{10,11... | collective-permute-start | bytes 1572872 | tf_op jit(solution)/shard_map/ppermute | solution.py:395
  65.9 14.5 %collective-permute-start.10 = (bf16[32,16,256]{2,1,0:T(8,128)(2,1)S(1)}, bf16[32,16,256]{2,1,0:T(8,128)(2,1)S(1)}, u32[]{:S(2)}, u32[]{:S(2)}) collective-permute-start(bf16[32,16,256]{2,1,0:T(8,128)(2,1)S(1)} %slice.29), channel_id=1, source_target_pairs={{0,63},{1,0},{2,1},{3,2},{4,3},{5,4},{6,5},{7,6},{8,7},{9,8},{10,9... | collective-permute-start | bytes 786440 | tf_op jit(solution)/shard_map/ppermute | solution.py:395
  80.4 13.4 %copy-start.1 = (bf16[2,416,256]{2,1,0:T(8,128)(2,1)S(1)}, bf16[2,416,256]{2,1,0:T(8,128)(2,1)}, u32[]{:S(2)}) copy-start(bf16[2,416,256]{2,1,0:T(8,128)(2,1)} %constant.55.clone.table_ref) | copy-start | bytes 1277956
  80.5 0.8 copy-start.9
  108.3 21.0 %collective-permute-start.11 = (bf16[4,416,256]{2,1,0:T(8,128)(2,1)S(1)}, bf16[4,416,256]{2,1,0:T(8,128)(2,1)S(1)}, u32[]{:S(2)}, u32[]{:S(2)}) collective-permute-start(bf16[4,416,256]{2,1,0:T(8,128)(2,1)S(1)} %get-tuple-element.17), channel_id=1, source_target_pairs={{0,64},{64,128},{128,192},{192,0},{1,65},{65,129},{129,193},{193,1... | collective-permute-start | bytes 2555912 | tf_op jit(solution)/shard_map/ppermute | solution.py:395
  110.0 19.9 %collective-permute-start.12 = (bf16[4,416,256]{2,1,0:T(8,128)(2,1)S(1)}, bf16[4,416,256]{2,1,0:T(8,128)(2,1)S(1)}, u32[]{:S(2)}, u32[]{:S(2)}) collective-permute-start(bf16[4,416,256]{2,1,0:T(8,128)(2,1)S(1)} %get-tuple-element.18), channel_id=1, source_target_pairs={{0,192},{64,0},{128,64},{192,128},{1,193},{65,1},{129,65},{193,129... | collective-permute-start | bytes 2555912 | tf_op jit(solution)/shard_map/ppermute | solution.py:395
  128.1 1.2 copy-start
  129.3 9.6 %copy-start.3 = (bf16[4,416,256]{2,1,0:T(8,128)(2,1)}, bf16[4,416,256]{2,1,0:T(8,128)(2,1)S(1)}, u32[]{:S(2)}) copy-start(bf16[4,416,256]{2,1,0:T(8,128)(2,1)S(1)} %collective-permute-done.11.below) | copy-start | bytes 2555908
  129.5 9.4 %collective-permute-start.13 = (bf16[2,416,256]{2,1,0:T(8,128)(2,1)S(1)}, bf16[2,416,256]{2,1,0:T(8,128)(2,1)S(1)}, u32[]{:S(2)}, u32[]{:S(2)}) collective-permute-start(bf16[2,416,256]{2,1,0:T(8,128)(2,1)S(1)} %add_convert_fusion.1), channel_id=1, source_target_pairs={{0,64},{64,128},{128,192},{192,0},{1,65},{65,129},{129,193},{193,1... | collective-permute-start | bytes 1277960 | tf_op jit(solution)/shard_map/ppermute | solution.py:395
  129.9 9.0 %copy-start.4 = (bf16[4,416,256]{2,1,0:T(8,128)(2,1)}, bf16[4,416,256]{2,1,0:T(8,128)(2,1)S(1)}, u32[]{:S(2)}) copy-start(bf16[4,416,256]{2,1,0:T(8,128)(2,1)S(1)} %collective-permute-done.12.above) | copy-start | bytes 2555908
  130.0 8.9 %collective-permute-start.14 = (bf16[2,416,256]{2,1,0:T(8,128)(2,1)S(1)}, bf16[2,416,256]{2,1,0:T(8,128)(2,1)S(1)}, u32[]{:S(2)}, u32[]{:S(2)}) collective-permute-start(bf16[2,416,256]{2,1,0:T(8,128)(2,1)S(1)} %add_convert_fusion), channel_id=1, source_target_pairs={{0,192},{64,0},{128,64},{192,128},{1,193},{65,1},{129,65},{193,129... | collective-permute-start | bytes 1277960 | tf_op jit(solution)/shard_map/ppermute | solution.py:395
  138.9 0.8 copy-start.5
  138.9 0.9 copy-start.6

commit v4 on v3

--- a/solution.py
+++ b/solution.py
@@ -18,7 +18,7 @@
 BINS = 256
 LEFT = 64
 BAND = 176
-CHUNKS = (32, 32)
+CHUNKS = (16, 48)
 PITCH = 513
 GROUP = 16
 
@@ -73,17 +73,17 @@
         whiten(i + 1, spec_b)
 
 
-def whiten_kernel(right_ref, odd_ref, table_ref, x0, b0, a1, b1, a2, b2, o5, out_ref,
+def whiten_kernel(offset, right_ref, odd_ref, table_ref, x0, b0, a1, b1, a2, b2, o5, out_ref,
                   band, spec_a, spec_b, bins_ref, packed, sems):
-    segs = x0.shape[0]
+    segs = a1.shape[0]
     depth = 2 * segs
     pitch = depth + 1
     odd = odd_ref[0] == 1
 
     @pl.loop(0, segs)
     def _(s):
-        band[s, 0:32, :] = x0[s]
-        band[s, 32:64, :] = jnp.where(odd, b1[s], b0[s])
+        band[s, 0:32, :] = x0[offset + s]
+        band[s, 32:64, :] = jnp.where(odd, b1[s], b0[offset + s])
         band[s, 64:96, :] = a1[s]
         band[s, 96:128, :] = jnp.where(odd, b2[s], b1[s])
         band[s, 128:160, :] = a2[s]
@@ -131,15 +131,15 @@
     return pl.BlockSpec(shape, lambda *_: (0,) * len(shape))
 
 
-def whiten_bins(right, odd, table, whole_pieces, pieces, segs, offset):
+def whiten_bins(right, odd, table, whole_pieces, pieces, offset):
     smem = pl.BlockSpec(memory_space=pltpu.SMEM)
-    share = pl.BlockSpec((segs, 32, BINS), lambda _: (offset // segs, 0, 0))
+    vmem = pl.BlockSpec(memory_space=pltpu.VMEM)
+    segs = pieces[0].shape[0]
     shape = (2, BINS, 2 * segs, 128)
     return pl.pallas_call(
-        whiten_kernel,
-        grid=(1,),
+        functools.partial(whiten_kernel, offset),
         out_shape=jax.ShapeDtypeStruct(shape, jnp.bfloat16),
-        in_specs=[smem, smem, whole(table.shape), share, share] + [whole(p.shape) for p in pieces],
+        in_specs=[smem, smem] + [vmem] * (3 + len(pieces)),
         out_specs=pl.BlockSpec(memory_space=pl.ANY),
         scratch_shapes=[
             pltpu.VMEM((segs, BAND, BINS), jnp.bfloat16),
@@ -149,7 +149,7 @@
             pltpu.VMEM(shape, jnp.bfloat16),
             pltpu.SemaphoreType.DMA((BINS // GROUP,)),
         ],
-        compiler_params=pltpu.CompilerParams(vmem_limit_bytes=52 * MIB),
+        compiler_params=pltpu.CompilerParams(vmem_limit_bytes=54 * MIB),
         cost_estimate=pl.CostEstimate(flops=240_000_000 * segs, bytes_accessed=8_000_000, transcendentals=0),
         name="whiten",
     )(right, odd, table, *whole_pieces, *pieces)
@@ -246,9 +246,10 @@
 
 
 def lag_sums(table_ref, cross_ref, lags):
-    @pl.loop(0, BLK // 4)
-    def _(four):
-        for a in (4 * four, 4 * four + 2):
+    @pl.loop(0, BLK // 8)
+    def _(eight):
+        for pair in range(4):
+            a = 8 * eight + 2 * pair
             for part in range(2):
                 cross = jnp.concatenate(
                     [
@@ -292,10 +293,10 @@
     first = first_ref[...]
     chosen = [jnp.broadcast_to(first == i, (BLK, 128)) for i in range(3)]
 
-    @pl.loop(0, bins // GROUP)
-    def _(group):
-        for step in range(GROUP):
-            local_bin = group * GROUP + step
+    @pl.loop(0, bins // 32)
+    def _(group):
+        for step in range(32):
+            local_bin = group * 32 + step
             f = block * bins + local_bin
             right = jnp.concatenate(
                 [p[0, local_bin, part * n:(part + 1) * n, :] for part in range(2) for p, n in zip(parts, CHUNKS)],
@@ -351,43 +352,50 @@
     )(live, first, table, left, *parts)
 
 
-def final_kernel(own, below, above, two_below, two_above, out):
-    row = lax.broadcasted_iota(jnp.int32, (8, 256), 0)
-
-    def reversed_rows(x):
-        x = pltpu.roll(x, 4, 0)
-        x = jnp.where((row & 2) == 2, pltpu.roll(x, 2, 0), pltpu.roll(x, 6, 0))
-        return jnp.where((row & 1) == 1, pltpu.roll(x, 1, 0), pltpu.roll(x, 7, 0))
-
+def final_kernel(near, low, high, out, later, earlier):
     middle = LAGS // 2
-    for pair, (near, far) in enumerate(((above, two_below), (below, two_above))):
-        @pl.loop(0, 2)
-        def _(k, pair=pair, near=near, far=far):
-            q = 2 * pair + k
-            for start in range(0, HALF, BLK):
-                even, odd = (
-                    own[q, rows, :] + near[2 + k, rows, :].astype(jnp.float32) + far[k, rows, :].astype(jnp.float32)
-                    for rows in (slice(start, start + BLK), slice(HALF + start, HALF + start + BLK))
-                )
-                later, earlier = even + odd, even - odd
-                for u in range(start, start + BLK, 8):
-                    n = min(8, middle + 1 - u)
-                    if n > 0:
-                        out[q, middle + u:middle + u + n, :] = later[u - start:u - start + n]
-                        turned = reversed_rows(earlier[u - start:u - start + 8])
-                        out[q, middle - u - n + 1:middle - u + 1, :] = turned[8 - n:]
-
-
-def final(own, below, above, two_below, two_above):
+
+    @pl.loop(0, HALF // BLK)
+    def _(tile):
+        start = pl.multiple_of(tile * BLK, BLK)
+        for q in range(4):
+            far = (low, high)[q // 2]
+            even, odd = (
+                near[q, rows, :] + far[q % 2, rows, :].astype(jnp.float32)
+                for rows in (pl.ds(start, BLK), pl.ds(HALF + start, BLK))
+            )
+            for h in range(2):
+                lanes = slice(h * 128, (h + 1) * 128)
+                rows = pl.ds(q * (HALF + 1) + start, BLK)
+                later[h, rows, :] = even[:, lanes] + odd[:, lanes]
+                earlier[h, rows, :] = even[:, lanes] - odd[:, lanes]
+
+    def put(u):
+        slots = pl.ds(u, 4, stride=HALF + 1)
+        for h in range(2):
+            lanes = slice(h * 128, (h + 1) * 128)
+            out[middle + u, :, lanes] = later[h, slots, :]
+            out[middle - u, :, lanes] = earlier[h, slots, :]
+
+    @pl.loop(0, middle // 20)
+    def _(group):
+        for k in range(20):
+            put(group * 20 + k)
+
+    put(middle)
+
+
+def final(near, low, high):
     vmem = pl.BlockSpec(memory_space=pltpu.VMEM)
     return pl.pallas_call(
         final_kernel,
-        out_shape=jax.ShapeDtypeStruct((4, LAGS, 256), jnp.float32),
-        in_specs=[vmem] * 5,
+        out_shape=jax.ShapeDtypeStruct((LAGS, 4, 256), jnp.float32),
+        in_specs=[vmem] * 3,
         out_specs=vmem,
+        scratch_shapes=[pltpu.VMEM((2, 4 * (HALF + 1), 128), jnp.float32)] * 2,
         cost_estimate=pl.CostEstimate(flops=10_000_000, bytes_accessed=7_000_000, transcendentals=0),
         name="final",
-    )(own, below, above, two_below, two_above)
+    )(near, low, high)
 
 
 def moved(block, axis, to):
@@ -425,19 +433,23 @@
 
     barrier = lax.optimization_barrier
     step = CHUNKS[0]
-    x_0, x_1 = records[:step], records[step:]
+    x_0, later = barrier((records[:step], records))
+    x_1 = later[step:]
 
     def whitened(c, *pieces):
-        return whiten_bins(right, odd, table, [records, b0], pieces, step, c * step)
-
-    a1_0, a1_1, b0 = one_chip(x_0), one_chip(x_1), swap(records)
+        return whiten_bins(right, odd, table, [records, b0], pieces, c * step)
+
+    a1_0, b0 = one_chip(x_0), swap(records)
+    x_1, a1_0 = barrier((x_1, a1_0))
+    a1_1 = one_chip(x_1)
     a2_0, b1_0 = one_chip(a1_0), swap(a1_0)
-    a2_1, b1_1 = one_chip(a1_1), swap(a1_1)
     b2_0, o5_0 = swap(a2_0), first_half(a2_0, 1)
     part_0 = whitened(0, a1_0, b1_0, a2_0, b2_0, o5_0)
-    a2_1, b1_1, part_0 = barrier((a2_1, b1_1, part_0))
+    a1_1, part_0 = barrier((a1_1, part_0))
+    a2_1, b1_1 = one_chip(a1_1), swap(a1_1)
+    left = left_bins(odd, table, records, b0, [b1_0, b1_1])
+    a2_1, left = barrier((a2_1, left))
     b2_1, o5_1 = swap(a2_1), first_half(a2_1, 1)
-    left = left_bins(odd, table, records, b0, [b1_0, b1_1])
     part_1 = whitened(1, a1_1, b1_1, a2_1, b2_1, o5_1)
 
     parts = [part_0, part_1]
@@ -450,7 +462,8 @@
     down = (other + from_above[:2].astype(jnp.float32)).astype(jnp.bfloat16)
     two_below = moved(up, "tm", lambda i: i + 1)
     two_above = moved(down, "tm", lambda i: i - 1)
-    return final(own, from_below, from_above, two_below, two_above)
+    near = own + jnp.concatenate([from_above[2:], from_below[2:]], axis=0).astype(jnp.float32)
+    return jnp.transpose(final(near, two_below, two_above), (1, 0, 2))
 
 
 def solution(mesh):

time: 149 us -> 157 us (1.054)
  waiting for transfers between devices: 29 us -> 41.3 us
  starting transfers between devices: 35.6 us -> 33.5 us
  local copies, waits for them, and re-layouts: 9.89 us -> 8.15 us
    ppermute x15, waiting for transfers between devices: 29 us -> 41.3 us  [moved(): return lax.ppermute(block, axis, [(i, to(i) % size) for i in range(size)])]
    pallas_call x1 -> x0, local copies, waits for them, and re-layouts: 3.24 us -> none  [final(): pl.pallas_call(final_kernel, out_shape=jax.ShapeDtypeStruct((4, LAGS, 256...]
    ppermute x15, starting transfers between devices: 35.6 us -> 33.5 us  [moved(): return lax.ppermute(block, axis, [(i, to(i) % size) for i in range(size)])]
    pallas_call x2, Pallas kernels: 30.9 us -> 28.9 us  [gram(): pl.pallas_call(functools.partial(gram_kernel, tile), grid=(BINS // step,)...]
    unnamed x21 -> x35, local copies, waits for them, and re-layouts: 4.63 us -> 5.17 us
  transfers between devices with their start and end apart: 15 -> 15, of which waited for: 4 -> 7; matrix products, arithmetic and copies ran while one was open for 2% -> 4% of each run, Pallas kernels for 27% -> 22%
where the time goes in v4:
time: 157 us; the launch traced here: 156 us
  Pallas kernels  70 us (45%)
  waiting for transfers between devices  41.3 us (26%)
  starting transfers between devices  33.5 us (21%)
  local copies, waits for them, and re-layouts  8.15 us (5%)
  other arithmetic  2.41 us (2%)
    ppermute x15, waiting for transfers between devices, moved(): return lax.ppermute(block, axis, [(i, to(i) % size) for i in range(size)])  41.3 us
    ppermute x15, starting transfers between devices, moved(): return lax.ppermute(block, axis, [(i, to(i) % size) for i in range(size)])  33.5 us
    pallas_call x2, Pallas kernels, gram(): pl.pallas_call(functools.partial(gram_kernel, tile), grid=(BINS // step,)...  28.9 us
    pallas_call x2, Pallas kernels, whiten_bins(): pl.pallas_call(functools.partial(whiten_kernel, offset), out_shape=jax.Sh...  26.8 us
    pallas_call x1, Pallas kernels, left_bins(): pl.pallas_call(left_kernel, out_shape=jax.ShapeDtypeStruct((BINS, 2 * LEF...  10.8 us
    unnamed x35, local copies, waits for them, and re-layouts  5.17 us
    pallas_call x1, Pallas kernels, final(): pl.pallas_call(final_kernel, out_shape=jax.ShapeDtypeStruct((LAGS, 4, 256...  3.51 us
  transfers between devices with their start and end apart: 15, of which 7 were waited for; matrix products, arithmetic and copies ran while one was open for 4% of the time, Pallas kernels for 22%

profile of v4, /device:TPU:0, one launch (start us, length us, event | category | flops | bytes accessed | tf_op | source)
XLA Modules:
  0.0 156.3 jit_solution(16936889822010596370)
XLA Ops:
  0.0 0.0 collective-permute-start.2
  0.0 1.0 slice.31
  1.0 6.4 %collective-permute-start = (bf16[16,32,256]{2,1,0:T(8,128)(2,1)S(1)}, bf16[16,32,256]{2,1,0:T(8,128)(2,1)S(1)}, u32[]{:S(2)}, u32[]{:S(2)}) collective-permute-start(bf16[16,32,256]{2,1,0:T(8,128)(2,1)S(1)} %slice.31), channel_id=1, source_target_pairs={{0,62},{1,63},{2,0},{3,1},{4,2},{5,3},{6,4},{7,5},{8,6},{9,7},{10,... | collective-permute-start | bytes 786440 | tf_op jit(solution)/shard_map/ppermute | solution.py:403
  7.4 0.8 copy.9
  8.1 1.2 slice.32
  9.3 4.3 %collective-permute-done.a1 = bf16[16,32,256]{2,1,0:T(8,128)(2,1)S(1)} collective-permute-done((bf16[16,32,256]{2,1,0:T(8,128)(2,1)S(1)}, bf16[16,32,256]{2,1,0:T(8,128)(2,1)S(1)}, u32[]{:S(2)}, u32[]{:S(2)}) %collective-permute-start) | collective-permute-done | bytes 262176 | tf_op jit(solution)/shard_map/ppermute | solution.py:403
  13.6 5.8 %collective-permute-start.4 = (bf16[16,32,256]{2,1,0:T(8,128)(2,1)S(1)}, bf16[16,32,256]{2,1,0:T(8,128)(2,1)S(1)}, u32[]{:S(2)}, u32[]{:S(2)}) collective-permute-start(bf16[16,32,256]{2,1,0:T(8,128)(2,1)S(1)} %collective-permute-done.a1), channel_id=1, source_target_pairs={{0,62},{1,63},{2,0},{3,1},{4,2},{5,3},{6,4},{7,5},{8,6},{9,7},{10,... | collective-permute-start | bytes 786440 | tf_op jit(solution)/shard_map/ppermute | solution.py:403
  19.4 0.0 copy-done.9
  19.4 0.0 copy-done.10
  19.4 0.1 collective-permute-start.1
  19.5 0.6 gather_fusion
  20.1 0.1 collective-permute-start.3
  20.2 5.9 %collective-permute-done.4.a2 = bf16[16,32,256]{2,1,0:T(8,128)(2,1)S(1)} collective-permute-done((bf16[16,32,256]{2,1,0:T(8,128)(2,1)S(1)}, bf16[16,32,256]{2,1,0:T(8,128)(2,1)S(1)}, u32[]{:S(2)}, u32[]{:S(2)}) %collective-permute-start.4) | collective-permute-done | bytes 262176 | tf_op jit(solution)/shard_map/ppermute | solution.py:403
  26.2 3.0 %collective-permute-start.6 = (bf16[16,16,256]{2,1,0:T(8,128)(2,1)S(1)}, bf16[16,16,256]{2,1,0:T(8,128)(2,1)S(1)}, u32[]{:S(2)}, u32[]{:S(2)}) collective-permute-start(bf16[16,16,256]{2,1,0:T(8,128)(2,1)S(1)} %slice.44), channel_id=1, source_target_pairs={{0,63},{1,0},{2,1},{3,2},{4,3},{5,4},{6,5},{7,6},{8,7},{9,8},{10,9... | collective-permute-start | bytes 393224 | tf_op jit(solution)/shard_map/ppermute | solution.py:403
  29.2 0.0 collective-permute-start.5
  29.2 0.7 fusion
  29.9 0.0 collective-permute-done.3.b1.refs_0_
  29.9 13.2 %collective-permute-done.6.o5 = bf16[16,16,256]{2,1,0:T(8,128)(2,1)S(1)} collective-permute-done((bf16[16,16,256]{2,1,0:T(8,128)(2,1)S(1)}, bf16[16,16,256]{2,1,0:T(8,128)(2,1)S(1)}, u32[]{:S(2)}, u32[]{:S(2)}) %collective-permute-start.6) | collective-permute-done | bytes 131104 | tf_op jit(solution)/shard_map/ppermute | solution.py:403
  43.1 0.0 collective-permute-done.5.b2
  43.1 0.0 collective-permute-done.2.b0
  43.1 0.0 copy-start.11
  43.1 0.0 copy-done.14
  43.1 0.0 copy-done.8
  43.1 0.0 copy-done.1
  43.2 0.6 copy-done.16
  43.8 0.1 copy-done.15
  43.9 0.3 copy-done.11
  44.2 8.1 %whiten.2.refs_0_ = bf16[2,256,32,128]{3,2,1,0:T(8,128)(2,1)} custom-call(s32[16]{0:T(128)} %get-tuple-element.31.right_ref, s32[1]{0:T(128)} %bitcast.1.odd_ref, bf16[512,256]{1,0:T(8,128)(2,1)} %constant.54.clone.table_ref, bf16[64,32,256]{2,1,0:T(8,128)(2,1)} %x0.5, bf16[64,32,256]{2,1,0:T(8,128)(2,1)} %copy-done.11, bf16[16,32,256]{2,1,0:T(8,128)(2,1)} %copy-done.14, ...), custom_call_target="tpu_custom_call" | custom-call | flops 3840000000 | bytes 8000000 | tf_op jit(solution)/shard_map/whiten/pallas_call | solution.py:139
  52.4 0.0 collective-permute-done.1.a1
  52.4 0.1 collective-permute-start.8
  52.5 5.6 %collective-permute-start.7 = (bf16[48,32,256]{2,1,0:T(8,128)(2,1)}, bf16[48,32,256]{2,1,0:T(8,128)(2,1)S(1)}, u32[]{:S(2)}, u32[]{:S(2)}) collective-permute-start(bf16[48,32,256]{2,1,0:T(8,128)(2,1)} %collective-permute-done.1.a1), channel_id=1, source_target_pairs={{0,62},{1,63},{2,0},{3,1},{4,2},{5,3},{6,4},{7,5},{8,6},{9,7},{10,... | collective-permute-start | bytes 2359304 | tf_op jit(solution)/shard_map/ppermute | solution.py:403
  58.1 0.0 collective-permute-done.8.refs_1_.b1
  58.1 0.0 copy-done.4
  58.1 0.9 copy-done.2
  59.0 10.8 %left.1.left_ref = bf16[256,128,128]{2,1,0:T(8,128)(2,1)} custom-call(s32[1]{0:T(128)} %bitcast.1.odd_ref, bf16[512,256]{1,0:T(8,128)(2,1)S(1)} %copy-done.4, bf16[64,32,256]{2,1,0:T(8,128)(2,1)} %x0.5, bf16[64,32,256]{2,1,0:T(8,128)(2,1)} %copy-done.11, bf16[16,32,256]{2,1,0:T(8,128)(2,1)S(1)} %copy-done.2, ...), custom_call_target="tpu_custom_call" | custom-call | flops 6000000000 | bytes 14000000 | tf_op jit(solution)/shard_map/left/pallas_call | solution.py:229
  69.8 0.0 copy-done
  69.9 5.6 %collective-permute-done.7.a2 = bf16[48,32,256]{2,1,0:T(8,128)(2,1)S(1)} collective-permute-done((bf16[48,32,256]{2,1,0:T(8,128)(2,1)}, bf16[48,32,256]{2,1,0:T(8,128)(2,1)S(1)}, u32[]{:S(2)}, u32[]{:S(2)}) %collective-permute-start.7) | collective-permute-done | bytes 786464 | tf_op jit(solution)/shard_map/ppermute | solution.py:403
  75.4 0.0 collective-permute-start.9
  75.5 5.9 %collective-permute-start.10 = (bf16[48,16,256]{2,1,0:T(8,128)(2,1)S(1)}, bf16[48,16,256]{2,1,0:T(8,128)(2,1)S(1)}, u32[]{:S(2)}, u32[]{:S(2)}) collective-permute-start(bf16[48,16,256]{2,1,0:T(8,128)(2,1)S(1)} %slice.35), channel_id=1, source_target_pairs={{0,63},{1,0},{2,1},{3,2},{4,3},{5,4},{6,5},{7,6},{8,7},{9,8},{10,9... | collective-permute-start | bytes 1179656 | tf_op jit(solution)/shard_map/ppermute | solution.py:403
  82.0 0.1 broadcast_in_dim.10
  82.1 0.1 broadcast_in_dim_reshape.3.first_ref
  82.2 0.0 copy-start.3
  82.2 4.5 %collective-permute-done.10.o5 = bf16[48,16,256]{2,1,0:T(8,128)(2,1)S(1)} collective-permute-done((bf16[48,16,256]{2,1,0:T(8,128)(2,1)S(1)}, bf16[48,16,256]{2,1,0:T(8,128)(2,1)S(1)}, u32[]{:S(2)}, u32[]{:S(2)}) %collective-permute-start.10) | collective-permute-done | bytes 393248 | tf_op jit(solution)/shard_map/ppermute | solution.py:403
  86.7 0.0 collective-permute-done.9.b2
  86.7 0.0 copy-done.7
  86.7 0.7 copy-done.13
  87.4 0.9 copy-done.12
  88.3 18.7 %whiten.3.refs_1_ = bf16[2,256,96,128]{3,2,1,0:T(8,128)(2,1)} custom-call(s32[16]{0:T(128)} %get-tuple-element.31.right_ref, s32[1]{0:T(128)} %bitcast.1.odd_ref, bf16[512,256]{1,0:T(8,128)(2,1)} %constant.54.clone.table_ref, bf16[64,32,256]{2,1,0:T(8,128)(2,1)} %x0.5, bf16[64,32,256]{2,1,0:T(8,128)(2,1)} %copy-done.11, ...), custom_call_target="tpu_custom_call" | custom-call | flops 11520000000 | bytes 8000000 | tf_op jit(solution)/shard_map/whiten/pallas_call | solution.py:139
  107.0 0.0 copy-done.3
  107.0 13.5 %gram.3 = (bf16[4,416,256]{2,1,0:T(8,128)(2,1)S(1)}, bf16[4,416,256]{2,1,0:T(8,128)(2,1)S(1)}) custom-call(s32[16]{0:T(128)S(1)} %compare_convert_fusion.live_ref, s32[1,256]{1,0:T(1,128)S(1)} %broadcast_in_dim_reshape.3.first_ref, bf16[2,416,256]{2,1,0:T(8,128)(2,1)S(1)} %copy-done.3, bf16[256,128,128]{2,1,0:T(8,128)(2,1)} %left.1.left_ref, ...), custom_call_target="tpu_custom_call" | custom-call | flops 16000000000 | bytes 20000000 | tf_op jit(solution)/shard_map/gram/pallas_call | solution.py:333
  120.5 3.1 %collective-permute-start.11 = (bf16[4,416,256]{2,1,0:T(8,128)(2,1)S(1)}, bf16[4,416,256]{2,1,0:T(8,128)(2,1)S(1)}, u32[]{:S(2)}, u32[]{:S(2)}) collective-permute-start(bf16[4,416,256]{2,1,0:T(8,128)(2,1)S(1)} %get-tuple-element.27), channel_id=1, source_target_pairs={{0,192},{64,0},{128,64},{192,128},{1,193},{65,1},{129,65},{193,129... | collective-permute-start | bytes 2555912 | tf_op jit(solution)/shard_map/ppermute | solution.py:403
  123.6 0.0 collective-permute-start.12
  123.6 15.4 %gram.2 = (f32[2,416,256]{2,1,0:T(8,128)S(1)}, f32[2,416,256]{2,1,0:T(8,128)S(1)}, f32[4,416,256]{2,1,0:T(8,128)S(1)}) custom-call(s32[16]{0:T(128)S(1)} %compare_convert_fusion.live_ref, s32[1,256]{1,0:T(1,128)S(1)} %broadcast_in_dim_reshape.3.first_ref, bf16[2,416,256]{2,1,0:T(8,128)(2,1)S(1)} %copy-done.3, bf16[256,128,128]{2,1,0:T(8,128)(2,1)} %left.1.left_ref, ...), custom_call_target="tpu_custom_call" | custom-call | flops 16000000000 | bytes 20000000 | tf_op jit(solution)/shard_map/gram/pallas_call | solution.py:333
  139.0 0.0 collective-permute-done.11
  139.0 0.1 add_convert_fusion
  139.1 3.4 %collective-permute-start.14 = (bf16[2,416,256]{2,1,0:T(8,128)(2,1)S(1)}, bf16[2,416,256]{2,1,0:T(8,128)(2,1)S(1)}, u32[]{:S(2)}, u32[]{:S(2)}) collective-permute-start(bf16[2,416,256]{2,1,0:T(8,128)(2,1)S(1)} %add_convert_fusion), channel_id=1, source_target_pairs={{0,192},{64,0},{128,64},{192,128},{1,193},{65,1},{129,65},{193,129... | collective-permute-start | bytes 1277960 | tf_op jit(solution)/shard_map/ppermute | solution.py:403
  142.5 0.0 collective-permute-done.12
  142.5 0.1 add_convert_fusion.1
  142.6 0.1 collective-permute-start.13
  142.8 1.4 convert_add_fusion.near
  144.2 3.9 %collective-permute-done.14.high = bf16[2,416,256]{2,1,0:T(8,128)(2,1)S(1)} collective-permute-done((bf16[2,416,256]{2,1,0:T(8,128)(2,1)S(1)}, bf16[2,416,256]{2,1,0:T(8,128)(2,1)S(1)}, u32[]{:S(2)}, u32[]{:S(2)}) %collective-permute-start.14) | collective-permute-done | bytes 426016 | tf_op jit(solution)/shard_map/ppermute | solution.py:403
  148.1 3.9 %collective-permute-done.13.low = bf16[2,416,256]{2,1,0:T(8,128)(2,1)S(1)} collective-permute-done((bf16[2,416,256]{2,1,0:T(8,128)(2,1)S(1)}, bf16[2,416,256]{2,1,0:T(8,128)(2,1)S(1)}, u32[]{:S(2)}, u32[]{:S(2)}) %collective-permute-start.13) | collective-permute-done | bytes 426016 | tf_op jit(solution)/shard_map/ppermute | solution.py:403
  152.0 0.8 copy-done.6
  152.8 3.5 %final.1 = f32[401,4,256]{2,1,0:T(4,128)} custom-call(f32[4,416,256]{2,1,0:T(8,128)} %convert_add_fusion.near, bf16[2,416,256]{2,1,0:T(8,128)(2,1)} %copy-done.6, bf16[2,416,256]{2,1,0:T(8,128)(2,1)} %copy-done.5), custom_call_target="tpu_custom_call" | custom-call | flops 10000000 | bytes 7000000 | tf_op jit(solution)/shard_map/final/pallas_call | solution.py:390
  (24 shorter events, 0.1 us)
Async XLA Ops:
  0.0 19.4 %copy-start.9 = (s32[16]{0:T(128)S(1)}, s32[16]{0:T(128)}, u32[]{:S(2)}) copy-start(s32[16]{0:T(128)} %constant.53.clone) | copy-start | bytes 196
  0.0 19.4 %copy-start.10 = (s32[16]{0:T(128)S(1)}, s32[16]{0:T(128)}, u32[]{:S(2)}) copy-start(s32[16]{0:T(128)} %constant.52.clone) | copy-start | bytes 196
  0.0 43.1 %collective-permute-start.2 = (bf16[64,32,256]{2,1,0:T(8,128)(2,1)}, bf16[64,32,256]{2,1,0:T(8,128)(2,1)S(1)}, u32[]{:S(2)}, u32[]{:S(2)}) collective-permute-start(bf16[64,32,256]{2,1,0:T(8,128)(2,1)} %x0.5), channel_id=1, source_target_pairs={{0,1},{1,0},{2,3},{3,2},{4,5},{5,4},{6,7},{7,6},{8,9},{9,8},{10,11... | collective-permute-start | bytes 3145736 | tf_op jit(solution)/shard_map/ppermute | solution.py:403
  1.0 12.6 %collective-permute-start = (bf16[16,32,256]{2,1,0:T(8,128)(2,1)S(1)}, bf16[16,32,256]{2,1,0:T(8,128)(2,1)S(1)}, u32[]{:S(2)}, u32[]{:S(2)}) collective-permute-start(bf16[16,32,256]{2,1,0:T(8,128)(2,1)S(1)} %slice.31), channel_id=1, source_target_pairs={{0,62},{1,63},{2,0},{3,1},{4,2},{5,3},{6,4},{7,5},{8,6},{9,7},{10,... | collective-permute-start | bytes 786440 | tf_op jit(solution)/shard_map/ppermute | solution.py:403
  13.6 29.5 %copy-start.14 = (bf16[16,32,256]{2,1,0:T(8,128)(2,1)}, bf16[16,32,256]{2,1,0:T(8,128)(2,1)S(1)}, u32[]{:S(2)}) copy-start(bf16[16,32,256]{2,1,0:T(8,128)(2,1)S(1)} %collective-permute-done.a1) | copy-start | bytes 786436
  13.6 12.5 %collective-permute-start.4 = (bf16[16,32,256]{2,1,0:T(8,128)(2,1)S(1)}, bf16[16,32,256]{2,1,0:T(8,128)(2,1)S(1)}, u32[]{:S(2)}, u32[]{:S(2)}) collective-permute-start(bf16[16,32,256]{2,1,0:T(8,128)(2,1)S(1)} %collective-permute-done.a1), channel_id=1, source_target_pairs={{0,62},{1,63},{2,0},{3,1},{4,2},{5,3},{6,4},{7,5},{8,6},{9,7},{10,... | collective-permute-start | bytes 786440 | tf_op jit(solution)/shard_map/ppermute | solution.py:403
  19.4 32.9 %collective-permute-start.1 = (bf16[48,32,256]{2,1,0:T(8,128)(2,1)S(1)}, bf16[48,32,256]{2,1,0:T(8,128)(2,1)}, u32[]{:S(2)}, u32[]{:S(2)}) collective-permute-start(bf16[48,32,256]{2,1,0:T(8,128)(2,1)S(1)} %slice.32), channel_id=1, source_target_pairs={{0,62},{1,63},{2,0},{3,1},{4,2},{5,3},{6,4},{7,5},{8,6},{9,7},{10,... | collective-permute-start | bytes 2359304 | tf_op jit(solution)/shard_map/ppermute | solution.py:403
  20.1 9.8 %collective-permute-start.3 = (bf16[16,32,256]{2,1,0:T(8,128)(2,1)S(1)}, bf16[16,32,256]{2,1,0:T(8,128)(2,1)S(1)}, u32[]{:S(2)}, u32[]{:S(2)}) collective-permute-start(bf16[16,32,256]{2,1,0:T(8,128)(2,1)S(1)} %collective-permute-done.a1), channel_id=1, source_target_pairs={{0,1},{1,0},{2,3},{3,2},{4,5},{5,4},{6,7},{7,6},{8,9},{9,8},{10,11... | collective-permute-start | bytes 786440 | tf_op jit(solution)/shard_map/ppermute | solution.py:403
  26.1 17.0 %copy-start.8 = (bf16[16,32,256]{2,1,0:T(8,128)(2,1)}, bf16[16,32,256]{2,1,0:T(8,128)(2,1)S(1)}, u32[]{:S(2)}) copy-start(bf16[16,32,256]{2,1,0:T(8,128)(2,1)S(1)} %collective-permute-done.4.a2) | copy-start | bytes 786436
  26.2 16.9 %collective-permute-start.6 = (bf16[16,16,256]{2,1,0:T(8,128)(2,1)S(1)}, bf16[16,16,256]{2,1,0:T(8,128)(2,1)S(1)}, u32[]{:S(2)}, u32[]{:S(2)}) collective-permute-start(bf16[16,16,256]{2,1,0:T(8,128)(2,1)S(1)} %slice.44), channel_id=1, source_target_pairs={{0,63},{1,0},{2,1},{3,2},{4,3},{5,4},{6,5},{7,6},{8,7},{9,8},{10,9... | collective-permute-start | bytes 393224 | tf_op jit(solution)/shard_map/ppermute | solution.py:403
  29.2 13.9 %collective-permute-start.5 = (bf16[16,32,256]{2,1,0:T(8,128)(2,1)S(1)}, bf16[16,32,256]{2,1,0:T(8,128)(2,1)S(1)}, u32[]{:S(2)}, u32[]{:S(2)}) collective-permute-start(bf16[16,32,256]{2,1,0:T(8,128)(2,1)S(1)} %collective-permute-done.4.a2), channel_id=1, source_target_pairs={{0,1},{1,0},{2,3},{3,2},{4,5},{5,4},{6,7},{7,6},{8,9},{9,8},{10,11... | collective-permute-start | bytes 786440 | tf_op jit(solution)/shard_map/ppermute | solution.py:403
  29.9 13.3 %copy-start.1 = (bf16[16,32,256]{2,1,0:T(8,128)(2,1)}, bf16[16,32,256]{2,1,0:T(8,128)(2,1)S(1)}, u32[]{:S(2)}) copy-start(bf16[16,32,256]{2,1,0:T(8,128)(2,1)S(1)} %collective-permute-done.3.b1.refs_0_) | copy-start | bytes 786436
  43.1 0.7 copy-start.16
  43.1 0.8 copy-start.15
  43.1 1.1 copy-start.11
  44.2 13.9 %copy-start.4 = (bf16[512,256]{1,0:T(8,128)(2,1)S(1)}, bf16[512,256]{1,0:T(8,128)(2,1)}, u32[]{:S(2)}) copy-start(bf16[512,256]{1,0:T(8,128)(2,1)} %constant.54.clone.table_ref) | copy-start | bytes 786436
  52.4 5.7 %collective-permute-start.8 = (bf16[48,32,256]{2,1,0:T(8,128)(2,1)}, bf16[48,32,256]{2,1,0:T(8,128)(2,1)S(1)}, u32[]{:S(2)}, u32[]{:S(2)}) collective-permute-start(bf16[48,32,256]{2,1,0:T(8,128)(2,1)} %collective-permute-done.1.a1), channel_id=1, source_target_pairs={{0,1},{1,0},{2,3},{3,2},{4,5},{5,4},{6,7},{7,6},{8,9},{9,8},{10,11... | collective-permute-start | bytes 2359304 | tf_op jit(solution)/shard_map/ppermute | solution.py:403
  52.5 23.0 %collective-permute-start.7 = (bf16[48,32,256]{2,1,0:T(8,128)(2,1)}, bf16[48,32,256]{2,1,0:T(8,128)(2,1)S(1)}, u32[]{:S(2)}, u32[]{:S(2)}) collective-permute-start(bf16[48,32,256]{2,1,0:T(8,128)(2,1)} %collective-permute-done.1.a1), channel_id=1, source_target_pairs={{0,62},{1,63},{2,0},{3,1},{4,2},{5,3},{6,4},{7,5},{8,6},{9,7},{10,... | collective-permute-start | bytes 2359304 | tf_op jit(solution)/shard_map/ppermute | solution.py:403
  58.1 1.0 copy-start.2
  59.0 10.8 %copy-start = (bf16[48,32,256]{2,1,0:T(8,128)(2,1)}, bf16[48,32,256]{2,1,0:T(8,128)(2,1)S(1)}, u32[]{:S(2)}) copy-start(bf16[48,32,256]{2,1,0:T(8,128)(2,1)S(1)} %collective-permute-done.8.refs_1_.b1) | copy-start | bytes 2359300
  75.4 11.2 %copy-start.7 = (bf16[48,32,256]{2,1,0:T(8,128)(2,1)}, bf16[48,32,256]{2,1,0:T(8,128)(2,1)S(1)}, u32[]{:S(2)}) copy-start(bf16[48,32,256]{2,1,0:T(8,128)(2,1)S(1)} %collective-permute-done.7.a2) | copy-start | bytes 2359300
  75.4 11.2 %collective-permute-start.9 = (bf16[48,32,256]{2,1,0:T(8,128)(2,1)S(1)}, bf16[48,32,256]{2,1,0:T(8,128)(2,1)S(1)}, u32[]{:S(2)}, u32[]{:S(2)}) collective-permute-start(bf16[48,32,256]{2,1,0:T(8,128)(2,1)S(1)} %collective-permute-done.7.a2), channel_id=1, source_target_pairs={{0,1},{1,0},{2,3},{3,2},{4,5},{5,4},{6,7},{7,6},{8,9},{9,8},{10,11... | collective-permute-start | bytes 2359304 | tf_op jit(solution)/shard_map/ppermute | solution.py:403
  75.5 11.2 %collective-permute-start.10 = (bf16[48,16,256]{2,1,0:T(8,128)(2,1)S(1)}, bf16[48,16,256]{2,1,0:T(8,128)(2,1)S(1)}, u32[]{:S(2)}, u32[]{:S(2)}) collective-permute-start(bf16[48,16,256]{2,1,0:T(8,128)(2,1)S(1)} %slice.35), channel_id=1, source_target_pairs={{0,63},{1,0},{2,1},{3,2},{4,3},{5,4},{6,5},{7,6},{8,7},{9,8},{10,9... | collective-permute-start | bytes 1179656 | tf_op jit(solution)/shard_map/ppermute | solution.py:403
  82.2 24.8 %copy-start.3 = (bf16[2,416,256]{2,1,0:T(8,128)(2,1)S(1)}, bf16[2,416,256]{2,1,0:T(8,128)(2,1)}, u32[]{:S(2)}) copy-start(bf16[2,416,256]{2,1,0:T(8,128)(2,1)} %constant.55.clone.table_ref) | copy-start | bytes 1277956
  86.7 0.7 copy-start.13
  87.4 0.9 copy-start.12
  120.5 18.4 %collective-permute-start.11 = (bf16[4,416,256]{2,1,0:T(8,128)(2,1)S(1)}, bf16[4,416,256]{2,1,0:T(8,128)(2,1)S(1)}, u32[]{:S(2)}, u32[]{:S(2)}) collective-permute-start(bf16[4,416,256]{2,1,0:T(8,128)(2,1)S(1)} %get-tuple-element.27), channel_id=1, source_target_pairs={{0,192},{64,0},{128,64},{192,128},{1,193},{65,1},{129,65},{193,129... | collective-permute-start | bytes 2555912 | tf_op jit(solution)/shard_map/ppermute | solution.py:403
  123.6 18.9 %collective-permute-start.12 = (bf16[4,416,256]{2,1,0:T(8,128)(2,1)S(1)}, bf16[4,416,256]{2,1,0:T(8,128)(2,1)S(1)}, u32[]{:S(2)}, u32[]{:S(2)}) collective-permute-start(bf16[4,416,256]{2,1,0:T(8,128)(2,1)S(1)} %get-tuple-element.28), channel_id=1, source_target_pairs={{0,64},{64,128},{128,192},{192,0},{1,65},{65,129},{129,193},{193,1... | collective-permute-start | bytes 2555912 | tf_op jit(solution)/shard_map/ppermute | solution.py:403
  139.1 9.0 %collective-permute-start.14 = (bf16[2,416,256]{2,1,0:T(8,128)(2,1)S(1)}, bf16[2,416,256]{2,1,0:T(8,128)(2,1)S(1)}, u32[]{:S(2)}, u32[]{:S(2)}) collective-permute-start(bf16[2,416,256]{2,1,0:T(8,128)(2,1)S(1)} %add_convert_fusion), channel_id=1, source_target_pairs={{0,192},{64,0},{128,64},{192,128},{1,193},{65,1},{129,65},{193,129... | collective-permute-start | bytes 1277960 | tf_op jit(solution)/shard_map/ppermute | solution.py:403
  142.6 9.4 %collective-permute-start.13 = (bf16[2,416,256]{2,1,0:T(8,128)(2,1)S(1)}, bf16[2,416,256]{2,1,0:T(8,128)(2,1)S(1)}, u32[]{:S(2)}, u32[]{:S(2)}) collective-permute-start(bf16[2,416,256]{2,1,0:T(8,128)(2,1)S(1)} %add_convert_fusion.1), channel_id=1, source_target_pairs={{0,64},{64,128},{128,192},{192,0},{1,65},{65,129},{129,193},{193,1... | collective-permute-start | bytes 1277960 | tf_op jit(solution)/shard_map/ppermute | solution.py:403
  148.1 3.9 %copy-start.5 = (bf16[2,416,256]{2,1,0:T(8,128)(2,1)}, bf16[2,416,256]{2,1,0:T(8,128)(2,1)S(1)}, u32[]{:S(2)}) copy-start(bf16[2,416,256]{2,1,0:T(8,128)(2,1)S(1)} %collective-permute-done.14.high) | copy-start | bytes 1277956
  152.0 0.8 copy-start.6

commit v5 on v4

--- a/solution.py
+++ b/solution.py
@@ -17,8 +17,9 @@
 SLOTS = 16
 BINS = 256
 LEFT = 64
+OWN = 32
 BAND = 176
-CHUNKS = (16, 48)
+CHUNKS = (32, 32)
 PITCH = 513
 GROUP = 16
 
@@ -73,7 +74,7 @@
         whiten(i + 1, spec_b)
 
 
-def whiten_kernel(offset, right_ref, odd_ref, table_ref, x0, b0, a1, b1, a2, b2, o5, out_ref,
+def whiten_kernel(right_ref, odd_ref, table_ref, x0, b0, a1, b1, a2, b2, o5, out_ref,
                   band, spec_a, spec_b, bins_ref, packed, sems):
     segs = a1.shape[0]
     depth = 2 * segs
@@ -82,8 +83,8 @@
 
     @pl.loop(0, segs)
     def _(s):
-        band[s, 0:32, :] = x0[offset + s]
-        band[s, 32:64, :] = jnp.where(odd, b1[s], b0[offset + s])
+        band[s, 0:32, :] = x0[s]
+        band[s, 32:64, :] = jnp.where(odd, b1[s], b0[s])
         band[s, 64:96, :] = a1[s]
         band[s, 96:128, :] = jnp.where(odd, b2[s], b1[s])
         band[s, 128:160, :] = a2[s]
@@ -131,15 +132,16 @@
     return pl.BlockSpec(shape, lambda *_: (0,) * len(shape))
 
 
-def whiten_bins(right, odd, table, whole_pieces, pieces, offset):
+def whiten_bins(right, odd, table, whole_pieces, pieces, chunk):
     smem = pl.BlockSpec(memory_space=pltpu.SMEM)
-    vmem = pl.BlockSpec(memory_space=pltpu.VMEM)
     segs = pieces[0].shape[0]
+    share = pl.BlockSpec((segs, 32, BINS), lambda _: (chunk, 0, 0))
     shape = (2, BINS, 2 * segs, 128)
     return pl.pallas_call(
-        functools.partial(whiten_kernel, offset),
+        whiten_kernel,
+        grid=(1,),
         out_shape=jax.ShapeDtypeStruct(shape, jnp.bfloat16),
-        in_specs=[smem, smem] + [vmem] * (3 + len(pieces)),
+        in_specs=[smem, smem, whole(table.shape), share, share] + [whole(p.shape) for p in pieces],
         out_specs=pl.BlockSpec(memory_space=pl.ANY),
         scratch_shapes=[
             pltpu.VMEM((segs, BAND, BINS), jnp.bfloat16),
@@ -149,29 +151,37 @@
             pltpu.VMEM(shape, jnp.bfloat16),
             pltpu.SemaphoreType.DMA((BINS // GROUP,)),
         ],
-        compiler_params=pltpu.CompilerParams(vmem_limit_bytes=54 * MIB),
+        compiler_params=pltpu.CompilerParams(vmem_limit_bytes=52 * MIB),
         cost_estimate=pl.CostEstimate(flops=240_000_000 * segs, bytes_accessed=8_000_000, transcendentals=0),
         name="whiten",
     )(right, odd, table, *whole_pieces, *pieces)
 
 
-def left_kernel(odd_ref, table_ref, x0, b0, *refs):
-    pieces = refs[:len(CHUNKS)]
-    out_ref, records, spec_a, spec_b, bins_ref, packed, sems = refs[len(CHUNKS):]
+def left_kernel(odd_ref, table_ref, *refs):
+    out_ref, records, spec_a, spec_b, bins_ref, packed, sems = refs[-7:]
+    pieces = refs[:-7]
     odd = odd_ref[0] == 1
-    segs = x0.shape[0]
-    spread = LEFT + 1
-    pitch = 2 * LEFT + 1
-    offset = 0
-    for piece in pieces:
-        @pl.loop(0, piece.shape[0])
-        def _(i, piece=piece, offset=offset):
-            s = offset + i
-            both = jnp.concatenate([x0[s], jnp.where(odd, piece[i], b0[s])], axis=0).astype(jnp.float32)
-            for h in range(2):
-                records[h, pl.ds(s * spread, LEFT), :] = both[:, h * 128:(h + 1) * 128]
-
-        offset += piece.shape[0]
+    segs = pieces[0].shape[0]
+    spread = OWN + 1
+    pitch = 2 * OWN + 1
+
+    def fill(s, channels):
+        channels = channels.astype(jnp.float32)
+        for h in range(2):
+            records[h, pl.ds(s * spread, OWN), :] = channels[:, h * 128:(h + 1) * 128]
+
+    if len(pieces) == 1:
+        @pl.loop(0, segs)
+        def _(s):
+            fill(s, pieces[0][s])
+    else:
+        offset = 0
+        for piece in pieces[1:]:
+            @pl.loop(0, piece.shape[0])
+            def _(i, piece=piece, offset=offset):
+                fill(offset + i, jnp.where(odd, piece[i], pieces[0][offset + i]))
+
+            offset += piece.shape[0]
 
     def transform(quad, spec):
         rows = [
@@ -196,16 +206,16 @@
                 imag_other = pltpu.roll(imag_part, LEFT, 1)
                 rows = [
                     (a, jnp.where(in_first, real_part, imag_other)),
-                    (LEFT + a, jnp.where(in_first, imag_part, -real_other)),
+                    (OWN + a, jnp.where(in_first, imag_part, -real_other)),
                     (a + 1, jnp.where(in_first, real_other, imag_part)),
-                    (LEFT + a + 1, jnp.where(in_first, imag_other, -real_part)),
+                    (OWN + a + 1, jnp.where(in_first, imag_other, -real_part)),
                 ]
                 for row, value in rows:
                     bins_ref[pl.ds(f * pitch + row, 8, stride=pitch), :] = value
 
             whiten_tile(spec, slice(h * 128, (h + 1) * 128), put)
 
-    in_turns(LEFT // 4, transform, whiten, spec_a, spec_b)
+    in_turns(OWN // 4, transform, whiten, spec_a, spec_b)
 
     def copy(group):
         some = pl.ds(group * GROUP, GROUP)
@@ -215,7 +225,7 @@
     def _(group):
         for step in range(GROUP):
             f = group * GROUP + step
-            packed[f] = bins_ref[pl.ds(f * pitch, 2 * LEFT), :].astype(jnp.bfloat16)
+            packed[f] = bins_ref[pl.ds(f * pitch, 2 * OWN), :].astype(jnp.bfloat16)
         copy(group).start()
 
     @pl.loop(0, BINS // GROUP)
@@ -223,26 +233,27 @@
         copy(group).wait()
 
 
-def left_bins(odd, table, x0, b0, pieces):
+def left_bins(odd, table, pieces):
     vmem = pl.BlockSpec(memory_space=pltpu.VMEM)
     smem = pl.BlockSpec(memory_space=pltpu.SMEM)
+    shape = (BINS, 2 * OWN, 128)
     return pl.pallas_call(
         left_kernel,
-        out_shape=jax.ShapeDtypeStruct((BINS, 2 * LEFT, 128), jnp.bfloat16),
-        in_specs=[smem] + [vmem] * (3 + len(pieces)),
+        out_shape=jax.ShapeDtypeStruct(shape, jnp.bfloat16),
+        in_specs=[smem] + [vmem] * (1 + len(pieces)),
         out_specs=pl.BlockSpec(memory_space=pl.ANY),
         scratch_shapes=[
-            pltpu.VMEM((2, x0.shape[0] * (LEFT + 1), 128), jnp.float32),
+            pltpu.VMEM((2, pieces[0].shape[0] * (OWN + 1), 128), jnp.float32),
             pltpu.VMEM((512, 256), jnp.float32),
             pltpu.VMEM((512, 256), jnp.float32),
-            pltpu.VMEM((BINS * (2 * LEFT + 1), 128), jnp.float32),
-            pltpu.VMEM((BINS, 2 * LEFT, 128), jnp.bfloat16),
+            pltpu.VMEM((BINS * (2 * OWN + 1), 128), jnp.float32),
+            pltpu.VMEM(shape, jnp.bfloat16),
             pltpu.SemaphoreType.DMA((BINS // GROUP,)),
         ],
-        compiler_params=pltpu.CompilerParams(vmem_limit_bytes=52 * MIB),
-        cost_estimate=pl.CostEstimate(flops=6_000_000_000, bytes_accessed=14_000_000, transcendentals=0),
+        compiler_params=pltpu.CompilerParams(vmem_limit_bytes=48 * MIB),
+        cost_estimate=pl.CostEstimate(flops=4_000_000_000, bytes_accessed=8_000_000, transcendentals=0),
         name="left",
-    )(odd, table, x0, b0, *pieces)
+    )(odd, table, *pieces)
 
 
 def lag_sums(table_ref, cross_ref, lags):
@@ -284,12 +295,12 @@
                     put(k, rows, slice(ha * 128, (ha + 1) * 128), arrays[k])
 
 
-def gram_kernel(tile, live_ref, first_ref, table_ref, left_ref, *refs):
+def gram_kernel(tile, live_ref, first_ref, table_ref, own_ref, next_ref, *refs):
     parts = refs[:len(CHUNKS)]
     outs = refs[len(CHUNKS):-2]
     sums, lags = refs[-2:]
     block = pl.program_id(0)
-    bins = left_ref.shape[0]
+    bins = own_ref.shape[0]
     first = first_ref[...]
     chosen = [jnp.broadcast_to(first == i, (BLK, 128)) for i in range(3)]
 
@@ -302,9 +313,11 @@
                 [p[0, local_bin, part * n:(part + 1) * n, :] for part in range(2) for p, n in zip(parts, CHUNKS)],
                 axis=0,
             )
-            cross = jnp.dot(left_ref[local_bin], right, preferred_element_type=jnp.float32)
+            left = jnp.concatenate([own_ref[local_bin], next_ref[local_bin]], axis=0)
+            cross = jnp.dot(left, right, preferred_element_type=jnp.float32)
             for part in range(2):
-                blocks = [cross[part * LEFT + i * BLK:part * LEFT + (i + 1) * BLK] for i in range(4)]
+                starts = [i // 2 * LEFT + part * OWN + i % 2 * BLK for i in range(4)]
+                blocks = [cross[start:start + BLK] for start in starts]
                 own = blocks[3]
                 for i in range(3):
                     own = jnp.where(chosen[i], blocks[i], own)
@@ -338,8 +351,8 @@
             pl.BlockSpec(memory_space=pltpu.SMEM),
             pl.BlockSpec((1, 128), lambda k: (0, tile)),
             whole(table.shape),
-            pl.BlockSpec((step,) + left.shape[1:], lambda k: (k, 0, 0)),
         ]
+        + [pl.BlockSpec((step,) + p.shape[1:], lambda k: (k, 0, 0)) for p in left]
         + [pl.BlockSpec((1, step) + p.shape[2:], lambda k: (tile, k, 0, 0)) for p in parts],
         out_specs=[whole(s) for s in shapes],
         scratch_shapes=[
@@ -349,7 +362,7 @@
         compiler_params=pltpu.CompilerParams(vmem_limit_bytes=48 * MIB),
         cost_estimate=pl.CostEstimate(flops=16_000_000_000, bytes_accessed=20_000_000, transcendentals=0),
         name="gram",
-    )(live, first, table, left, *parts)
+    )(live, first, table, *left, *parts)
 
 
 def final_kernel(near, low, high, out, later, earlier):
@@ -433,25 +446,24 @@
 
     barrier = lax.optimization_barrier
     step = CHUNKS[0]
-    x_0, later = barrier((records[:step], records))
-    x_1 = later[step:]
+    x_0, x_1 = records[:step], records[step:]
 
     def whitened(c, *pieces):
-        return whiten_bins(right, odd, table, [records, b0], pieces, c * step)
-
-    a1_0, b0 = one_chip(x_0), swap(records)
-    x_1, a1_0 = barrier((x_1, a1_0))
-    a1_1 = one_chip(x_1)
+        return whiten_bins(right, odd, table, [records, b0], pieces, c)
+
+    a1_0, a1_1, b0 = one_chip(x_0), one_chip(x_1), swap(records)
+    left_own = left_bins(odd, table, [records])
+    a1_0, left_own = barrier((a1_0, left_own))
     a2_0, b1_0 = one_chip(a1_0), swap(a1_0)
+    a2_1, b1_1 = one_chip(a1_1), swap(a1_1)
     b2_0, o5_0 = swap(a2_0), first_half(a2_0, 1)
     part_0 = whitened(0, a1_0, b1_0, a2_0, b2_0, o5_0)
-    a1_1, part_0 = barrier((a1_1, part_0))
-    a2_1, b1_1 = one_chip(a1_1), swap(a1_1)
-    left = left_bins(odd, table, records, b0, [b1_0, b1_1])
-    a2_1, left = barrier((a2_1, left))
+    a2_1, b1_1, part_0 = barrier((a2_1, b1_1, part_0))
     b2_1, o5_1 = swap(a2_1), first_half(a2_1, 1)
+    left_next = left_bins(odd, table, [b0, b1_0, b1_1])
     part_1 = whitened(1, a1_1, b1_1, a2_1, b2_1, o5_1)
 
+    left = [left_own, left_next]
     parts = [part_0, part_1]
     plus, minus = gram(0, live, first_lanes, backward, left, parts, (4, 4), jnp.bfloat16)
     keep, other, own = gram(1, live, first_lanes, backward, left, parts, (2, 2, 4), jnp.float32)

time: 157 us -> 143 us (0.911)
  waiting for transfers between devices: 41.3 us -> 24.8 us
  local copies, waits for them, and re-layouts: 8.15 us -> 10.4 us
  Pallas kernels: 70 us -> 68.1 us
  starting transfers between devices: 33.5 us -> 35.3 us
    ppermute x15, waiting for transfers between devices: 41.3 us -> 24.8 us  [moved(): return lax.ppermute(block, axis, [(i, to(i) % size) for i in range(size)])]
    pallas_call x3 -> x4, Pallas kernels: 37.6 us -> 35.8 us  [the longest x2 25.2 us: whiten_bins(): pl.pallas_call(whiten_kernel, grid=(1,), out_shape=jax.ShapeDtypeStruct(s...]
    ppermute x15, starting transfers between devices: 33.5 us -> 35.3 us  [moved(): return lax.ppermute(block, axis, [(i, to(i) % size) for i in range(size)])]
    slice x2, local copies, waits for them, and re-layouts: 0.04 us -> 1.72 us  [first_half(): return moved(block[:, :BLK], 'chan', lambda i: i - distance)]
    unnamed x35 -> x29, local copies, waits for them, and re-layouts: 5.17 us -> 5.78 us
  transfers between devices with their start and end apart: 15 -> 15, of which waited for: 7 -> 4; matrix products, arithmetic and copies ran while one was open for 4% -> 3% of each run, Pallas kernels for 22% -> 27%
where the time goes in v5:
time: 143 us; the launch traced here: 141 us
  Pallas kernels  68.1 us (48%)
  starting transfers between devices  35.3 us (25%)
  waiting for transfers between devices  24.8 us (17%)
  local copies, waits for them, and re-layouts  10.4 us (7%)
  other arithmetic  1.82 us (1%)
    ppermute x15, starting transfers between devices, moved(): return lax.ppermute(block, axis, [(i, to(i) % size) for i in range(size)])  35.3 us
    pallas_call x2, Pallas kernels, gram(): pl.pallas_call(functools.partial(gram_kernel, tile), grid=(BINS // step,)...  28.8 us
    pallas_call x2, Pallas kernels, whiten_bins(): pl.pallas_call(whiten_kernel, grid=(1,), out_shape=jax.ShapeDtypeStruct(s...  25.2 us
    ppermute x15, waiting for transfers between devices, moved(): return lax.ppermute(block, axis, [(i, to(i) % size) for i in range(size)])  24.8 us
    pallas_call x2, Pallas kernels, left_bins(): pl.pallas_call(left_kernel, out_shape=jax.ShapeDtypeStruct(shape, jnp.bfl...  10.5 us
    unnamed x29, local copies, waits for them, and re-layouts  5.78 us
    pallas_call x1, Pallas kernels, final(): pl.pallas_call(final_kernel, out_shape=jax.ShapeDtypeStruct((LAGS, 4, 256...  3.51 us
  transfers between devices with their start and end apart: 15, of which 4 were waited for; matrix products, arithmetic and copies ran while one was open for 3% of the time, Pallas kernels for 27%

profile of v5, /device:TPU:0, one launch (start us, length us, event | category | flops | bytes accessed | tf_op | source)
XLA Modules:
  0.0 141.3 jit_solution(15658299666220687595)
XLA Ops:
  0.0 2.2 %fusion.6 = (bf16[32,32,256]{2,1,0:T(8,128)(2,1)}, bf16[32,32,256]{2,1,0:T(8,128)(2,1)S(1)}) fusion(bf16[64,32,256]{2,1,0:T(8,128)(2,1)} %x0.3), kind=kLoop, calls=%fused_computation.18 | loop fusion | bytes 2097152 | tf_op jit(solution)/shard_map/slice | solution.py:449
  2.2 6.3 %collective-permute-start = (bf16[32,32,256]{2,1,0:T(8,128)(2,1)S(1)}, bf16[32,32,256]{2,1,0:T(8,128)(2,1)S(1)}, u32[]{:S(2)}, u32[]{:S(2)}) collective-permute-start(bf16[32,32,256]{2,1,0:T(8,128)(2,1)S(1)} %get-tuple-element.30), channel_id=1, source_target_pairs={{0,62},{1,63},{2,0},{3,1},{4,2},{5,3},{6,4},{7,5},{8,6},{9,7},{10,... | collective-permute-start | bytes 1572872 | tf_op jit(solution)/shard_map/ppermute | solution.py:416
  8.5 0.0 copy-done.4
  8.5 0.0 copy-done
  8.5 0.0 copy-start.10
  8.5 4.1 %left.2.own_ref = bf16[256,64,128]{2,1,0:T(8,128)(2,1)S(1)} custom-call(s32[1]{0:T(128)} %bitcast.1.odd_ref, bf16[512,256]{1,0:T(8,128)(2,1)S(1)} %copy-done.4, bf16[64,32,256]{2,1,0:T(8,128)(2,1)S(1)} %copy-done), custom_call_target="tpu_custom_call" | custom-call | flops 4000000000 | bytes 8000000 | tf_op jit(solution)/shard_map/left/pallas_call | solution.py:240
  12.7 0.0 copy-start.6
  12.7 1.9 %copy-done.6 = bf16[256,64,128]{2,1,0:T(8,128)(2,1)} copy-done((bf16[256,64,128]{2,1,0:T(8,128)(2,1)}, bf16[256,64,128]{2,1,0:T(8,128)(2,1)S(1)}, u32[]{:S(2)}) %copy-start.6) | copy-done | bytes 4194328
  14.6 5.1 %collective-permute-done.a1 = bf16[32,32,256]{2,1,0:T(8,128)(2,1)S(1)} collective-permute-done((bf16[32,32,256]{2,1,0:T(8,128)(2,1)S(1)}, bf16[32,32,256]{2,1,0:T(8,128)(2,1)S(1)}, u32[]{:S(2)}, u32[]{:S(2)}) %collective-permute-start) | collective-permute-done | bytes 524320 | tf_op jit(solution)/shard_map/ppermute | solution.py:416
  19.7 5.8 %collective-permute-start.6 = (bf16[32,32,256]{2,1,0:T(8,128)(2,1)S(1)}, bf16[32,32,256]{2,1,0:T(8,128)(2,1)}, u32[]{:S(2)}, u32[]{:S(2)}) collective-permute-start(bf16[32,32,256]{2,1,0:T(8,128)(2,1)S(1)} %collective-permute-done.a1), channel_id=1, source_target_pairs={{0,62},{1,63},{2,0},{3,1},{4,2},{5,3},{6,4},{7,5},{8,6},{9,7},{10,... | collective-permute-start | bytes 1572872 | tf_op jit(solution)/shard_map/ppermute | solution.py:416
  25.5 0.0 collective-permute-start.1
  25.5 0.0 collective-permute-start.3
  25.5 0.5 collective-permute-start.2
  26.0 11.9 %collective-permute-done.6.a2 = bf16[32,32,256]{2,1,0:T(8,128)(2,1)} collective-permute-done((bf16[32,32,256]{2,1,0:T(8,128)(2,1)S(1)}, bf16[32,32,256]{2,1,0:T(8,128)(2,1)}, u32[]{:S(2)}, u32[]{:S(2)}) %collective-permute-start.6) | collective-permute-done | bytes 524320 | tf_op jit(solution)/shard_map/ppermute | solution.py:416
  37.8 0.0 collective-permute-start.7
  37.9 0.0 copy-done.11
  37.9 0.0 copy-done.12
  38.5 0.1 copy.9
  38.6 0.6 gather_fusion
  39.2 1.7 %slice.44 = bf16[32,16,256]{2,1,0:T(8,128)(2,1)} slice(bf16[32,32,256]{2,1,0:T(8,128)(2,1)} %collective-permute-done.6.a2), slice={[0:32], [0:16], [0:256]} | slice | bytes 524288 | tf_op jit(solution)/shard_map/slice | solution.py:428
  40.9 6.0 %collective-permute-start.8 = (bf16[32,16,256]{2,1,0:T(8,128)(2,1)}, bf16[32,16,256]{2,1,0:T(8,128)(2,1)S(1)}, u32[]{:S(2)}, u32[]{:S(2)}) collective-permute-start(bf16[32,16,256]{2,1,0:T(8,128)(2,1)} %slice.44), channel_id=1, source_target_pairs={{0,63},{1,0},{2,1},{3,2},{4,3},{5,4},{6,5},{7,6},{8,7},{9,8},{10,9... | collective-permute-start | bytes 786440 | tf_op jit(solution)/shard_map/ppermute | solution.py:416
  46.9 0.2 fusion
  47.1 0.1 broadcast_in_dim.10
  47.2 0.1 broadcast_in_dim_reshape.3.first_ref
  47.2 0.0 collective-permute-done.3.a1
  47.3 0.1 collective-permute-start.5
  47.4 0.0 collective-permute-done.1.b0.refs_0_
  47.4 0.0 copy-start.1
  47.4 5.5 %collective-permute-start.4 = (bf16[32,32,256]{2,1,0:T(8,128)(2,1)S(1)}, bf16[32,32,256]{2,1,0:T(8,128)(2,1)S(1)}, u32[]{:S(2)}, u32[]{:S(2)}) collective-permute-start(bf16[32,32,256]{2,1,0:T(8,128)(2,1)S(1)} %collective-permute-done.3.a1), channel_id=1, source_target_pairs={{0,62},{1,63},{2,0},{3,1},{4,2},{5,3},{6,4},{7,5},{8,6},{9,7},{10,... | collective-permute-start | bytes 1572872 | tf_op jit(solution)/shard_map/ppermute | solution.py:416
  52.9 0.0 collective-permute-done.2.b1.refs_1_
  52.9 0.0 collective-permute-done.8.o5
  52.9 0.0 collective-permute-done.7.b2
  52.9 0.0 copy-done.1
  52.9 0.0 copy-start.5
  52.9 0.9 copy-done.5
  53.9 12.7 %whiten.2.refs_0_ = bf16[2,256,64,128]{3,2,1,0:T(8,128)(2,1)} custom-call(s32[16]{0:T(128)S(1)} %get-tuple-element.25.right_ref, s32[1]{0:T(128)} %bitcast.1.odd_ref, bf16[512,256]{1,0:T(8,128)(2,1)S(1)} %copy-done.5, bf16[64,32,256]{2,1,0:T(8,128)(2,1)} %x0.3, bf16[64,32,256]{2,1,0:T(8,128)(2,1)} %copy-done.1, ...), custom_call_target="tpu_custom_call" | custom-call | flops 7680000000 | bytes 8000000 | tf_op jit(solution)/shard_map/whiten/pallas_call | solution.py:140
  66.6 0.0 collective-permute-done.5.refs_2_.b1
  66.6 0.0 collective-permute-done.4.a2
  66.6 0.3 collective-permute-start.9
  66.9 3.8 %collective-permute-start.10 = (bf16[32,16,256]{2,1,0:T(8,128)(2,1)S(1)}, bf16[32,16,256]{2,1,0:T(8,128)(2,1)S(1)}, u32[]{:S(2)}, u32[]{:S(2)}) collective-permute-start(bf16[32,16,256]{2,1,0:T(8,128)(2,1)S(1)} %slice.35), channel_id=1, source_target_pairs={{0,63},{1,0},{2,1},{3,2},{4,3},{5,4},{6,5},{7,6},{8,7},{9,8},{10,9... | collective-permute-start | bytes 786440 | tf_op jit(solution)/shard_map/ppermute | solution.py:416
  70.7 1.2 copy-done.2
  71.9 6.4 %left.3.next_ref = bf16[256,64,128]{2,1,0:T(8,128)(2,1)} custom-call(s32[1]{0:T(128)} %bitcast.1.odd_ref, bf16[512,256]{1,0:T(8,128)(2,1)S(1)} %copy-done.5, bf16[64,32,256]{2,1,0:T(8,128)(2,1)S(1)} %copy-done.2, bf16[32,32,256]{2,1,0:T(8,128)(2,1)} %collective-permute-done.2.b1.refs_1_, bf16[32,32,256]{2,1,0:T(8,128)(2,1)S(1)} %collective-permute-done.5.refs_2_.b1), custom_call_target="tpu_custom_call" | custom-call | flops 4000000000 | bytes 8000000 | tf_op jit(solution)/shard_map/left/pallas_call | solution.py:240
  78.3 0.0 copy-start.3
  78.3 0.0 collective-permute-done.10.o5
  78.3 0.0 collective-permute-done.9.b2
  78.4 0.0 copy-start.13
  78.4 0.8 copy-done.13
  79.2 12.5 %whiten.3.refs_1_ = bf16[2,256,64,128]{3,2,1,0:T(8,128)(2,1)} custom-call(s32[16]{0:T(128)S(1)} %get-tuple-element.25.right_ref, s32[1]{0:T(128)} %bitcast.1.odd_ref, bf16[512,256]{1,0:T(8,128)(2,1)S(1)} %copy-done.5, bf16[64,32,256]{2,1,0:T(8,128)(2,1)} %x0.3, bf16[64,32,256]{2,1,0:T(8,128)(2,1)} %copy-done.1, ...), custom_call_target="tpu_custom_call" | custom-call | flops 7680000000 | bytes 8000000 | tf_op jit(solution)/shard_map/whiten/pallas_call | solution.py:140
  91.7 13.5 %gram.3 = (bf16[4,416,256]{2,1,0:T(8,128)(2,1)S(1)}, bf16[4,416,256]{2,1,0:T(8,128)(2,1)S(1)}) custom-call(s32[16]{0:T(128)S(1)} %compare_convert_fusion.live_ref, s32[1,256]{1,0:T(1,128)S(1)} %broadcast_in_dim_reshape.3.first_ref, bf16[2,416,256]{2,1,0:T(8,128)(2,1)S(1)} %copy-done.3, bf16[256,64,128]{2,1,0:T(8,128)(2,1)} %copy-done.6, ...), custom_call_target="tpu_custom_call" | custom-call | flops 16000000000 | bytes 20000000 | tf_op jit(solution)/shard_map/gram/pallas_call | solution.py:346
  105.2 3.3 %collective-permute-start.11 = (bf16[4,416,256]{2,1,0:T(8,128)(2,1)S(1)}, bf16[4,416,256]{2,1,0:T(8,128)(2,1)S(1)}, u32[]{:S(2)}, u32[]{:S(2)}) collective-permute-start(bf16[4,416,256]{2,1,0:T(8,128)(2,1)S(1)} %get-tuple-element.21), channel_id=1, source_target_pairs={{0,192},{64,0},{128,64},{192,128},{1,193},{65,1},{129,65},{193,129... | collective-permute-start | bytes 2555912 | tf_op jit(solution)/shard_map/ppermute | solution.py:416
  108.5 0.0 collective-permute-start.12
  108.5 15.3 %gram.2 = (f32[2,416,256]{2,1,0:T(8,128)S(1)}, f32[2,416,256]{2,1,0:T(8,128)S(1)}, f32[4,416,256]{2,1,0:T(8,128)S(1)}) custom-call(s32[16]{0:T(128)S(1)} %compare_convert_fusion.live_ref, s32[1,256]{1,0:T(1,128)S(1)} %broadcast_in_dim_reshape.3.first_ref, bf16[2,416,256]{2,1,0:T(8,128)(2,1)S(1)} %copy-done.3, bf16[256,64,128]{2,1,0:T(8,128)(2,1)} %copy-done.6, ...), custom_call_target="tpu_custom_call" | custom-call | flops 16000000000 | bytes 20000000 | tf_op jit(solution)/shard_map/gram/pallas_call | solution.py:346
  123.8 0.0 collective-permute-done.11
  123.8 0.1 add_convert_fusion
  123.9 3.6 %collective-permute-start.14 = (bf16[2,416,256]{2,1,0:T(8,128)(2,1)S(1)}, bf16[2,416,256]{2,1,0:T(8,128)(2,1)S(1)}, u32[]{:S(2)}, u32[]{:S(2)}) collective-permute-start(bf16[2,416,256]{2,1,0:T(8,128)(2,1)S(1)} %add_convert_fusion), channel_id=1, source_target_pairs={{0,192},{64,0},{128,64},{192,128},{1,193},{65,1},{129,65},{193,129... | collective-permute-start | bytes 1277960 | tf_op jit(solution)/shard_map/ppermute | solution.py:416
  127.5 0.0 collective-permute-done.12
  127.5 0.1 add_convert_fusion.1
  127.6 0.1 collective-permute-start.13
  127.8 1.4 convert_add_fusion.near
  129.2 4.0 %collective-permute-done.14.high = bf16[2,416,256]{2,1,0:T(8,128)(2,1)S(1)} collective-permute-done((bf16[2,416,256]{2,1,0:T(8,128)(2,1)S(1)}, bf16[2,416,256]{2,1,0:T(8,128)(2,1)S(1)}, u32[]{:S(2)}, u32[]{:S(2)}) %collective-permute-start.14) | collective-permute-done | bytes 426016 | tf_op jit(solution)/shard_map/ppermute | solution.py:416
  133.2 3.9 %collective-permute-done.13.low = bf16[2,416,256]{2,1,0:T(8,128)(2,1)S(1)} collective-permute-done((bf16[2,416,256]{2,1,0:T(8,128)(2,1)S(1)}, bf16[2,416,256]{2,1,0:T(8,128)(2,1)S(1)}, u32[]{:S(2)}, u32[]{:S(2)}) %collective-permute-start.13) | collective-permute-done | bytes 426016 | tf_op jit(solution)/shard_map/ppermute | solution.py:416
  137.1 0.0 copy-done.7
  137.1 0.8 copy-done.8
  137.8 3.5 %final.1 = f32[401,4,256]{2,1,0:T(4,128)} custom-call(f32[4,416,256]{2,1,0:T(8,128)} %convert_add_fusion.near, bf16[2,416,256]{2,1,0:T(8,128)(2,1)} %copy-done.8, bf16[2,416,256]{2,1,0:T(8,128)(2,1)} %copy-done.7), custom_call_target="tpu_custom_call" | custom-call | flops 10000000 | bytes 7000000 | tf_op jit(solution)/shard_map/final/pallas_call | solution.py:403
  (18 shorter events, 0.1 us)
Async XLA Ops:
  0.0 8.5 %copy-start.4 = (bf16[512,256]{1,0:T(8,128)(2,1)S(1)}, bf16[512,256]{1,0:T(8,128)(2,1)}, u32[]{:S(2)}) copy-start(bf16[512,256]{1,0:T(8,128)(2,1)} %constant.54.clone.table_ref) | copy-start | bytes 786436
  0.0 8.5 %copy-start = (bf16[64,32,256]{2,1,0:T(8,128)(2,1)S(1)}, bf16[64,32,256]{2,1,0:T(8,128)(2,1)}, u32[]{:S(2)}) copy-start(bf16[64,32,256]{2,1,0:T(8,128)(2,1)} %x0.3) | copy-start | bytes 3145732
  2.2 17.5 %collective-permute-start = (bf16[32,32,256]{2,1,0:T(8,128)(2,1)S(1)}, bf16[32,32,256]{2,1,0:T(8,128)(2,1)S(1)}, u32[]{:S(2)}, u32[]{:S(2)}) collective-permute-start(bf16[32,32,256]{2,1,0:T(8,128)(2,1)S(1)} %get-tuple-element.30), channel_id=1, source_target_pairs={{0,62},{1,63},{2,0},{3,1},{4,2},{5,3},{6,4},{7,5},{8,6},{9,7},{10,... | collective-permute-start | bytes 1572872 | tf_op jit(solution)/shard_map/ppermute | solution.py:416
  8.5 29.4 %copy-start.11 = (s32[16]{0:T(128)S(1)}, s32[16]{0:T(128)}, u32[]{:S(2)}) copy-start(s32[16]{0:T(128)} %constant.53.clone) | copy-start | bytes 196
  8.5 29.4 %copy-start.12 = (s32[16]{0:T(128)S(1)}, s32[16]{0:T(128)}, u32[]{:S(2)}) copy-start(s32[16]{0:T(128)} %constant.52.clone) | copy-start | bytes 196
  8.5 30.0 %copy-start.10 = (s32[16,2]{0,1:T(2,128)S(1)}, s32[16,2]{0,1:T(2,128)}, u32[]{:S(2)}) copy-start(s32[16,2]{0,1:T(2,128)} %param.8) | copy-start | bytes 388
  12.7 1.9 %copy-start.6 = (bf16[256,64,128]{2,1,0:T(8,128)(2,1)}, bf16[256,64,128]{2,1,0:T(8,128)(2,1)S(1)}, u32[]{:S(2)}) copy-start(bf16[256,64,128]{2,1,0:T(8,128)(2,1)S(1)} %left.2.own_ref) | copy-start | bytes 12582916
  19.7 18.2 %collective-permute-start.6 = (bf16[32,32,256]{2,1,0:T(8,128)(2,1)S(1)}, bf16[32,32,256]{2,1,0:T(8,128)(2,1)}, u32[]{:S(2)}, u32[]{:S(2)}) collective-permute-start(bf16[32,32,256]{2,1,0:T(8,128)(2,1)S(1)} %collective-permute-done.a1), channel_id=1, source_target_pairs={{0,62},{1,63},{2,0},{3,1},{4,2},{5,3},{6,4},{7,5},{8,6},{9,7},{10,... | collective-permute-start | bytes 1572872 | tf_op jit(solution)/shard_map/ppermute | solution.py:416
  25.5 21.9 %collective-permute-start.1 = (bf16[64,32,256]{2,1,0:T(8,128)(2,1)S(1)}, bf16[64,32,256]{2,1,0:T(8,128)(2,1)S(1)}, u32[]{:S(2)}, u32[]{:S(2)}) collective-permute-start(bf16[64,32,256]{2,1,0:T(8,128)(2,1)S(1)} %copy-done), channel_id=1, source_target_pairs={{0,1},{1,0},{2,3},{3,2},{4,5},{5,4},{6,7},{7,6},{8,9},{9,8},{10,11... | collective-permute-start | bytes 3145736 | tf_op jit(solution)/shard_map/ppermute | solution.py:416
  25.5 21.8 %collective-permute-start.3 = (bf16[32,32,256]{2,1,0:T(8,128)(2,1)}, bf16[32,32,256]{2,1,0:T(8,128)(2,1)S(1)}, u32[]{:S(2)}, u32[]{:S(2)}) collective-permute-start(bf16[32,32,256]{2,1,0:T(8,128)(2,1)} %get-tuple-element.29), channel_id=1, source_target_pairs={{0,62},{1,63},{2,0},{3,1},{4,2},{5,3},{6,4},{7,5},{8,6},{9,7},{10,... | collective-permute-start | bytes 1572872 | tf_op jit(solution)/shard_map/ppermute | solution.py:416
  25.5 27.4 %collective-permute-start.2 = (bf16[32,32,256]{2,1,0:T(8,128)(2,1)S(1)}, bf16[32,32,256]{2,1,0:T(8,128)(2,1)}, u32[]{:S(2)}, u32[]{:S(2)}) collective-permute-start(bf16[32,32,256]{2,1,0:T(8,128)(2,1)S(1)} %collective-permute-done.a1), channel_id=1, source_target_pairs={{0,1},{1,0},{2,3},{3,2},{4,5},{5,4},{6,7},{7,6},{8,9},{9,8},{10,11... | collective-permute-start | bytes 1572872 | tf_op jit(solution)/shard_map/ppermute | solution.py:416
  37.8 15.1 %collective-permute-start.7 = (bf16[32,32,256]{2,1,0:T(8,128)(2,1)}, bf16[32,32,256]{2,1,0:T(8,128)(2,1)}, u32[]{:S(2)}, u32[]{:S(2)}) collective-permute-start(bf16[32,32,256]{2,1,0:T(8,128)(2,1)} %collective-permute-done.6.a2), channel_id=1, source_target_pairs={{0,1},{1,0},{2,3},{3,2},{4,5},{5,4},{6,7},{7,6},{8,9},{9,8},{10,11... | collective-permute-start | bytes 1572872 | tf_op jit(solution)/shard_map/ppermute | solution.py:416
  40.9 12.0 %collective-permute-start.8 = (bf16[32,16,256]{2,1,0:T(8,128)(2,1)}, bf16[32,16,256]{2,1,0:T(8,128)(2,1)S(1)}, u32[]{:S(2)}, u32[]{:S(2)}) collective-permute-start(bf16[32,16,256]{2,1,0:T(8,128)(2,1)} %slice.44), channel_id=1, source_target_pairs={{0,63},{1,0},{2,1},{3,2},{4,3},{5,4},{6,5},{7,6},{8,7},{9,8},{10,9... | collective-permute-start | bytes 786440 | tf_op jit(solution)/shard_map/ppermute | solution.py:416
  47.3 19.4 %collective-permute-start.5 = (bf16[32,32,256]{2,1,0:T(8,128)(2,1)S(1)}, bf16[32,32,256]{2,1,0:T(8,128)(2,1)S(1)}, u32[]{:S(2)}, u32[]{:S(2)}) collective-permute-start(bf16[32,32,256]{2,1,0:T(8,128)(2,1)S(1)} %collective-permute-done.3.a1), channel_id=1, source_target_pairs={{0,1},{1,0},{2,3},{3,2},{4,5},{5,4},{6,7},{7,6},{8,9},{9,8},{10,11... | collective-permute-start | bytes 1572872 | tf_op jit(solution)/shard_map/ppermute | solution.py:416
  47.4 5.6 %copy-start.1 = (bf16[64,32,256]{2,1,0:T(8,128)(2,1)}, bf16[64,32,256]{2,1,0:T(8,128)(2,1)S(1)}, u32[]{:S(2)}) copy-start(bf16[64,32,256]{2,1,0:T(8,128)(2,1)S(1)} %collective-permute-done.1.b0.refs_0_) | copy-start | bytes 3145732
  47.4 19.2 %collective-permute-start.4 = (bf16[32,32,256]{2,1,0:T(8,128)(2,1)S(1)}, bf16[32,32,256]{2,1,0:T(8,128)(2,1)S(1)}, u32[]{:S(2)}, u32[]{:S(2)}) collective-permute-start(bf16[32,32,256]{2,1,0:T(8,128)(2,1)S(1)} %collective-permute-done.3.a1), channel_id=1, source_target_pairs={{0,62},{1,63},{2,0},{3,1},{4,2},{5,3},{6,4},{7,5},{8,6},{9,7},{10,... | collective-permute-start | bytes 1572872 | tf_op jit(solution)/shard_map/ppermute | solution.py:416
  52.9 1.0 copy-start.5
  66.6 11.7 %copy-start.9 = (bf16[32,32,256]{2,1,0:T(8,128)(2,1)}, bf16[32,32,256]{2,1,0:T(8,128)(2,1)S(1)}, u32[]{:S(2)}) copy-start(bf16[32,32,256]{2,1,0:T(8,128)(2,1)S(1)} %collective-permute-done.4.a2) | copy-start | bytes 1572868
  66.6 11.7 %collective-permute-start.9 = (bf16[32,32,256]{2,1,0:T(8,128)(2,1)S(1)}, bf16[32,32,256]{2,1,0:T(8,128)(2,1)S(1)}, u32[]{:S(2)}, u32[]{:S(2)}) collective-permute-start(bf16[32,32,256]{2,1,0:T(8,128)(2,1)S(1)} %collective-permute-done.4.a2), channel_id=1, source_target_pairs={{0,1},{1,0},{2,3},{3,2},{4,5},{5,4},{6,7},{7,6},{8,9},{9,8},{10,11... | collective-permute-start | bytes 1572872 | tf_op jit(solution)/shard_map/ppermute | solution.py:416
  66.9 11.4 %collective-permute-start.10 = (bf16[32,16,256]{2,1,0:T(8,128)(2,1)S(1)}, bf16[32,16,256]{2,1,0:T(8,128)(2,1)S(1)}, u32[]{:S(2)}, u32[]{:S(2)}) collective-permute-start(bf16[32,16,256]{2,1,0:T(8,128)(2,1)S(1)} %slice.35), channel_id=1, source_target_pairs={{0,63},{1,0},{2,1},{3,2},{4,3},{5,4},{6,5},{7,6},{8,7},{9,8},{10,9... | collective-permute-start | bytes 786440 | tf_op jit(solution)/shard_map/ppermute | solution.py:416
  70.7 1.2 copy-start.2
  78.3 13.4 %copy-start.3 = (bf16[2,416,256]{2,1,0:T(8,128)(2,1)S(1)}, bf16[2,416,256]{2,1,0:T(8,128)(2,1)}, u32[]{:S(2)}) copy-start(bf16[2,416,256]{2,1,0:T(8,128)(2,1)} %constant.55.clone.table_ref) | copy-start | bytes 1277956
  78.4 0.8 copy-start.13
  105.2 18.6 %collective-permute-start.11 = (bf16[4,416,256]{2,1,0:T(8,128)(2,1)S(1)}, bf16[4,416,256]{2,1,0:T(8,128)(2,1)S(1)}, u32[]{:S(2)}, u32[]{:S(2)}) collective-permute-start(bf16[4,416,256]{2,1,0:T(8,128)(2,1)S(1)} %get-tuple-element.21), channel_id=1, source_target_pairs={{0,192},{64,0},{128,64},{192,128},{1,193},{65,1},{129,65},{193,129... | collective-permute-start | bytes 2555912 | tf_op jit(solution)/shard_map/ppermute | solution.py:416
  108.5 19.1 %collective-permute-start.12 = (bf16[4,416,256]{2,1,0:T(8,128)(2,1)S(1)}, bf16[4,416,256]{2,1,0:T(8,128)(2,1)S(1)}, u32[]{:S(2)}, u32[]{:S(2)}) collective-permute-start(bf16[4,416,256]{2,1,0:T(8,128)(2,1)S(1)} %get-tuple-element.22), channel_id=1, source_target_pairs={{0,64},{64,128},{128,192},{192,0},{1,65},{65,129},{129,193},{193,1... | collective-permute-start | bytes 2555912 | tf_op jit(solution)/shard_map/ppermute | solution.py:416
  123.9 9.3 %collective-permute-start.14 = (bf16[2,416,256]{2,1,0:T(8,128)(2,1)S(1)}, bf16[2,416,256]{2,1,0:T(8,128)(2,1)S(1)}, u32[]{:S(2)}, u32[]{:S(2)}) collective-permute-start(bf16[2,416,256]{2,1,0:T(8,128)(2,1)S(1)} %add_convert_fusion), channel_id=1, source_target_pairs={{0,192},{64,0},{128,64},{192,128},{1,193},{65,1},{129,65},{193,129... | collective-permute-start | bytes 1277960 | tf_op jit(solution)/shard_map/ppermute | solution.py:416
  127.6 9.4 %collective-permute-start.13 = (bf16[2,416,256]{2,1,0:T(8,128)(2,1)S(1)}, bf16[2,416,256]{2,1,0:T(8,128)(2,1)S(1)}, u32[]{:S(2)}, u32[]{:S(2)}) collective-permute-start(bf16[2,416,256]{2,1,0:T(8,128)(2,1)S(1)} %add_convert_fusion.1), channel_id=1, source_target_pairs={{0,64},{64,128},{128,192},{192,0},{1,65},{65,129},{129,193},{193,1... | collective-permute-start | bytes 1277960 | tf_op jit(solution)/shard_map/ppermute | solution.py:416
  133.2 3.9 %copy-start.7 = (bf16[2,416,256]{2,1,0:T(8,128)(2,1)}, bf16[2,416,256]{2,1,0:T(8,128)(2,1)S(1)}, u32[]{:S(2)}) copy-start(bf16[2,416,256]{2,1,0:T(8,128)(2,1)S(1)} %collective-permute-done.14.high) | copy-start | bytes 1277956
  137.1 0.8 copy-start.8

commit v6 on v5

--- a/solution.py
+++ b/solution.py
@@ -74,21 +74,36 @@
         whiten(i + 1, spec_b)
 
 
-def whiten_kernel(right_ref, odd_ref, table_ref, x0, b0, a1, b1, a2, b2, o5, out_ref,
-                  band, spec_a, spec_b, bins_ref, packed, sems):
+def whiten_kernel(chunk, right_ref, odd_ref, table_ref, x0, b0, a1, b1, a2, b2, o5, out_ref,
+                  band, spec_a, spec_b, bins_ref, packed, sems, band_sems):
     segs = a1.shape[0]
     depth = 2 * segs
     pitch = depth + 1
     odd = odd_ref[0] == 1
-
-    @pl.loop(0, segs)
-    def _(s):
-        band[s, 0:32, :] = x0[s]
-        band[s, 32:64, :] = jnp.where(odd, b1[s], b0[s])
-        band[s, 64:96, :] = a1[s]
-        band[s, 96:128, :] = jnp.where(odd, b2[s], b1[s])
-        band[s, 128:160, :] = a2[s]
-        band[s, 160:176, :] = o5[s]
+    share = pl.ds(chunk * segs, segs)
+
+    def fetch(source, place, channels=32):
+        return pltpu.make_async_copy(source, band.at[:, pl.ds(32 * place, channels)], band_sems.at[place])
+
+    fetch(x0.at[share], 0).start()
+    fetch(a1, 2).start()
+    fetch(a2, 4).start()
+
+    @pl.when(odd)
+    def _():
+        fetch(b1, 1).start()
+        fetch(b2, 3).start()
+        fetch(o5, 5, BLK).start()
+
+    @pl.when(jnp.logical_not(odd))
+    def _():
+        fetch(b0.at[share], 1).start()
+        fetch(b1, 3).start()
+        fetch(b2.at[:, pl.ds(0, BLK)], 5, BLK).start()
+
+    for place in range(5):
+        fetch(a1, place).wait()
+    fetch(o5, 5, BLK).wait()
 
     starts = [pl.multiple_of(right_ref[q] * BLK, BLK) for q in range(SLOTS)]
 
@@ -134,14 +149,13 @@
 
 def whiten_bins(right, odd, table, whole_pieces, pieces, chunk):
     smem = pl.BlockSpec(memory_space=pltpu.SMEM)
+    anywhere = pl.BlockSpec(memory_space=pl.ANY)
     segs = pieces[0].shape[0]
-    share = pl.BlockSpec((segs, 32, BINS), lambda _: (chunk, 0, 0))
     shape = (2, BINS, 2 * segs, 128)
     return pl.pallas_call(
-        whiten_kernel,
-        grid=(1,),
+        functools.partial(whiten_kernel, chunk),
         out_shape=jax.ShapeDtypeStruct(shape, jnp.bfloat16),
-        in_specs=[smem, smem, whole(table.shape), share, share] + [whole(p.shape) for p in pieces],
+        in_specs=[smem, smem, pl.BlockSpec(memory_space=pltpu.VMEM)] + [anywhere] * (2 + len(pieces)),
         out_specs=pl.BlockSpec(memory_space=pl.ANY),
         scratch_shapes=[
             pltpu.VMEM((segs, BAND, BINS), jnp.bfloat16),
@@ -150,6 +164,7 @@
             pltpu.VMEM((2, BINS * (2 * segs + 1), 128), jnp.float32),
             pltpu.VMEM(shape, jnp.bfloat16),
             pltpu.SemaphoreType.DMA((BINS // GROUP,)),
+            pltpu.SemaphoreType.DMA((6,)),
         ],
         compiler_params=pltpu.CompilerParams(vmem_limit_bytes=52 * MIB),
         cost_estimate=pl.CostEstimate(flops=240_000_000 * segs, bytes_accessed=8_000_000, transcendentals=0),
@@ -365,8 +380,16 @@
     )(live, first, table, *left, *parts)
 
 
-def final_kernel(near, low, high, out, later, earlier):
+def final_kernel(near_any, low_any, high_any, out, near, low, high, later, earlier, sems):
     middle = LAGS // 2
+    copies = [
+        pltpu.make_async_copy(source, target, sems.at[k])
+        for k, (source, target) in enumerate(((near_any, near), (low_any, low), (high_any, high)))
+    ]
+    for copy in copies:
+        copy.start()
+    for copy in copies:
+        copy.wait()
 
     @pl.loop(0, HALF // BLK)
     def _(tile):
@@ -403,9 +426,11 @@
     return pl.pallas_call(
         final_kernel,
         out_shape=jax.ShapeDtypeStruct((LAGS, 4, 256), jnp.float32),
-        in_specs=[vmem] * 3,
+        in_specs=[pl.BlockSpec(memory_space=pl.ANY)] * 3,
         out_specs=vmem,
-        scratch_shapes=[pltpu.VMEM((2, 4 * (HALF + 1), 128), jnp.float32)] * 2,
+        scratch_shapes=[pltpu.VMEM(x.shape, x.dtype) for x in (near, low, high)]
+        + [pltpu.VMEM((2, 4 * (HALF + 1), 128), jnp.float32)] * 2
+        + [pltpu.SemaphoreType.DMA((3,))],
         cost_estimate=pl.CostEstimate(flops=10_000_000, bytes_accessed=7_000_000, transcendentals=0),
         name="final",
     )(near, low, high)
@@ -424,8 +449,12 @@
     return moved(block, "chan", lambda i: i ^ 1)
 
 
-def first_half(block, distance):
-    return moved(block[:, :BLK], "chan", lambda i: i - distance)
+def first_half(block):
+    return moved(block[:, :BLK], "chan", lambda i: i - 1)
+
+
+def one_row(block, step):
+    return moved(block, "tm", lambda i: i + step)
 
 
 def local(records, pair_blocks, pair_counts):
@@ -446,7 +475,8 @@
 
     barrier = lax.optimization_barrier
     step = CHUNKS[0]
-    x_0, x_1 = records[:step], records[step:]
+    x_0, later = barrier((records[:step], records))
+    x_1 = later[step:]
 
     def whitened(c, *pieces):
         return whiten_bins(right, odd, table, [records, b0], pieces, c)
@@ -456,25 +486,26 @@
     a1_0, left_own = barrier((a1_0, left_own))
     a2_0, b1_0 = one_chip(a1_0), swap(a1_0)
     a2_1, b1_1 = one_chip(a1_1), swap(a1_1)
-    b2_0, o5_0 = swap(a2_0), first_half(a2_0, 1)
+    b2_0, o5_0 = swap(a2_0), first_half(a2_0)
     part_0 = whitened(0, a1_0, b1_0, a2_0, b2_0, o5_0)
     a2_1, b1_1, part_0 = barrier((a2_1, b1_1, part_0))
-    b2_1, o5_1 = swap(a2_1), first_half(a2_1, 1)
+    b2_1, o5_1 = swap(a2_1), first_half(a2_1)
     left_next = left_bins(odd, table, [b0, b1_0, b1_1])
     part_1 = whitened(1, a1_1, b1_1, a2_1, b2_1, o5_1)
 
     left = [left_own, left_next]
     parts = [part_0, part_1]
-    plus, minus = gram(0, live, first_lanes, backward, left, parts, (4, 4), jnp.bfloat16)
+    relay_up, plain_up, relay_down, plain_down = gram(
+        0, live, first_lanes, backward, left, parts, (2, 2, 2, 2), jnp.bfloat16
+    )
+    up_in, down_in = one_row(relay_up, 1), one_row(relay_down, -1)
+    plain_below, plain_above = one_row(plain_up, 1), one_row(plain_down, -1)
     keep, other, own = gram(1, live, first_lanes, backward, left, parts, (2, 2, 4), jnp.float32)
 
-    from_below = moved(plus, "tm", lambda i: i + 1)
-    from_above = moved(minus, "tm", lambda i: i - 1)
-    up = (keep + from_below[:2].astype(jnp.float32)).astype(jnp.bfloat16)
-    down = (other + from_above[:2].astype(jnp.float32)).astype(jnp.bfloat16)
-    two_below = moved(up, "tm", lambda i: i + 1)
-    two_above = moved(down, "tm", lambda i: i - 1)
-    near = own + jnp.concatenate([from_above[2:], from_below[2:]], axis=0).astype(jnp.float32)
+    f32 = jnp.float32
+    two_below = one_row((keep + up_in.astype(f32)).astype(jnp.bfloat16), 1)
+    two_above = one_row((other + down_in.astype(f32)).astype(jnp.bfloat16), -1)
+    near = own + jnp.concatenate([plain_above, plain_below], axis=0).astype(f32)
     return jnp.transpose(final(near, two_below, two_above), (1, 0, 2))
 
 

time: 143 us -> 147 us (1.028)
  starting transfers between devices: 35.3 us -> 38.5 us
    ppermute x15 -> x17, starting transfers between devices: 35.3 us -> 38.5 us  [moved(): return lax.ppermute(block, axis, [(i, to(i) % size) for i in range(size)])]
    unnamed x29 -> x27, local copies, waits for them, and re-layouts: 5.78 us -> 6.52 us
    ppermute x15 -> x17, waiting for transfers between devices: 24.8 us -> 25.1 us  [moved(): return lax.ppermute(block, axis, [(i, to(i) % size) for i in range(size)])]
    slice x5 -> x4, local copies, waits for them, and re-layouts: 3.94 us -> 3.94 us  [the longest x1 1.87 us: local(): x_1 = later[step:]]
  transfers between devices with their start and end apart: 15 -> 17, of which waited for: 4 -> 6; matrix products, arithmetic and copies ran while one was open for 3% -> 4% of each run, Pallas kernels for 27% -> 27%
where the time goes in v6:
time: 147 us; the launch traced here: 146 us
  Pallas kernels  68.6 us (47%)
  starting transfers between devices  38.5 us (26%)
  waiting for transfers between devices  25.1 us (17%)
  local copies, waits for them, and re-layouts  11.2 us (8%)
  other arithmetic  1.84 us (1%)
    ppermute x17, starting transfers between devices, moved(): return lax.ppermute(block, axis, [(i, to(i) % size) for i in range(size)])  38.5 us
    pallas_call x2, Pallas kernels, gram(): pl.pallas_call(functools.partial(gram_kernel, tile), grid=(BINS // step,)...  28.8 us
    pallas_call x2, Pallas kernels, whiten_bins(): pl.pallas_call(functools.partial(whiten_kernel, chunk), out_shape=jax.Sha...  25.5 us
    ppermute x17, waiting for transfers between devices, moved(): return lax.ppermute(block, axis, [(i, to(i) % size) for i in range(size)])  25.1 us
    pallas_call x2, Pallas kernels, left_bins(): pl.pallas_call(left_kernel, out_shape=jax.ShapeDtypeStruct(shape, jnp.bfl...  10.8 us
    unnamed x27, local copies, waits for them, and re-layouts  6.52 us
    pallas_call x1, Pallas kernels, final(): pl.pallas_call(final_kernel, out_shape=jax.ShapeDtypeStruct((LAGS, 4, 256...  3.54 us
  transfers between devices with their start and end apart: 17, of which 6 were waited for; matrix products, arithmetic and copies ran while one was open for 4% of the time, Pallas kernels for 27%

profile of v6, /device:TPU:0, one launch (start us, length us, event | category | flops | bytes accessed | tf_op | source)
XLA Modules:
  0.0 146.3 jit_solution(17254472377677463845)
XLA Ops:
  0.0 1.1 slice.19
  1.1 6.4 %collective-permute-start = (bf16[32,32,256]{2,1,0:T(8,128)(2,1)S(1)}, bf16[32,32,256]{2,1,0:T(8,128)(2,1)S(1)}, u32[]{:S(2)}, u32[]{:S(2)}) collective-permute-start(bf16[32,32,256]{2,1,0:T(8,128)(2,1)S(1)} %slice.19), channel_id=1, source_target_pairs={{0,62},{1,63},{2,0},{3,1},{4,2},{5,3},{6,4},{7,5},{8,6},{9,7},{10,... | collective-permute-start | bytes 1572872 | tf_op jit(solution)/shard_map/ppermute | solution.py:441
  7.5 0.9 copy-done.3
  8.4 5.5 %left.2.own_ref = bf16[256,64,128]{2,1,0:T(8,128)(2,1)S(1)} custom-call(s32[1]{0:T(128)} %bitcast.1.odd_ref, bf16[512,256]{1,0:T(8,128)(2,1)S(1)} %copy-done.3, bf16[64,32,256]{2,1,0:T(8,128)(2,1)} %x0.3), custom_call_target="tpu_custom_call" | custom-call | flops 4000000000 | bytes 8000000 | tf_op jit(solution)/shard_map/left/pallas_call | solution.py:255
  13.9 0.0 copy-start.5
  13.9 1.9 %copy-done.5 = bf16[256,64,128]{2,1,0:T(8,128)(2,1)} copy-done((bf16[256,64,128]{2,1,0:T(8,128)(2,1)}, bf16[256,64,128]{2,1,0:T(8,128)(2,1)S(1)}, u32[]{:S(2)}) %copy-start.5) | copy-done | bytes 4194328
  15.8 2.8 %collective-permute-done.a1 = bf16[32,32,256]{2,1,0:T(8,128)(2,1)S(1)} collective-permute-done((bf16[32,32,256]{2,1,0:T(8,128)(2,1)S(1)}, bf16[32,32,256]{2,1,0:T(8,128)(2,1)S(1)}, u32[]{:S(2)}, u32[]{:S(2)}) %collective-permute-start) | collective-permute-done | bytes 524320 | tf_op jit(solution)/shard_map/ppermute | solution.py:441
  18.7 5.8 %collective-permute-start.6 = (bf16[32,32,256]{2,1,0:T(8,128)(2,1)S(1)}, bf16[32,32,256]{2,1,0:T(8,128)(2,1)}, u32[]{:S(2)}, u32[]{:S(2)}) collective-permute-start(bf16[32,32,256]{2,1,0:T(8,128)(2,1)S(1)} %collective-permute-done.a1), channel_id=1, source_target_pairs={{0,62},{1,63},{2,0},{3,1},{4,2},{5,3},{6,4},{7,5},{8,6},{9,7},{10,... | collective-permute-start | bytes 1572872 | tf_op jit(solution)/shard_map/ppermute | solution.py:441
  24.5 0.0 collective-permute-start.1
  24.5 1.9 %slice.20 = bf16[32,32,256]{2,1,0:T(8,128)(2,1)} slice(bf16[64,32,256]{2,1,0:T(8,128)(2,1)} %x0.3), slice={[32:64], [0:32], [0:256]} | slice | bytes 1048576 | tf_op jit(solution)/shard_map/slice | solution.py:479
  26.3 0.0 collective-permute-start.3
  26.3 0.5 collective-permute-start.2
  26.8 10.0 %collective-permute-done.6.a2 = bf16[32,32,256]{2,1,0:T(8,128)(2,1)} collective-permute-done((bf16[32,32,256]{2,1,0:T(8,128)(2,1)S(1)}, bf16[32,32,256]{2,1,0:T(8,128)(2,1)}, u32[]{:S(2)}, u32[]{:S(2)}) %collective-permute-start.6) | collective-permute-done | bytes 524320 | tf_op jit(solution)/shard_map/ppermute | solution.py:441
  36.8 0.0 collective-permute-start.7
  36.8 0.0 copy-done.10
  36.8 0.0 copy-done.11
  37.5 0.0 copy-done.9
  37.5 0.1 copy.9
  37.6 0.6 gather_fusion
  38.2 1.0 slice.28
  39.2 6.1 %collective-permute-start.8 = (bf16[32,16,256]{2,1,0:T(8,128)(2,1)S(1)}, bf16[32,16,256]{2,1,0:T(8,128)(2,1)S(1)}, u32[]{:S(2)}, u32[]{:S(2)}) collective-permute-start(bf16[32,16,256]{2,1,0:T(8,128)(2,1)S(1)} %slice.28), channel_id=1, source_target_pairs={{0,63},{1,0},{2,1},{3,2},{4,3},{5,4},{6,5},{7,6},{8,7},{9,8},{10,9... | collective-permute-start | bytes 786440 | tf_op jit(solution)/shard_map/ppermute | solution.py:441
  45.2 0.2 fusion
  45.4 0.1 broadcast_in_dim.10
  45.5 0.1 broadcast_in_dim_reshape.3.first_ref
  45.6 0.5 collective-permute-done.3.a1
  46.1 0.0 collective-permute-start.5
  46.1 0.0 collective-permute-done.1.b0.refs_0_
  46.1 5.8 %collective-permute-start.4 = (bf16[32,32,256]{2,1,0:T(8,128)(2,1)S(1)}, bf16[32,32,256]{2,1,0:T(8,128)(2,1)S(1)}, u32[]{:S(2)}, u32[]{:S(2)}) collective-permute-start(bf16[32,32,256]{2,1,0:T(8,128)(2,1)S(1)} %collective-permute-done.3.a1), channel_id=1, source_target_pairs={{0,62},{1,63},{2,0},{3,1},{4,2},{5,3},{6,4},{7,5},{8,6},{9,7},{10,... | collective-permute-start | bytes 1572872 | tf_op jit(solution)/shard_map/ppermute | solution.py:441
  51.9 0.0 collective-permute-done.2.b1.refs_1_
  51.9 0.0 collective-permute-done.8.o5
  51.9 0.0 collective-permute-done.7.b2
  51.9 0.0 copy-done
  51.9 12.8 %whiten.2.refs_0_ = bf16[2,256,64,128]{3,2,1,0:T(8,128)(2,1)} custom-call(s32[16]{0:T(128)S(1)} %get-tuple-element.33.right_ref, s32[1]{0:T(128)} %bitcast.1.odd_ref, bf16[512,256]{1,0:T(8,128)(2,1)S(1)} %copy-done.4, bf16[64,32,256]{2,1,0:T(8,128)(2,1)} %x0.3, bf16[64,32,256]{2,1,0:T(8,128)(2,1)} %copy-done, ...), custom_call_target="tpu_custom_call" | custom-call | flops 7680000000 | bytes 8000000 | tf_op jit(solution)/shard_map/whiten/pallas_call | solution.py:155
  64.7 0.0 collective-permute-done.5.refs_2_.b1
  64.7 0.0 collective-permute-done.4.a2
  64.8 0.2 collective-permute-start.9
  65.0 4.7 %collective-permute-start.10 = (bf16[32,16,256]{2,1,0:T(8,128)(2,1)S(1)}, bf16[32,16,256]{2,1,0:T(8,128)(2,1)S(1)}, u32[]{:S(2)}, u32[]{:S(2)}) collective-permute-start(bf16[32,16,256]{2,1,0:T(8,128)(2,1)S(1)} %slice.23), channel_id=1, source_target_pairs={{0,63},{1,0},{2,1},{3,2},{4,3},{5,4},{6,5},{7,6},{8,7},{9,8},{10,9... | collective-permute-start | bytes 786440 | tf_op jit(solution)/shard_map/ppermute | solution.py:441
  69.7 1.2 copy-done.1
  70.9 5.3 %left.3.next_ref = bf16[256,64,128]{2,1,0:T(8,128)(2,1)} custom-call(s32[1]{0:T(128)} %bitcast.1.odd_ref, bf16[512,256]{1,0:T(8,128)(2,1)S(1)} %copy-done.4, bf16[64,32,256]{2,1,0:T(8,128)(2,1)S(1)} %copy-done.1, bf16[32,32,256]{2,1,0:T(8,128)(2,1)S(1)} %collective-permute-done.2.b1.refs_1_, bf16[32,32,256]{2,1,0:T(8,128)(2,1)S(1)} %collective-permute-done.5.refs_2_.b1), custom_call_target="tpu_custom_call" | custom-call | flops 4000000000 | bytes 8000000 | tf_op jit(solution)/shard_map/left/pallas_call | solution.py:255
  76.3 0.0 copy-start.2
  76.3 0.0 collective-permute-done.10.o5
  76.3 0.0 collective-permute-done.9.b2
  76.3 0.8 copy-done.12
  77.1 12.7 %whiten.3.refs_1_ = bf16[2,256,64,128]{3,2,1,0:T(8,128)(2,1)} custom-call(s32[16]{0:T(128)S(1)} %get-tuple-element.33.right_ref, s32[1]{0:T(128)} %bitcast.1.odd_ref, bf16[512,256]{1,0:T(8,128)(2,1)S(1)} %copy-done.4, bf16[64,32,256]{2,1,0:T(8,128)(2,1)} %x0.3, bf16[64,32,256]{2,1,0:T(8,128)(2,1)} %copy-done, ...), custom_call_target="tpu_custom_call" | custom-call | flops 7680000000 | bytes 8000000 | tf_op jit(solution)/shard_map/whiten/pallas_call | solution.py:155
  89.9 13.5 %gram.3 = (bf16[2,416,256]{2,1,0:T(8,128)(2,1)S(1)}, bf16[2,416,256]{2,1,0:T(8,128)(2,1)S(1)}, bf16[2,416,256]{2,1,0:T(8,128)(2,1)S(1)}, bf16[2,416,256]{2,1,0:T(8,128)(2,1)S(1)}) custom-call(s32[16]{0:T(128)S(1)} %compare_convert_fusion.live_ref, s32[1,256]{1,0:T(1,128)S(1)} %broadcast_in_dim_reshape.3.first_ref, bf16[2,416,256]{2,1,0:T(8,128)(2,1)S(1)} %copy-done.2, ...), custom_call_target="tpu_custom_call" | custom-call | flops 16000000000 | bytes 20000000 | tf_op jit(solution)/shard_map/gram/pallas_call | solution.py:361
  103.4 1.8 %collective-permute-start.13 = (bf16[2,416,256]{2,1,0:T(8,128)(2,1)S(1)}, bf16[2,416,256]{2,1,0:T(8,128)(2,1)S(1)}, u32[]{:S(2)}, u32[]{:S(2)}) collective-permute-start(bf16[2,416,256]{2,1,0:T(8,128)(2,1)S(1)} %get-tuple-element.30), channel_id=1, source_target_pairs={{0,64},{64,128},{128,192},{192,0},{1,65},{65,129},{129,193},{193,1... | collective-permute-start | bytes 1277960 | tf_op jit(solution)/shard_map/ppermute | solution.py:441
  105.2 1.7 %collective-permute-start.15 = (bf16[2,416,256]{2,1,0:T(8,128)(2,1)S(1)}, bf16[2,416,256]{2,1,0:T(8,128)(2,1)S(1)}, u32[]{:S(2)}, u32[]{:S(2)}) collective-permute-start(bf16[2,416,256]{2,1,0:T(8,128)(2,1)S(1)} %get-tuple-element.32), channel_id=1, source_target_pairs={{0,192},{64,0},{128,64},{192,128},{1,193},{65,1},{129,65},{193,129... | collective-permute-start | bytes 1277960 | tf_op jit(solution)/shard_map/ppermute | solution.py:441
  106.9 15.3 %gram.2 = (f32[2,416,256]{2,1,0:T(8,128)S(1)}, f32[2,416,256]{2,1,0:T(8,128)S(1)}, f32[4,416,256]{2,1,0:T(8,128)S(1)}) custom-call(s32[16]{0:T(128)S(1)} %compare_convert_fusion.live_ref, s32[1,256]{1,0:T(1,128)S(1)} %broadcast_in_dim_reshape.3.first_ref, bf16[2,416,256]{2,1,0:T(8,128)(2,1)S(1)} %copy-done.2, bf16[256,64,128]{2,1,0:T(8,128)(2,1)} %copy-done.5, ...), custom_call_target="tpu_custom_call" | custom-call | flops 16000000000 | bytes 20000000 | tf_op jit(solution)/shard_map/gram/pallas_call | solution.py:361
  122.2 1.9 %collective-permute-start.11 = (bf16[2,416,256]{2,1,0:T(8,128)(2,1)S(1)}, bf16[2,416,256]{2,1,0:T(8,128)(2,1)S(1)}, u32[]{:S(2)}, u32[]{:S(2)}) collective-permute-start(bf16[2,416,256]{2,1,0:T(8,128)(2,1)S(1)} %get-tuple-element.27), channel_id=1, source_target_pairs={{0,192},{64,0},{128,64},{192,128},{1,193},{65,1},{129,65},{193,129... | collective-permute-start | bytes 1277960 | tf_op jit(solution)/shard_map/ppermute | solution.py:441
  124.0 0.2 collective-permute-start.12
  124.3 0.0 collective-permute-done.13
  124.3 0.1 add_convert_fusion.1
  124.4 0.4 collective-permute-start.14
  124.8 0.0 collective-permute-done.15
  124.8 0.1 add_convert_fusion
  124.9 3.0 %collective-permute-start.16 = (bf16[2,416,256]{2,1,0:T(8,128)(2,1)S(1)}, bf16[2,416,256]{2,1,0:T(8,128)(2,1)S(1)}, u32[]{:S(2)}, u32[]{:S(2)}) collective-permute-start(bf16[2,416,256]{2,1,0:T(8,128)(2,1)S(1)} %add_convert_fusion), channel_id=1, source_target_pairs={{0,192},{64,0},{128,64},{192,128},{1,193},{65,1},{129,65},{193,129... | collective-permute-start | bytes 1277960 | tf_op jit(solution)/shard_map/ppermute | solution.py:441
  127.9 6.0 %collective-permute-done.11 = bf16[2,416,256]{2,1,0:T(8,128)(2,1)S(1)} collective-permute-done((bf16[2,416,256]{2,1,0:T(8,128)(2,1)S(1)}, bf16[2,416,256]{2,1,0:T(8,128)(2,1)S(1)}, u32[]{:S(2)}, u32[]{:S(2)}) %collective-permute-start.11) | collective-permute-done | bytes 426016 | tf_op jit(solution)/shard_map/ppermute | solution.py:441
  133.9 2.6 %collective-permute-done.12 = bf16[2,416,256]{2,1,0:T(8,128)(2,1)S(1)} collective-permute-done((bf16[2,416,256]{2,1,0:T(8,128)(2,1)S(1)}, bf16[2,416,256]{2,1,0:T(8,128)(2,1)S(1)}, u32[]{:S(2)}, u32[]{:S(2)}) %collective-permute-start.12) | collective-permute-done | bytes 426016 | tf_op jit(solution)/shard_map/ppermute | solution.py:441
  136.5 1.4 convert_add_fusion.near_any
  137.9 3.2 %collective-permute-done.14.low_any = bf16[2,416,256]{2,1,0:T(8,128)(2,1)S(1)} collective-permute-done((bf16[2,416,256]{2,1,0:T(8,128)(2,1)S(1)}, bf16[2,416,256]{2,1,0:T(8,128)(2,1)S(1)}, u32[]{:S(2)}, u32[]{:S(2)}) %collective-permute-start.14) | collective-permute-done | bytes 426016 | tf_op jit(solution)/shard_map/ppermute | solution.py:441
  141.1 0.0 collective-permute-done.16.high_any
  141.1 0.8 copy-done.6
  141.8 0.8 copy-done.7
  142.6 3.5 %final.1 = f32[401,4,256]{2,1,0:T(4,128)} custom-call(f32[4,416,256]{2,1,0:T(8,128)} %convert_add_fusion.near_any, bf16[2,416,256]{2,1,0:T(8,128)(2,1)} %copy-done.6, bf16[2,416,256]{2,1,0:T(8,128)(2,1)} %copy-done.7), custom_call_target="tpu_custom_call" | custom-call | flops 10000000 | bytes 7000000 | tf_op jit(solution)/shard_map/final/pallas_call | solution.py:426
  (19 shorter events, 0.1 us)
Async XLA Ops:
  1.1 17.6 %collective-permute-start = (bf16[32,32,256]{2,1,0:T(8,128)(2,1)S(1)}, bf16[32,32,256]{2,1,0:T(8,128)(2,1)S(1)}, u32[]{:S(2)}, u32[]{:S(2)}) collective-permute-start(bf16[32,32,256]{2,1,0:T(8,128)(2,1)S(1)} %slice.19), channel_id=1, source_target_pairs={{0,62},{1,63},{2,0},{3,1},{4,2},{5,3},{6,4},{7,5},{8,6},{9,7},{10,... | collective-permute-start | bytes 1572872 | tf_op jit(solution)/shard_map/ppermute | solution.py:441
  7.5 0.9 copy-start.3
  8.4 28.4 %copy-start.10 = (s32[16]{0:T(128)S(1)}, s32[16]{0:T(128)}, u32[]{:S(2)}) copy-start(s32[16]{0:T(128)} %constant.53.clone) | copy-start | bytes 196
  8.4 28.4 %copy-start.11 = (s32[16]{0:T(128)S(1)}, s32[16]{0:T(128)}, u32[]{:S(2)}) copy-start(s32[16]{0:T(128)} %constant.52.clone) | copy-start | bytes 196
  8.4 29.1 %copy-start.9 = (s32[16,2]{0,1:T(2,128)S(1)}, s32[16,2]{0,1:T(2,128)}, u32[]{:S(2)}) copy-start(s32[16,2]{0,1:T(2,128)} %param.8) | copy-start | bytes 388
  13.9 1.9 %copy-start.5 = (bf16[256,64,128]{2,1,0:T(8,128)(2,1)}, bf16[256,64,128]{2,1,0:T(8,128)(2,1)S(1)}, u32[]{:S(2)}) copy-start(bf16[256,64,128]{2,1,0:T(8,128)(2,1)S(1)} %left.2.own_ref) | copy-start | bytes 12582916
  15.8 36.1 %copy-start.4 = (bf16[512,256]{1,0:T(8,128)(2,1)S(1)}, bf16[512,256]{1,0:T(8,128)(2,1)}, u32[]{:S(2)}) copy-start(bf16[512,256]{1,0:T(8,128)(2,1)} %constant.54.clone.table_ref) | copy-start | bytes 786436
  18.7 18.2 %collective-permute-start.6 = (bf16[32,32,256]{2,1,0:T(8,128)(2,1)S(1)}, bf16[32,32,256]{2,1,0:T(8,128)(2,1)}, u32[]{:S(2)}, u32[]{:S(2)}) collective-permute-start(bf16[32,32,256]{2,1,0:T(8,128)(2,1)S(1)} %collective-permute-done.a1), channel_id=1, source_target_pairs={{0,62},{1,63},{2,0},{3,1},{4,2},{5,3},{6,4},{7,5},{8,6},{9,7},{10,... | collective-permute-start | bytes 1572872 | tf_op jit(solution)/shard_map/ppermute | solution.py:441
  24.5 21.7 %collective-permute-start.1 = (bf16[64,32,256]{2,1,0:T(8,128)(2,1)}, bf16[64,32,256]{2,1,0:T(8,128)(2,1)S(1)}, u32[]{:S(2)}, u32[]{:S(2)}) collective-permute-start(bf16[64,32,256]{2,1,0:T(8,128)(2,1)} %x0.3), channel_id=1, source_target_pairs={{0,1},{1,0},{2,3},{3,2},{4,5},{5,4},{6,7},{7,6},{8,9},{9,8},{10,11... | collective-permute-start | bytes 3145736 | tf_op jit(solution)/shard_map/ppermute | solution.py:441
  26.3 19.8 %collective-permute-start.3 = (bf16[32,32,256]{2,1,0:T(8,128)(2,1)}, bf16[32,32,256]{2,1,0:T(8,128)(2,1)S(1)}, u32[]{:S(2)}, u32[]{:S(2)}) collective-permute-start(bf16[32,32,256]{2,1,0:T(8,128)(2,1)} %slice.20), channel_id=1, source_target_pairs={{0,62},{1,63},{2,0},{3,1},{4,2},{5,3},{6,4},{7,5},{8,6},{9,7},{10,... | collective-permute-start | bytes 1572872 | tf_op jit(solution)/shard_map/ppermute | solution.py:441
  26.3 25.6 %collective-permute-start.2 = (bf16[32,32,256]{2,1,0:T(8,128)(2,1)S(1)}, bf16[32,32,256]{2,1,0:T(8,128)(2,1)S(1)}, u32[]{:S(2)}, u32[]{:S(2)}) collective-permute-start(bf16[32,32,256]{2,1,0:T(8,128)(2,1)S(1)} %collective-permute-done.a1), channel_id=1, source_target_pairs={{0,1},{1,0},{2,3},{3,2},{4,5},{5,4},{6,7},{7,6},{8,9},{9,8},{10,11... | collective-permute-start | bytes 1572872 | tf_op jit(solution)/shard_map/ppermute | solution.py:441
  36.8 15.1 %collective-permute-start.7 = (bf16[32,32,256]{2,1,0:T(8,128)(2,1)}, bf16[32,32,256]{2,1,0:T(8,128)(2,1)}, u32[]{:S(2)}, u32[]{:S(2)}) collective-permute-start(bf16[32,32,256]{2,1,0:T(8,128)(2,1)} %collective-permute-done.6.a2), channel_id=1, source_target_pairs={{0,1},{1,0},{2,3},{3,2},{4,5},{5,4},{6,7},{7,6},{8,9},{9,8},{10,11... | collective-permute-start | bytes 1572872 | tf_op jit(solution)/shard_map/ppermute | solution.py:441
  39.2 12.7 %collective-permute-start.8 = (bf16[32,16,256]{2,1,0:T(8,128)(2,1)S(1)}, bf16[32,16,256]{2,1,0:T(8,128)(2,1)S(1)}, u32[]{:S(2)}, u32[]{:S(2)}) collective-permute-start(bf16[32,16,256]{2,1,0:T(8,128)(2,1)S(1)} %slice.28), channel_id=1, source_target_pairs={{0,63},{1,0},{2,1},{3,2},{4,3},{5,4},{6,5},{7,6},{8,7},{9,8},{10,9... | collective-permute-start | bytes 786440 | tf_op jit(solution)/shard_map/ppermute | solution.py:441
  46.1 18.6 %collective-permute-start.5 = (bf16[32,32,256]{2,1,0:T(8,128)(2,1)S(1)}, bf16[32,32,256]{2,1,0:T(8,128)(2,1)S(1)}, u32[]{:S(2)}, u32[]{:S(2)}) collective-permute-start(bf16[32,32,256]{2,1,0:T(8,128)(2,1)S(1)} %collective-permute-done.3.a1), channel_id=1, source_target_pairs={{0,1},{1,0},{2,3},{3,2},{4,5},{5,4},{6,7},{7,6},{8,9},{9,8},{10,11... | collective-permute-start | bytes 1572872 | tf_op jit(solution)/shard_map/ppermute | solution.py:441
  46.1 5.8 %copy-start = (bf16[64,32,256]{2,1,0:T(8,128)(2,1)}, bf16[64,32,256]{2,1,0:T(8,128)(2,1)S(1)}, u32[]{:S(2)}) copy-start(bf16[64,32,256]{2,1,0:T(8,128)(2,1)S(1)} %collective-permute-done.1.b0.refs_0_) | copy-start | bytes 3145732
  46.1 18.6 %collective-permute-start.4 = (bf16[32,32,256]{2,1,0:T(8,128)(2,1)S(1)}, bf16[32,32,256]{2,1,0:T(8,128)(2,1)S(1)}, u32[]{:S(2)}, u32[]{:S(2)}) collective-permute-start(bf16[32,32,256]{2,1,0:T(8,128)(2,1)S(1)} %collective-permute-done.3.a1), channel_id=1, source_target_pairs={{0,62},{1,63},{2,0},{3,1},{4,2},{5,3},{6,4},{7,5},{8,6},{9,7},{10,... | collective-permute-start | bytes 1572872 | tf_op jit(solution)/shard_map/ppermute | solution.py:441
  64.7 11.5 %copy-start.8 = (bf16[32,32,256]{2,1,0:T(8,128)(2,1)}, bf16[32,32,256]{2,1,0:T(8,128)(2,1)S(1)}, u32[]{:S(2)}) copy-start(bf16[32,32,256]{2,1,0:T(8,128)(2,1)S(1)} %collective-permute-done.4.a2) | copy-start | bytes 1572868
  64.8 11.6 %collective-permute-start.9 = (bf16[32,32,256]{2,1,0:T(8,128)(2,1)S(1)}, bf16[32,32,256]{2,1,0:T(8,128)(2,1)S(1)}, u32[]{:S(2)}, u32[]{:S(2)}) collective-permute-start(bf16[32,32,256]{2,1,0:T(8,128)(2,1)S(1)} %collective-permute-done.4.a2), channel_id=1, source_target_pairs={{0,1},{1,0},{2,3},{3,2},{4,5},{5,4},{6,7},{7,6},{8,9},{9,8},{10,11... | collective-permute-start | bytes 1572872 | tf_op jit(solution)/shard_map/ppermute | solution.py:441
  65.0 11.3 %collective-permute-start.10 = (bf16[32,16,256]{2,1,0:T(8,128)(2,1)S(1)}, bf16[32,16,256]{2,1,0:T(8,128)(2,1)S(1)}, u32[]{:S(2)}, u32[]{:S(2)}) collective-permute-start(bf16[32,16,256]{2,1,0:T(8,128)(2,1)S(1)} %slice.23), channel_id=1, source_target_pairs={{0,63},{1,0},{2,1},{3,2},{4,3},{5,4},{6,5},{7,6},{8,7},{9,8},{10,9... | collective-permute-start | bytes 786440 | tf_op jit(solution)/shard_map/ppermute | solution.py:441
  69.7 1.2 copy-start.1
  76.3 13.6 %copy-start.2 = (bf16[2,416,256]{2,1,0:T(8,128)(2,1)S(1)}, bf16[2,416,256]{2,1,0:T(8,128)(2,1)}, u32[]{:S(2)}) copy-start(bf16[2,416,256]{2,1,0:T(8,128)(2,1)} %constant.55.clone.table_ref) | copy-start | bytes 1277956
  76.3 0.8 copy-start.12
  103.4 20.9 %collective-permute-start.13 = (bf16[2,416,256]{2,1,0:T(8,128)(2,1)S(1)}, bf16[2,416,256]{2,1,0:T(8,128)(2,1)S(1)}, u32[]{:S(2)}, u32[]{:S(2)}) collective-permute-start(bf16[2,416,256]{2,1,0:T(8,128)(2,1)S(1)} %get-tuple-element.30), channel_id=1, source_target_pairs={{0,64},{64,128},{128,192},{192,0},{1,65},{65,129},{129,193},{193,1... | collective-permute-start | bytes 1277960 | tf_op jit(solution)/shard_map/ppermute | solution.py:441
  105.2 19.6 %collective-permute-start.15 = (bf16[2,416,256]{2,1,0:T(8,128)(2,1)S(1)}, bf16[2,416,256]{2,1,0:T(8,128)(2,1)S(1)}, u32[]{:S(2)}, u32[]{:S(2)}) collective-permute-start(bf16[2,416,256]{2,1,0:T(8,128)(2,1)S(1)} %get-tuple-element.32), channel_id=1, source_target_pairs={{0,192},{64,0},{128,64},{192,128},{1,193},{65,1},{129,65},{193,129... | collective-permute-start | bytes 1277960 | tf_op jit(solution)/shard_map/ppermute | solution.py:441
  122.2 11.7 %collective-permute-start.11 = (bf16[2,416,256]{2,1,0:T(8,128)(2,1)S(1)}, bf16[2,416,256]{2,1,0:T(8,128)(2,1)S(1)}, u32[]{:S(2)}, u32[]{:S(2)}) collective-permute-start(bf16[2,416,256]{2,1,0:T(8,128)(2,1)S(1)} %get-tuple-element.27), channel_id=1, source_target_pairs={{0,192},{64,0},{128,64},{192,128},{1,193},{65,1},{129,65},{193,129... | collective-permute-start | bytes 1277960 | tf_op jit(solution)/shard_map/ppermute | solution.py:441
  124.0 12.5 %collective-permute-start.12 = (bf16[2,416,256]{2,1,0:T(8,128)(2,1)S(1)}, bf16[2,416,256]{2,1,0:T(8,128)(2,1)S(1)}, u32[]{:S(2)}, u32[]{:S(2)}) collective-permute-start(bf16[2,416,256]{2,1,0:T(8,128)(2,1)S(1)} %get-tuple-element.28), channel_id=1, source_target_pairs={{0,64},{64,128},{128,192},{192,0},{1,65},{65,129},{129,193},{193,1... | collective-permute-start | bytes 1277960 | tf_op jit(solution)/shard_map/ppermute | solution.py:441
  124.4 16.7 %collective-permute-start.14 = (bf16[2,416,256]{2,1,0:T(8,128)(2,1)S(1)}, bf16[2,416,256]{2,1,0:T(8,128)(2,1)S(1)}, u32[]{:S(2)}, u32[]{:S(2)}) collective-permute-start(bf16[2,416,256]{2,1,0:T(8,128)(2,1)S(1)} %add_convert_fusion.1), channel_id=1, source_target_pairs={{0,64},{64,128},{128,192},{192,0},{1,65},{65,129},{129,193},{193,1... | collective-permute-start | bytes 1277960 | tf_op jit(solution)/shard_map/ppermute | solution.py:441
  124.9 16.1 %collective-permute-start.16 = (bf16[2,416,256]{2,1,0:T(8,128)(2,1)S(1)}, bf16[2,416,256]{2,1,0:T(8,128)(2,1)S(1)}, u32[]{:S(2)}, u32[]{:S(2)}) collective-permute-start(bf16[2,416,256]{2,1,0:T(8,128)(2,1)S(1)} %add_convert_fusion), channel_id=1, source_target_pairs={{0,192},{64,0},{128,64},{192,128},{1,193},{65,1},{129,65},{193,129... | collective-permute-start | bytes 1277960 | tf_op jit(solution)/shard_map/ppermute | solution.py:441
  141.1 0.8 copy-start.6
  141.8 0.8 copy-start.7

commit v7 on v6

--- a/solution.py
+++ b/solution.py
@@ -22,6 +22,7 @@
 CHUNKS = (32, 32)
 PITCH = 513
 GROUP = 16
+BLOCK = 32
 
 water_share = 0.1
 tiny_eps = 1e-06
@@ -173,8 +174,17 @@
 
 
 def left_kernel(odd_ref, table_ref, *refs):
-    out_ref, records, spec_a, spec_b, bins_ref, packed, sems = refs[-7:]
-    pieces = refs[:-7]
+    count = (len(refs) - 8) // 2
+    sources, pieces = refs[:count], refs[-count:]
+    out_ref, records, spec_a, spec_b, bins_ref, packed, sems, piece_sems = refs[count:-count]
+    fetches = [
+        pltpu.make_async_copy(source, piece, piece_sems.at[k])
+        for k, (source, piece) in enumerate(zip(sources, pieces))
+    ]
+    for fetch in fetches:
+        fetch.start()
+    for fetch in fetches:
+        fetch.wait()
     odd = odd_ref[0] == 1
     segs = pieces[0].shape[0]
     spread = OWN + 1
@@ -255,7 +265,7 @@
     return pl.pallas_call(
         left_kernel,
         out_shape=jax.ShapeDtypeStruct(shape, jnp.bfloat16),
-        in_specs=[smem] + [vmem] * (1 + len(pieces)),
+        in_specs=[smem, vmem] + [pl.BlockSpec(memory_space=pl.ANY)] * len(pieces),
         out_specs=pl.BlockSpec(memory_space=pl.ANY),
         scratch_shapes=[
             pltpu.VMEM((2, pieces[0].shape[0] * (OWN + 1), 128), jnp.float32),
@@ -264,7 +274,9 @@
             pltpu.VMEM((BINS * (2 * OWN + 1), 128), jnp.float32),
             pltpu.VMEM(shape, jnp.bfloat16),
             pltpu.SemaphoreType.DMA((BINS // GROUP,)),
-        ],
+            pltpu.SemaphoreType.DMA((len(pieces),)),
+        ]
+        + [pltpu.VMEM(p.shape, p.dtype) for p in pieces],
         compiler_params=pltpu.CompilerParams(vmem_limit_bytes=48 * MIB),
         cost_estimate=pl.CostEstimate(flops=4_000_000_000, bytes_accessed=8_000_000, transcendentals=0),
         name="left",
@@ -310,25 +322,39 @@
                     put(k, rows, slice(ha * 128, (ha + 1) * 128), arrays[k])
 
 
-def gram_kernel(tile, live_ref, first_ref, table_ref, own_ref, next_ref, *refs):
-    parts = refs[:len(CHUNKS)]
-    outs = refs[len(CHUNKS):-2]
-    sums, lags = refs[-2:]
-    block = pl.program_id(0)
-    bins = own_ref.shape[0]
+def gram_kernel(tile, live_ref, first_ref, table_ref, *refs):
+    count = 2 + len(CHUNKS)
+    sources, outs = refs[:count], refs[count:-count - 3]
+    sums, lags, sems = refs[-count - 3:-count]
+    own_ref, next_ref, *parts = refs[-count:]
     first = first_ref[...]
     chosen = [jnp.broadcast_to(first == i, (BLK, 128)) for i in range(3)]
 
-    @pl.loop(0, bins // 32)
-    def _(group):
-        for step in range(32):
-            local_bin = group * 32 + step
-            f = block * bins + local_bin
+    def fetches(block):
+        some = pl.ds(block * BLOCK, BLOCK)
+        return [
+            pltpu.make_async_copy(
+                source.at[some] if k < 2 else source.at[tile, some], refs[k - count].at[some], sems.at[k, block]
+            )
+            for k, source in enumerate(sources)
+        ]
+
+    @pl.loop(0, BINS // BLOCK)
+    def _(block):
+        for fetch in fetches(block):
+            fetch.start()
+
+    @pl.loop(0, BINS // BLOCK)
+    def _(block):
+        for fetch in fetches(block):
+            fetch.wait()
+        for step in range(BLOCK):
+            f = block * BLOCK + step
             right = jnp.concatenate(
-                [p[0, local_bin, part * n:(part + 1) * n, :] for part in range(2) for p, n in zip(parts, CHUNKS)],
+                [p[f, part * n:(part + 1) * n, :] for part in range(2) for p, n in zip(parts, CHUNKS)],
                 axis=0,
             )
-            left = jnp.concatenate([own_ref[local_bin], next_ref[local_bin]], axis=0)
+            left = jnp.concatenate([own_ref[f], next_ref[f]], axis=0)
             cross = jnp.dot(left, right, preferred_element_type=jnp.float32)
             for part in range(2):
                 starts = [i // 2 * LEFT + part * OWN + i % 2 * BLK for i in range(4)]
@@ -339,45 +365,39 @@
                 for a in range(0, BLK, 8):
                     sums[pl.ds(a * PITCH + part * BINS + f, 8, stride=PITCH), :] = own[a:a + 8]
 
-    @pl.when(block == pl.num_programs(0) - 1)
-    def _():
-        lag_sums(table_ref, sums, lags)
-        live = [live_ref[8 * tile + q] == 1 for q in range(8)]
-
-        def put(q, rows, lanes, value):
-            value = jnp.where(live[q], value, 0.0)
-            for out in outs:
-                if q < out.shape[0]:
-                    out[q, rows, lanes] = value.astype(out.dtype)
-                    return
-                q -= out.shape[0]
-
-        by_slot(lags, put)
+    lag_sums(table_ref, sums, lags)
+    live = [live_ref[8 * tile + q] == 1 for q in range(8)]
+
+    def put(q, rows, lanes, value):
+        value = jnp.where(live[q], value, 0.0)
+        for out in outs:
+            if q < out.shape[0]:
+                out[q, rows, lanes] = value.astype(out.dtype)
+                return
+            q -= out.shape[0]
+
+    by_slot(lags, put)
 
 
 def gram(tile, live, first, table, left, parts, counts, dtype):
-    step = 32
-    shapes = [(n, ROWS, 256) for n in counts]
+    vmem = pl.BlockSpec(memory_space=pltpu.VMEM)
+    arrays = [*left, *parts]
     return pl.pallas_call(
         functools.partial(gram_kernel, tile),
-        grid=(BINS // step,),
-        out_shape=[jax.ShapeDtypeStruct(s, dtype) for s in shapes],
-        in_specs=[
-            pl.BlockSpec(memory_space=pltpu.SMEM),
-            pl.BlockSpec((1, 128), lambda k: (0, tile)),
-            whole(table.shape),
-        ]
-        + [pl.BlockSpec((step,) + p.shape[1:], lambda k: (k, 0, 0)) for p in left]
-        + [pl.BlockSpec((1, step) + p.shape[2:], lambda k: (tile, k, 0, 0)) for p in parts],
-        out_specs=[whole(s) for s in shapes],
+        out_shape=[jax.ShapeDtypeStruct((n, ROWS, 256), dtype) for n in counts],
+        in_specs=[pl.BlockSpec(memory_space=pltpu.SMEM), vmem, vmem]
+        + [pl.BlockSpec(memory_space=pl.ANY)] * len(arrays),
+        out_specs=[vmem] * len(counts),
         scratch_shapes=[
             pltpu.VMEM((BLK * PITCH, 128), jnp.float32),
             pltpu.VMEM((BLK, ROWS, 128), jnp.float32),
-        ],
+            pltpu.SemaphoreType.DMA((len(arrays), BINS // BLOCK)),
+        ]
+        + [pltpu.VMEM(p.shape[-3:], p.dtype) for p in arrays],
         compiler_params=pltpu.CompilerParams(vmem_limit_bytes=48 * MIB),
         cost_estimate=pl.CostEstimate(flops=16_000_000_000, bytes_accessed=20_000_000, transcendentals=0),
         name="gram",
-    )(live, first, table, *left, *parts)
+    )(live, first[:, tile * 128:(tile + 1) * 128], table, *arrays)
 
 
 def final_kernel(near_any, low_any, high_any, out, near, low, high, later, earlier, sems):
@@ -431,6 +451,7 @@
         scratch_shapes=[pltpu.VMEM(x.shape, x.dtype) for x in (near, low, high)]
         + [pltpu.VMEM((2, 4 * (HALF + 1), 128), jnp.float32)] * 2
         + [pltpu.SemaphoreType.DMA((3,))],
+        compiler_params=pltpu.CompilerParams(vmem_limit_bytes=16 * MIB),
         cost_estimate=pl.CostEstimate(flops=10_000_000, bytes_accessed=7_000_000, transcendentals=0),
         name="final",
     )(near, low, high)
@@ -495,17 +516,14 @@
 
     left = [left_own, left_next]
     parts = [part_0, part_1]
-    relay_up, plain_up, relay_down, plain_down = gram(
-        0, live, first_lanes, backward, left, parts, (2, 2, 2, 2), jnp.bfloat16
-    )
-    up_in, down_in = one_row(relay_up, 1), one_row(relay_down, -1)
-    plain_below, plain_above = one_row(plain_up, 1), one_row(plain_down, -1)
+    up_out, down_out = gram(0, live, first_lanes, backward, left, parts, (4, 4), jnp.bfloat16)
+    from_below, from_above = one_row(up_out, 1), one_row(down_out, -1)
     keep, other, own = gram(1, live, first_lanes, backward, left, parts, (2, 2, 4), jnp.float32)
 
     f32 = jnp.float32
-    two_below = one_row((keep + up_in.astype(f32)).astype(jnp.bfloat16), 1)
-    two_above = one_row((other + down_in.astype(f32)).astype(jnp.bfloat16), -1)
-    near = own + jnp.concatenate([plain_above, plain_below], axis=0).astype(f32)
+    two_below = one_row((keep + from_below[:2].astype(f32)).astype(jnp.bfloat16), 1)
+    two_above = one_row((other + from_above[:2].astype(f32)).astype(jnp.bfloat16), -1)
+    near = own + jnp.concatenate([from_above[2:], from_below[2:]], axis=0).astype(f32)
     return jnp.transpose(final(near, two_below, two_above), (1, 0, 2))
 
 

time: 147 us -> 137 us (0.932)
  Pallas kernels: 68.6 us -> 64 us
  starting transfers between devices: 38.5 us -> 36.6 us
  local copies, waits for them, and re-layouts: 11.2 us -> 9.72 us
    pallas_call x2, Pallas kernels: 28.8 us -> 24.9 us  [gram(): pl.pallas_call(functools.partial(gram_kernel, tile), out_shape=[jax.Shape...]
    ppermute x17 -> x15, starting transfers between devices: 38.5 us -> 36.6 us  [moved(): return lax.ppermute(block, axis, [(i, to(i) % size) for i in range(size)])]
    unnamed x27 -> x23, local copies, waits for them, and re-layouts: 6.52 us -> 5.01 us
    ppermute x17 -> x15, waiting for transfers between devices: 25.1 us -> 24.2 us  [moved(): return lax.ppermute(block, axis, [(i, to(i) % size) for i in range(size)])]
  transfers between devices with their start and end apart: 17 -> 15, of which waited for: 6 -> 6; matrix products, arithmetic and copies ran while one was open for 4% -> 3% of each run, Pallas kernels for 27% -> 27%
where the time goes in v7:
time: 137 us; the launch traced here: 136 us
  Pallas kernels  64 us (47%)
  starting transfers between devices  36.6 us (27%)
  waiting for transfers between devices  24.2 us (18%)
  local copies, waits for them, and re-layouts  9.72 us (7%)
    ppermute x15, starting transfers between devices, moved(): return lax.ppermute(block, axis, [(i, to(i) % size) for i in range(size)])  36.6 us
    pallas_call x2, Pallas kernels, whiten_bins(): pl.pallas_call(functools.partial(whiten_kernel, chunk), out_shape=jax.Sha...  25.5 us
    pallas_call x2, Pallas kernels, gram(): pl.pallas_call(functools.partial(gram_kernel, tile), out_shape=[jax.Shape...  24.9 us
    ppermute x15, waiting for transfers between devices, moved(): return lax.ppermute(block, axis, [(i, to(i) % size) for i in range(size)])  24.2 us
    pallas_call x2, Pallas kernels, left_bins(): pl.pallas_call(left_kernel, out_shape=jax.ShapeDtypeStruct(shape, jnp.bfl...  10.9 us
    unnamed x23, local copies, waits for them, and re-layouts  5.01 us
  transfers between devices with their start and end apart: 15, of which 6 were waited for; matrix products, arithmetic and copies ran while one was open for 3% of the time, Pallas kernels for 27%

profile of v7, /device:TPU:0, one launch (start us, length us, event | category | flops | bytes accessed | tf_op | source)
XLA Modules:
  0.0 136.2 jit_solution(10000573982096233295)
XLA Ops:
  0.0 1.1 slice.38
  1.1 6.4 %collective-permute-start = (bf16[32,32,256]{2,1,0:T(8,128)(2,1)S(1)}, bf16[32,32,256]{2,1,0:T(8,128)(2,1)S(1)}, u32[]{:S(2)}, u32[]{:S(2)}) collective-permute-start(bf16[32,32,256]{2,1,0:T(8,128)(2,1)S(1)} %slice.38), channel_id=1, source_target_pairs={{0,62},{1,63},{2,0},{3,1},{4,2},{5,3},{6,4},{7,5},{8,6},{9,7},{10,... | collective-permute-start | bytes 1572872 | tf_op jit(solution)/shard_map/ppermute | solution.py:462
  7.5 0.0 copy-start.3
  7.5 0.9 copy-done.3
  8.4 5.5 %left.2.refs_0_ = bf16[256,64,128]{2,1,0:T(8,128)(2,1)S(1)} custom-call(s32[1]{0:T(128)} %bitcast.1.odd_ref, bf16[512,256]{1,0:T(8,128)(2,1)S(1)} %copy-done.3, bf16[64,32,256]{2,1,0:T(8,128)(2,1)} %x0.3), custom_call_target="tpu_custom_call" | custom-call | flops 4000000000 | bytes 8000000 | tf_op jit(solution)/shard_map/left/pallas_call | solution.py:265
  13.9 0.0 copy-start.5
  13.9 1.9 %copy-done.5 = bf16[256,64,128]{2,1,0:T(8,128)(2,1)} copy-done((bf16[256,64,128]{2,1,0:T(8,128)(2,1)}, bf16[256,64,128]{2,1,0:T(8,128)(2,1)S(1)}, u32[]{:S(2)}) %copy-start.5) | copy-done | bytes 4194328
  15.8 2.8 %collective-permute-done.a1 = bf16[32,32,256]{2,1,0:T(8,128)(2,1)S(1)} collective-permute-done((bf16[32,32,256]{2,1,0:T(8,128)(2,1)S(1)}, bf16[32,32,256]{2,1,0:T(8,128)(2,1)S(1)}, u32[]{:S(2)}, u32[]{:S(2)}) %collective-permute-start) | collective-permute-done | bytes 524320 | tf_op jit(solution)/shard_map/ppermute | solution.py:462
  18.7 5.8 %collective-permute-start.6 = (bf16[32,32,256]{2,1,0:T(8,128)(2,1)S(1)}, bf16[32,32,256]{2,1,0:T(8,128)(2,1)}, u32[]{:S(2)}, u32[]{:S(2)}) collective-permute-start(bf16[32,32,256]{2,1,0:T(8,128)(2,1)S(1)} %collective-permute-done.a1), channel_id=1, source_target_pairs={{0,62},{1,63},{2,0},{3,1},{4,2},{5,3},{6,4},{7,5},{8,6},{9,7},{10,... | collective-permute-start | bytes 1572872 | tf_op jit(solution)/shard_map/ppermute | solution.py:462
  24.5 0.0 collective-permute-start.1
  24.5 1.9 %slice.39 = bf16[32,32,256]{2,1,0:T(8,128)(2,1)} slice(bf16[64,32,256]{2,1,0:T(8,128)(2,1)} %x0.3), slice={[32:64], [0:32], [0:256]} | slice | bytes 1048576 | tf_op jit(solution)/shard_map/slice | solution.py:500
  26.3 0.0 collective-permute-start.3
  26.3 0.0 copy-done.7
  26.3 0.1 copy.9
  26.4 0.0 copy-done.8
  26.4 0.0 copy-done.9
  26.4 0.6 gather_fusion
  27.0 0.6 collective-permute-start.2
  27.6 9.2 %collective-permute-done.6.a2 = bf16[32,32,256]{2,1,0:T(8,128)(2,1)} collective-permute-done((bf16[32,32,256]{2,1,0:T(8,128)(2,1)S(1)}, bf16[32,32,256]{2,1,0:T(8,128)(2,1)}, u32[]{:S(2)}, u32[]{:S(2)}) %collective-permute-start.6) | collective-permute-done | bytes 524320 | tf_op jit(solution)/shard_map/ppermute | solution.py:462
  36.8 0.0 collective-permute-start.7
  36.8 1.0 slice.53
  37.8 6.1 %collective-permute-start.8 = (bf16[32,16,256]{2,1,0:T(8,128)(2,1)S(1)}, bf16[32,16,256]{2,1,0:T(8,128)(2,1)S(1)}, u32[]{:S(2)}, u32[]{:S(2)}) collective-permute-start(bf16[32,16,256]{2,1,0:T(8,128)(2,1)S(1)} %slice.53), channel_id=1, source_target_pairs={{0,63},{1,0},{2,1},{3,2},{4,3},{5,4},{6,5},{7,6},{8,7},{9,8},{10,9... | collective-permute-start | bytes 786440 | tf_op jit(solution)/shard_map/ppermute | solution.py:462
  43.9 0.2 fusion
  44.7 0.1 broadcast_in_dim.10
  44.8 0.1 broadcast_in_dim_reshape.3
  44.9 1.2 collective-permute-done.3.a1
  46.1 0.0 collective-permute-start.5
  46.1 0.0 collective-permute-done.1.b0.refs_0_
  46.1 5.8 %collective-permute-start.4 = (bf16[32,32,256]{2,1,0:T(8,128)(2,1)S(1)}, bf16[32,32,256]{2,1,0:T(8,128)(2,1)S(1)}, u32[]{:S(2)}, u32[]{:S(2)}) collective-permute-start(bf16[32,32,256]{2,1,0:T(8,128)(2,1)S(1)} %collective-permute-done.3.a1), channel_id=1, source_target_pairs={{0,62},{1,63},{2,0},{3,1},{4,2},{5,3},{6,4},{7,5},{8,6},{9,7},{10,... | collective-permute-start | bytes 1572872 | tf_op jit(solution)/shard_map/ppermute | solution.py:462
  51.9 0.0 collective-permute-done.2.b1.refs_1_
  51.9 0.0 collective-permute-done.8.o5
  51.9 0.0 collective-permute-done.7.b2
  51.9 0.0 copy-done
  51.9 0.0 copy-done.4
  51.9 12.8 %whiten.2.refs_2_ = bf16[2,256,64,128]{3,2,1,0:T(8,128)(2,1)} custom-call(s32[16]{0:T(128)S(1)} %get-tuple-element.29.right_ref, s32[1]{0:T(128)} %bitcast.1.odd_ref, bf16[512,256]{1,0:T(8,128)(2,1)S(1)} %copy-done.4, bf16[64,32,256]{2,1,0:T(8,128)(2,1)} %x0.3, bf16[64,32,256]{2,1,0:T(8,128)(2,1)} %copy-done, ...), custom_call_target="tpu_custom_call" | custom-call | flops 7680000000 | bytes 8000000 | tf_op jit(solution)/shard_map/whiten/pallas_call | solution.py:156
  64.7 0.0 collective-permute-done.5.refs_2_.b1
  64.8 0.0 collective-permute-done.4.a2
  64.8 0.0 copy-start.6
  64.8 0.2 collective-permute-start.9
  65.0 4.7 %collective-permute-start.10 = (bf16[32,16,256]{2,1,0:T(8,128)(2,1)S(1)}, bf16[32,16,256]{2,1,0:T(8,128)(2,1)S(1)}, u32[]{:S(2)}, u32[]{:S(2)}) collective-permute-start(bf16[32,16,256]{2,1,0:T(8,128)(2,1)S(1)} %slice.42), channel_id=1, source_target_pairs={{0,63},{1,0},{2,1},{3,2},{4,3},{5,4},{6,5},{7,6},{8,7},{9,8},{10,9... | collective-permute-start | bytes 786440 | tf_op jit(solution)/shard_map/ppermute | solution.py:462
  69.7 1.2 copy-done.1
  70.9 5.5 %left.3.refs_1_ = bf16[256,64,128]{2,1,0:T(8,128)(2,1)} custom-call(s32[1]{0:T(128)} %bitcast.1.odd_ref, bf16[512,256]{1,0:T(8,128)(2,1)S(1)} %copy-done.4, bf16[64,32,256]{2,1,0:T(8,128)(2,1)S(1)} %copy-done.1, bf16[32,32,256]{2,1,0:T(8,128)(2,1)S(1)} %collective-permute-done.2.b1.refs_1_, bf16[32,32,256]{2,1,0:T(8,128)(2,1)S(1)} %collective-permute-done.5.refs_2_.b1), custom_call_target="tpu_custom_call" | custom-call | flops 4000000000 | bytes 8000000 | tf_op jit(solution)/shard_map/left/pallas_call | solution.py:265
  76.4 0.0 copy-done.6
  76.4 0.0 copy-start.2
  76.4 0.0 collective-permute-done.10.o5
  76.4 0.0 collective-permute-done.9.b2
  76.5 0.0 copy-start.10
  76.5 0.8 copy-done.10
  77.3 12.7 %whiten.3.refs_3_ = bf16[2,256,64,128]{3,2,1,0:T(8,128)(2,1)} custom-call(s32[16]{0:T(128)S(1)} %get-tuple-element.29.right_ref, s32[1]{0:T(128)} %bitcast.1.odd_ref, bf16[512,256]{1,0:T(8,128)(2,1)S(1)} %copy-done.4, bf16[64,32,256]{2,1,0:T(8,128)(2,1)} %x0.3, bf16[64,32,256]{2,1,0:T(8,128)(2,1)} %copy-done, ...), custom_call_target="tpu_custom_call" | custom-call | flops 7680000000 | bytes 8000000 | tf_op jit(solution)/shard_map/whiten/pallas_call | solution.py:156
  90.0 0.0 copy-done.2
  90.0 11.5 %gram.3 = (bf16[4,416,256]{2,1,0:T(8,128)(2,1)S(1)}, bf16[4,416,256]{2,1,0:T(8,128)(2,1)S(1)}) custom-call(s32[16]{0:T(128)S(1)} %compare_convert_fusion.live_ref, s32[1,128]{1,0:T(1,128)S(1)} %get-tuple-element.33.first_ref, bf16[2,416,256]{2,1,0:T(8,128)(2,1)S(1)} %copy-done.2, bf16[256,64,128]{2,1,0:T(8,128)(2,1)} %copy-done.5, ...), custom_call_target="tpu_custom_call" | custom-call | flops 16000000000 | bytes 20000000 | tf_op jit(solution)/shard_map/gram/pallas_call | solution.py:385
  101.5 3.3 %collective-permute-start.11 = (bf16[4,416,256]{2,1,0:T(8,128)(2,1)S(1)}, bf16[4,416,256]{2,1,0:T(8,128)(2,1)S(1)}, u32[]{:S(2)}, u32[]{:S(2)}) collective-permute-start(bf16[4,416,256]{2,1,0:T(8,128)(2,1)S(1)} %get-tuple-element.25), channel_id=1, source_target_pairs={{0,192},{64,0},{128,64},{192,128},{1,193},{65,1},{129,65},{193,129... | collective-permute-start | bytes 2555912 | tf_op jit(solution)/shard_map/ppermute | solution.py:462
  104.8 0.0 collective-permute-start.12
  104.8 13.3 %gram.2 = (f32[2,416,256]{2,1,0:T(8,128)S(1)}, f32[2,416,256]{2,1,0:T(8,128)S(1)}, f32[4,416,256]{2,1,0:T(8,128)S(1)}) custom-call(s32[16]{0:T(128)S(1)} %compare_convert_fusion.live_ref, s32[1,128]{1,0:T(1,128)S(1)} %get-tuple-element.34.first_ref, bf16[2,416,256]{2,1,0:T(8,128)(2,1)S(1)} %copy-done.2, bf16[256,64,128]{2,1,0:T(8,128)(2,1)} %copy-done.5, ...), custom_call_target="tpu_custom_call" | custom-call | flops 16000000000 | bytes 20000000 | tf_op jit(solution)/shard_map/gram/pallas_call | solution.py:385
  118.1 2.0 %collective-permute-done.11 = bf16[4,416,256]{2,1,0:T(8,128)(2,1)S(1)} collective-permute-done((bf16[4,416,256]{2,1,0:T(8,128)(2,1)S(1)}, bf16[4,416,256]{2,1,0:T(8,128)(2,1)S(1)}, u32[]{:S(2)}, u32[]{:S(2)}) %collective-permute-start.11) | collective-permute-done | bytes 852000 | tf_op jit(solution)/shard_map/ppermute | solution.py:462
  120.1 0.1 add_convert_fusion
  120.2 3.7 %collective-permute-start.14 = (bf16[2,416,256]{2,1,0:T(8,128)(2,1)S(1)}, bf16[2,416,256]{2,1,0:T(8,128)(2,1)S(1)}, u32[]{:S(2)}, u32[]{:S(2)}) collective-permute-start(bf16[2,416,256]{2,1,0:T(8,128)(2,1)S(1)} %add_convert_fusion), channel_id=1, source_target_pairs={{0,192},{64,0},{128,64},{192,128},{1,193},{65,1},{129,65},{193,129... | collective-permute-start | bytes 1277960 | tf_op jit(solution)/shard_map/ppermute | solution.py:462
  123.9 0.0 collective-permute-done.12
  123.9 0.1 add_convert_fusion.1
  124.0 0.1 collective-permute-start.13
  124.2 0.2 convert_add_fusion.near_any
  124.4 5.1 %collective-permute-done.14.high_any = bf16[2,416,256]{2,1,0:T(8,128)(2,1)S(1)} collective-permute-done((bf16[2,416,256]{2,1,0:T(8,128)(2,1)S(1)}, bf16[2,416,256]{2,1,0:T(8,128)(2,1)S(1)}, u32[]{:S(2)}, u32[]{:S(2)}) %collective-permute-start.14) | collective-permute-done | bytes 426016 | tf_op jit(solution)/shard_map/ppermute | solution.py:462
  129.5 3.9 %collective-permute-done.13.low_any = bf16[2,416,256]{2,1,0:T(8,128)(2,1)S(1)} collective-permute-done((bf16[2,416,256]{2,1,0:T(8,128)(2,1)S(1)}, bf16[2,416,256]{2,1,0:T(8,128)(2,1)S(1)}, u32[]{:S(2)}, u32[]{:S(2)}) %collective-permute-start.13) | collective-permute-done | bytes 426016 | tf_op jit(solution)/shard_map/ppermute | solution.py:462
  133.4 2.6 %final.1 = f32[401,4,256]{2,1,0:T(4,128)} custom-call(f32[4,416,256]{2,1,0:T(8,128)S(1)} %convert_add_fusion.near_any, bf16[2,416,256]{2,1,0:T(8,128)(2,1)S(1)} %collective-permute-done.13.low_any, bf16[2,416,256]{2,1,0:T(8,128)(2,1)S(1)} %collective-permute-done.14.high_any), custom_call_target="tpu_custom_call" | custom-call | flops 10000000 | bytes 7000000 | tf_op jit(solution)/shard_map/final/pallas_call | solution.py:446
  (14 shorter events, 0.1 us)
Async XLA Ops:
  1.1 17.6 %collective-permute-start = (bf16[32,32,256]{2,1,0:T(8,128)(2,1)S(1)}, bf16[32,32,256]{2,1,0:T(8,128)(2,1)S(1)}, u32[]{:S(2)}, u32[]{:S(2)}) collective-permute-start(bf16[32,32,256]{2,1,0:T(8,128)(2,1)S(1)} %slice.38), channel_id=1, source_target_pairs={{0,62},{1,63},{2,0},{3,1},{4,2},{5,3},{6,4},{7,5},{8,6},{9,7},{10,... | collective-permute-start | bytes 1572872 | tf_op jit(solution)/shard_map/ppermute | solution.py:462
  7.5 0.9 copy-start.3
  8.4 17.9 %copy-start.7 = (s32[16,2]{0,1:T(2,128)S(1)}, s32[16,2]{0,1:T(2,128)}, u32[]{:S(2)}) copy-start(s32[16,2]{0,1:T(2,128)} %param.8) | copy-start | bytes 388
  8.4 18.0 %copy-start.8 = (s32[16]{0:T(128)S(1)}, s32[16]{0:T(128)}, u32[]{:S(2)}) copy-start(s32[16]{0:T(128)} %constant.53.clone) | copy-start | bytes 196
  8.4 18.0 %copy-start.9 = (s32[16]{0:T(128)S(1)}, s32[16]{0:T(128)}, u32[]{:S(2)}) copy-start(s32[16]{0:T(128)} %constant.52.clone) | copy-start | bytes 196
  13.9 1.9 %copy-start.5 = (bf16[256,64,128]{2,1,0:T(8,128)(2,1)}, bf16[256,64,128]{2,1,0:T(8,128)(2,1)S(1)}, u32[]{:S(2)}) copy-start(bf16[256,64,128]{2,1,0:T(8,128)(2,1)S(1)} %left.2.refs_0_) | copy-start | bytes 12582916
  15.8 36.1 %copy-start.4 = (bf16[512,256]{1,0:T(8,128)(2,1)S(1)}, bf16[512,256]{1,0:T(8,128)(2,1)}, u32[]{:S(2)}) copy-start(bf16[512,256]{1,0:T(8,128)(2,1)} %constant.54.clone.table_ref) | copy-start | bytes 786436
  18.7 18.2 %collective-permute-start.6 = (bf16[32,32,256]{2,1,0:T(8,128)(2,1)S(1)}, bf16[32,32,256]{2,1,0:T(8,128)(2,1)}, u32[]{:S(2)}, u32[]{:S(2)}) collective-permute-start(bf16[32,32,256]{2,1,0:T(8,128)(2,1)S(1)} %collective-permute-done.a1), channel_id=1, source_target_pairs={{0,62},{1,63},{2,0},{3,1},{4,2},{5,3},{6,4},{7,5},{8,6},{9,7},{10,... | collective-permute-start | bytes 1572872 | tf_op jit(solution)/shard_map/ppermute | solution.py:462
  24.5 21.7 %collective-permute-start.1 = (bf16[64,32,256]{2,1,0:T(8,128)(2,1)}, bf16[64,32,256]{2,1,0:T(8,128)(2,1)S(1)}, u32[]{:S(2)}, u32[]{:S(2)}) collective-permute-start(bf16[64,32,256]{2,1,0:T(8,128)(2,1)} %x0.3), channel_id=1, source_target_pairs={{0,1},{1,0},{2,3},{3,2},{4,5},{5,4},{6,7},{7,6},{8,9},{9,8},{10,11... | collective-permute-start | bytes 3145736 | tf_op jit(solution)/shard_map/ppermute | solution.py:462
  26.3 19.8 %collective-permute-start.3 = (bf16[32,32,256]{2,1,0:T(8,128)(2,1)}, bf16[32,32,256]{2,1,0:T(8,128)(2,1)S(1)}, u32[]{:S(2)}, u32[]{:S(2)}) collective-permute-start(bf16[32,32,256]{2,1,0:T(8,128)(2,1)} %slice.39), channel_id=1, source_target_pairs={{0,62},{1,63},{2,0},{3,1},{4,2},{5,3},{6,4},{7,5},{8,6},{9,7},{10,... | collective-permute-start | bytes 1572872 | tf_op jit(solution)/shard_map/ppermute | solution.py:462
  27.0 24.9 %collective-permute-start.2 = (bf16[32,32,256]{2,1,0:T(8,128)(2,1)S(1)}, bf16[32,32,256]{2,1,0:T(8,128)(2,1)S(1)}, u32[]{:S(2)}, u32[]{:S(2)}) collective-permute-start(bf16[32,32,256]{2,1,0:T(8,128)(2,1)S(1)} %collective-permute-done.a1), channel_id=1, source_target_pairs={{0,1},{1,0},{2,3},{3,2},{4,5},{5,4},{6,7},{7,6},{8,9},{9,8},{10,11... | collective-permute-start | bytes 1572872 | tf_op jit(solution)/shard_map/ppermute | solution.py:462
  36.8 15.1 %collective-permute-start.7 = (bf16[32,32,256]{2,1,0:T(8,128)(2,1)}, bf16[32,32,256]{2,1,0:T(8,128)(2,1)}, u32[]{:S(2)}, u32[]{:S(2)}) collective-permute-start(bf16[32,32,256]{2,1,0:T(8,128)(2,1)} %collective-permute-done.6.a2), channel_id=1, source_target_pairs={{0,1},{1,0},{2,3},{3,2},{4,5},{5,4},{6,7},{7,6},{8,9},{9,8},{10,11... | collective-permute-start | bytes 1572872 | tf_op jit(solution)/shard_map/ppermute | solution.py:462
  37.8 14.1 %collective-permute-start.8 = (bf16[32,16,256]{2,1,0:T(8,128)(2,1)S(1)}, bf16[32,16,256]{2,1,0:T(8,128)(2,1)S(1)}, u32[]{:S(2)}, u32[]{:S(2)}) collective-permute-start(bf16[32,16,256]{2,1,0:T(8,128)(2,1)S(1)} %slice.53), channel_id=1, source_target_pairs={{0,63},{1,0},{2,1},{3,2},{4,3},{5,4},{6,5},{7,6},{8,7},{9,8},{10,9... | collective-permute-start | bytes 786440 | tf_op jit(solution)/shard_map/ppermute | solution.py:462
  46.1 18.6 %collective-permute-start.5 = (bf16[32,32,256]{2,1,0:T(8,128)(2,1)S(1)}, bf16[32,32,256]{2,1,0:T(8,128)(2,1)S(1)}, u32[]{:S(2)}, u32[]{:S(2)}) collective-permute-start(bf16[32,32,256]{2,1,0:T(8,128)(2,1)S(1)} %collective-permute-done.3.a1), channel_id=1, source_target_pairs={{0,1},{1,0},{2,3},{3,2},{4,5},{5,4},{6,7},{7,6},{8,9},{9,8},{10,11... | collective-permute-start | bytes 1572872 | tf_op jit(solution)/shard_map/ppermute | solution.py:462
  46.1 5.8 %copy-start = (bf16[64,32,256]{2,1,0:T(8,128)(2,1)}, bf16[64,32,256]{2,1,0:T(8,128)(2,1)S(1)}, u32[]{:S(2)}) copy-start(bf16[64,32,256]{2,1,0:T(8,128)(2,1)S(1)} %collective-permute-done.1.b0.refs_0_) | copy-start | bytes 3145732
  46.1 18.6 %collective-permute-start.4 = (bf16[32,32,256]{2,1,0:T(8,128)(2,1)S(1)}, bf16[32,32,256]{2,1,0:T(8,128)(2,1)S(1)}, u32[]{:S(2)}, u32[]{:S(2)}) collective-permute-start(bf16[32,32,256]{2,1,0:T(8,128)(2,1)S(1)} %collective-permute-done.3.a1), channel_id=1, source_target_pairs={{0,62},{1,63},{2,0},{3,1},{4,2},{5,3},{6,4},{7,5},{8,6},{9,7},{10,... | collective-permute-start | bytes 1572872 | tf_op jit(solution)/shard_map/ppermute | solution.py:462
  64.8 11.6 %copy-start.6 = (bf16[32,32,256]{2,1,0:T(8,128)(2,1)}, bf16[32,32,256]{2,1,0:T(8,128)(2,1)S(1)}, u32[]{:S(2)}) copy-start(bf16[32,32,256]{2,1,0:T(8,128)(2,1)S(1)} %collective-permute-done.4.a2) | copy-start | bytes 1572868
  64.8 11.7 %collective-permute-start.9 = (bf16[32,32,256]{2,1,0:T(8,128)(2,1)S(1)}, bf16[32,32,256]{2,1,0:T(8,128)(2,1)S(1)}, u32[]{:S(2)}, u32[]{:S(2)}) collective-permute-start(bf16[32,32,256]{2,1,0:T(8,128)(2,1)S(1)} %collective-permute-done.4.a2), channel_id=1, source_target_pairs={{0,1},{1,0},{2,3},{3,2},{4,5},{5,4},{6,7},{7,6},{8,9},{9,8},{10,11... | collective-permute-start | bytes 1572872 | tf_op jit(solution)/shard_map/ppermute | solution.py:462
  65.0 11.5 %collective-permute-start.10 = (bf16[32,16,256]{2,1,0:T(8,128)(2,1)S(1)}, bf16[32,16,256]{2,1,0:T(8,128)(2,1)S(1)}, u32[]{:S(2)}, u32[]{:S(2)}) collective-permute-start(bf16[32,16,256]{2,1,0:T(8,128)(2,1)S(1)} %slice.42), channel_id=1, source_target_pairs={{0,63},{1,0},{2,1},{3,2},{4,3},{5,4},{6,5},{7,6},{8,7},{9,8},{10,9... | collective-permute-start | bytes 786440 | tf_op jit(solution)/shard_map/ppermute | solution.py:462
  69.7 1.2 copy-start.1
  76.4 13.5 %copy-start.2 = (bf16[2,416,256]{2,1,0:T(8,128)(2,1)S(1)}, bf16[2,416,256]{2,1,0:T(8,128)(2,1)}, u32[]{:S(2)}) copy-start(bf16[2,416,256]{2,1,0:T(8,128)(2,1)} %constant.55.clone.table_ref) | copy-start | bytes 1277956
  76.5 0.8 copy-start.10
  101.5 18.6 %collective-permute-start.11 = (bf16[4,416,256]{2,1,0:T(8,128)(2,1)S(1)}, bf16[4,416,256]{2,1,0:T(8,128)(2,1)S(1)}, u32[]{:S(2)}, u32[]{:S(2)}) collective-permute-start(bf16[4,416,256]{2,1,0:T(8,128)(2,1)S(1)} %get-tuple-element.25), channel_id=1, source_target_pairs={{0,192},{64,0},{128,64},{192,128},{1,193},{65,1},{129,65},{193,129... | collective-permute-start | bytes 2555912 | tf_op jit(solution)/shard_map/ppermute | solution.py:462
  104.8 19.1 %collective-permute-start.12 = (bf16[4,416,256]{2,1,0:T(8,128)(2,1)S(1)}, bf16[4,416,256]{2,1,0:T(8,128)(2,1)S(1)}, u32[]{:S(2)}, u32[]{:S(2)}) collective-permute-start(bf16[4,416,256]{2,1,0:T(8,128)(2,1)S(1)} %get-tuple-element.26), channel_id=1, source_target_pairs={{0,64},{64,128},{128,192},{192,0},{1,65},{65,129},{129,193},{193,1... | collective-permute-start | bytes 2555912 | tf_op jit(solution)/shard_map/ppermute | solution.py:462
  120.2 9.3 %collective-permute-start.14 = (bf16[2,416,256]{2,1,0:T(8,128)(2,1)S(1)}, bf16[2,416,256]{2,1,0:T(8,128)(2,1)S(1)}, u32[]{:S(2)}, u32[]{:S(2)}) collective-permute-start(bf16[2,416,256]{2,1,0:T(8,128)(2,1)S(1)} %add_convert_fusion), channel_id=1, source_target_pairs={{0,192},{64,0},{128,64},{192,128},{1,193},{65,1},{129,65},{193,129... | collective-permute-start | bytes 1277960 | tf_op jit(solution)/shard_map/ppermute | solution.py:462
  124.0 9.4 %collective-permute-start.13 = (bf16[2,416,256]{2,1,0:T(8,128)(2,1)S(1)}, bf16[2,416,256]{2,1,0:T(8,128)(2,1)S(1)}, u32[]{:S(2)}, u32[]{:S(2)}) collective-permute-start(bf16[2,416,256]{2,1,0:T(8,128)(2,1)S(1)} %add_convert_fusion.1), channel_id=1, source_target_pairs={{0,64},{64,128},{128,192},{192,0},{1,65},{65,129},{129,193},{193,1... | collective-permute-start | bytes 1277960 | tf_op jit(solution)/shard_map/ppermute | solution.py:462

commit v8 on v7

--- a/solution.py
+++ b/solution.py
@@ -48,19 +48,26 @@
     return (np.ascontiguousarray(forward.astype(ml_dtypes.bfloat16).T), np.concatenate([high, low], axis=1))
 
 
-def whiten_tile(spec, lanes, put):
-    total = jnp.zeros((8, 128), jnp.float32)
+def whiten_tiles(spec, put):
+    def parts(h, f):
+        lanes = slice(h * 128, (h + 1) * 128)
+        return spec[f:f + 8, lanes], spec[BINS + f:BINS + f + 8, lanes]
+
+    floors = []
+    for h in range(2):
+        totals = [None] * 4
+        for k, f in enumerate(range(0, BINS, 8)):
+            real_part, imag_part = parts(h, f)
+            energy = real_part * real_part + imag_part * imag_part
+            totals[k % 4] = energy if k < 4 else totals[k % 4] + energy
+        total = (totals[0] + totals[1]) + (totals[2] + totals[3])
+        level = jnp.sum(total, axis=0, keepdims=True) * (1.0 / BINS)
+        floors.append(jnp.broadcast_to(water_share * level + tiny_eps, (8, 128)))
     for f in range(0, BINS, 8):
-        real_part = spec[f:f + 8, lanes]
-        imag_part = spec[BINS + f:BINS + f + 8, lanes]
-        total = total + (real_part * real_part + imag_part * imag_part)
-    level = jnp.sum(total, axis=0, keepdims=True) * (1.0 / BINS)
-    floor = jnp.broadcast_to(water_share * level + tiny_eps, (8, 128))
-    for f in range(0, BINS, 8):
-        real_part = spec[f:f + 8, lanes]
-        imag_part = spec[BINS + f:BINS + f + 8, lanes]
-        inverse = lax.rsqrt(real_part * real_part + imag_part * imag_part + floor)
-        put(f, real_part * inverse, imag_part * inverse)
+        for h in range(2):
+            real_part, imag_part = parts(h, f)
+            inverse = lax.rsqrt(real_part * real_part + imag_part * imag_part + floors[h])
+            put(h, f, real_part * inverse, imag_part * inverse)
 
 
 def in_turns(count, transform, whiten, spec_a, spec_b):
@@ -118,12 +125,11 @@
         )
 
     def whiten(s, spec):
-        for h in range(2):
-            def put(f, real_part, imag_part):
-                bins_ref[h, pl.ds(f * pitch + s, 8, stride=pitch), :] = real_part
-                bins_ref[h, pl.ds(f * pitch + segs + s, 8, stride=pitch), :] = imag_part
-
-            whiten_tile(spec, slice(h * 128, (h + 1) * 128), put)
+        def put(h, f, real_part, imag_part):
+            bins_ref[h, pl.ds(f * pitch + s, 8, stride=pitch), :] = real_part
+            bins_ref[h, pl.ds(f * pitch + segs + s, 8, stride=pitch), :] = imag_part
+
+        whiten_tiles(spec, put)
 
     in_turns(segs, transform, whiten, spec_a, spec_b)
 
@@ -223,22 +229,20 @@
     in_first = lax.broadcasted_iota(jnp.int32, (8, 128), 1) < LEFT
 
     def whiten(quad, spec):
-        for h in range(2):
+        def put(h, f, real_part, imag_part):
             a = quad * 4 + 2 * h
-
-            def put(f, real_part, imag_part):
-                real_other = pltpu.roll(real_part, LEFT, 1)
-                imag_other = pltpu.roll(imag_part, LEFT, 1)
-                rows = [
-                    (a, jnp.where(in_first, real_part, imag_other)),
-                    (OWN + a, jnp.where(in_first, imag_part, -real_other)),
-                    (a + 1, jnp.where(in_first, real_other, imag_part)),
-                    (OWN + a + 1, jnp.where(in_first, imag_other, -real_part)),
-                ]
-                for row, value in rows:
-                    bins_ref[pl.ds(f * pitch + row, 8, stride=pitch), :] = value
-
-            whiten_tile(spec, slice(h * 128, (h + 1) * 128), put)
+            real_other = pltpu.roll(real_part, LEFT, 1)
+            imag_other = pltpu.roll(imag_part, LEFT, 1)
+            rows = [
+                (a, jnp.where(in_first, real_part, imag_other)),
+                (OWN + a, jnp.where(in_first, imag_part, -real_other)),
+                (a + 1, jnp.where(in_first, real_other, imag_part)),
+                (OWN + a + 1, jnp.where(in_first, imag_other, -real_part)),
+            ]
+            for row, value in rows:
+                bins_ref[pl.ds(f * pitch + row, 8, stride=pitch), :] = value
+
+        whiten_tiles(spec, put)
 
     in_turns(OWN // 4, transform, whiten, spec_a, spec_b)
 

time: 137 us -> 138 us (level)
  no operation moved by 1% of the time
where the time goes in v8:
time: 138 us; the launch traced here: 137 us
  Pallas kernels  64.5 us (47%)
  starting transfers between devices  36.4 us (26%)
  waiting for transfers between devices  24.1 us (17%)
  local copies, waits for them, and re-layouts  9.72 us (7%)
    ppermute x15, starting transfers between devices, moved(): return lax.ppermute(block, axis, [(i, to(i) % size) for i in range(size)])  36.4 us
    pallas_call x2, Pallas kernels, whiten_bins(): pl.pallas_call(functools.partial(whiten_kernel, chunk), out_shape=jax.Sha...  25.9 us
    pallas_call x2, Pallas kernels, gram(): pl.pallas_call(functools.partial(gram_kernel, tile), out_shape=[jax.Shape...  24.9 us
    ppermute x15, waiting for transfers between devices, moved(): return lax.ppermute(block, axis, [(i, to(i) % size) for i in range(size)])  24.1 us
    pallas_call x2, Pallas kernels, left_bins(): pl.pallas_call(left_kernel, out_shape=jax.ShapeDtypeStruct(shape, jnp.bfl...  11.1 us
    unnamed x23, local copies, waits for them, and re-layouts  5.01 us
  transfers between devices with their start and end apart: 15, of which 6 were waited for; matrix products, arithmetic and copies ran while one was open for 3% of the time, Pallas kernels for 27%

profile of v8, /device:TPU:0, one launch (start us, length us, event | category | flops | bytes accessed | tf_op | source)
XLA Modules:
  0.0 136.5 jit_solution(13020654151643836697)
XLA Ops:
  0.0 1.1 slice.38
  1.1 6.4 %collective-permute-start = (bf16[32,32,256]{2,1,0:T(8,128)(2,1)S(1)}, bf16[32,32,256]{2,1,0:T(8,128)(2,1)S(1)}, u32[]{:S(2)}, u32[]{:S(2)}) collective-permute-start(bf16[32,32,256]{2,1,0:T(8,128)(2,1)S(1)} %slice.38), channel_id=1, source_target_pairs={{0,62},{1,63},{2,0},{3,1},{4,2},{5,3},{6,4},{7,5},{8,6},{9,7},{10,... | collective-permute-start | bytes 1572872 | tf_op jit(solution)/shard_map/ppermute | solution.py:466
  7.5 0.0 copy-start.3
  7.5 0.9 copy-done.3
  8.4 5.6 %left.2.refs_0_ = bf16[256,64,128]{2,1,0:T(8,128)(2,1)S(1)} custom-call(s32[1]{0:T(128)} %bitcast.1.odd_ref, bf16[512,256]{1,0:T(8,128)(2,1)S(1)} %copy-done.3, bf16[64,32,256]{2,1,0:T(8,128)(2,1)} %x0.3), custom_call_target="tpu_custom_call" | custom-call | flops 4000000000 | bytes 8000000 | tf_op jit(solution)/shard_map/left/pallas_call | solution.py:269
  14.0 0.0 copy-start.5
  14.0 1.9 %copy-done.5 = bf16[256,64,128]{2,1,0:T(8,128)(2,1)} copy-done((bf16[256,64,128]{2,1,0:T(8,128)(2,1)}, bf16[256,64,128]{2,1,0:T(8,128)(2,1)S(1)}, u32[]{:S(2)}) %copy-start.5) | copy-done | bytes 4194328
  16.0 2.7 %collective-permute-done.a1 = bf16[32,32,256]{2,1,0:T(8,128)(2,1)S(1)} collective-permute-done((bf16[32,32,256]{2,1,0:T(8,128)(2,1)S(1)}, bf16[32,32,256]{2,1,0:T(8,128)(2,1)S(1)}, u32[]{:S(2)}, u32[]{:S(2)}) %collective-permute-start) | collective-permute-done | bytes 524320 | tf_op jit(solution)/shard_map/ppermute | solution.py:466
  18.7 5.8 %collective-permute-start.6 = (bf16[32,32,256]{2,1,0:T(8,128)(2,1)S(1)}, bf16[32,32,256]{2,1,0:T(8,128)(2,1)}, u32[]{:S(2)}, u32[]{:S(2)}) collective-permute-start(bf16[32,32,256]{2,1,0:T(8,128)(2,1)S(1)} %collective-permute-done.a1), channel_id=1, source_target_pairs={{0,62},{1,63},{2,0},{3,1},{4,2},{5,3},{6,4},{7,5},{8,6},{9,7},{10,... | collective-permute-start | bytes 1572872 | tf_op jit(solution)/shard_map/ppermute | solution.py:466
  24.5 0.0 collective-permute-start.1
  24.5 1.9 %slice.39 = bf16[32,32,256]{2,1,0:T(8,128)(2,1)} slice(bf16[64,32,256]{2,1,0:T(8,128)(2,1)} %x0.3), slice={[32:64], [0:32], [0:256]} | slice | bytes 1048576 | tf_op jit(solution)/shard_map/slice | solution.py:504
  26.3 0.0 collective-permute-start.3
  26.3 0.0 copy-done.7
  26.3 0.1 copy.9
  26.4 0.0 copy-done.8
  26.4 0.0 copy-done.9
  26.4 0.6 gather_fusion
  27.0 0.6 collective-permute-start.2
  27.6 9.2 %collective-permute-done.6.a2 = bf16[32,32,256]{2,1,0:T(8,128)(2,1)} collective-permute-done((bf16[32,32,256]{2,1,0:T(8,128)(2,1)S(1)}, bf16[32,32,256]{2,1,0:T(8,128)(2,1)}, u32[]{:S(2)}, u32[]{:S(2)}) %collective-permute-start.6) | collective-permute-done | bytes 524320 | tf_op jit(solution)/shard_map/ppermute | solution.py:466
  36.8 0.0 collective-permute-start.7
  36.8 1.0 slice.53
  37.8 6.1 %collective-permute-start.8 = (bf16[32,16,256]{2,1,0:T(8,128)(2,1)S(1)}, bf16[32,16,256]{2,1,0:T(8,128)(2,1)S(1)}, u32[]{:S(2)}, u32[]{:S(2)}) collective-permute-start(bf16[32,16,256]{2,1,0:T(8,128)(2,1)S(1)} %slice.53), channel_id=1, source_target_pairs={{0,63},{1,0},{2,1},{3,2},{4,3},{5,4},{6,5},{7,6},{8,7},{9,8},{10,9... | collective-permute-start | bytes 786440 | tf_op jit(solution)/shard_map/ppermute | solution.py:466
  43.9 0.2 fusion
  44.7 0.1 broadcast_in_dim.10
  44.8 0.1 broadcast_in_dim_reshape.3
  44.9 1.2 collective-permute-done.3.a1
  46.1 0.0 collective-permute-start.5
  46.1 0.0 collective-permute-done.1.b0.refs_0_
  46.1 5.8 %collective-permute-start.4 = (bf16[32,32,256]{2,1,0:T(8,128)(2,1)S(1)}, bf16[32,32,256]{2,1,0:T(8,128)(2,1)S(1)}, u32[]{:S(2)}, u32[]{:S(2)}) collective-permute-start(bf16[32,32,256]{2,1,0:T(8,128)(2,1)S(1)} %collective-permute-done.3.a1), channel_id=1, source_target_pairs={{0,62},{1,63},{2,0},{3,1},{4,2},{5,3},{6,4},{7,5},{8,6},{9,7},{10,... | collective-permute-start | bytes 1572872 | tf_op jit(solution)/shard_map/ppermute | solution.py:466
  51.9 0.0 collective-permute-done.2.b1.refs_1_
  51.9 0.0 collective-permute-done.8.o5
  51.9 0.0 collective-permute-done.7.b2
  51.9 0.0 copy-done
  51.9 0.0 copy-done.4
  51.9 13.0 %whiten.2.refs_2_ = bf16[2,256,64,128]{3,2,1,0:T(8,128)(2,1)} custom-call(s32[16]{0:T(128)S(1)} %get-tuple-element.29.right_ref, s32[1]{0:T(128)} %bitcast.1.odd_ref, bf16[512,256]{1,0:T(8,128)(2,1)S(1)} %copy-done.4, bf16[64,32,256]{2,1,0:T(8,128)(2,1)} %x0.3, bf16[64,32,256]{2,1,0:T(8,128)(2,1)} %copy-done, ...), custom_call_target="tpu_custom_call" | custom-call | flops 7680000000 | bytes 8000000 | tf_op jit(solution)/shard_map/whiten/pallas_call | solution.py:162
  64.9 0.0 collective-permute-done.5.refs_2_.b1
  64.9 0.0 collective-permute-done.4.a2
  64.9 0.0 copy-start.6
  64.9 0.2 collective-permute-start.9
  65.1 4.6 %collective-permute-start.10 = (bf16[32,16,256]{2,1,0:T(8,128)(2,1)S(1)}, bf16[32,16,256]{2,1,0:T(8,128)(2,1)S(1)}, u32[]{:S(2)}, u32[]{:S(2)}) collective-permute-start(bf16[32,16,256]{2,1,0:T(8,128)(2,1)S(1)} %slice.42), channel_id=1, source_target_pairs={{0,63},{1,0},{2,1},{3,2},{4,3},{5,4},{6,5},{7,6},{8,7},{9,8},{10,9... | collective-permute-start | bytes 786440 | tf_op jit(solution)/shard_map/ppermute | solution.py:466
  69.7 1.2 copy-done.1
  70.9 5.6 %left.3.refs_1_ = bf16[256,64,128]{2,1,0:T(8,128)(2,1)} custom-call(s32[1]{0:T(128)} %bitcast.1.odd_ref, bf16[512,256]{1,0:T(8,128)(2,1)S(1)} %copy-done.4, bf16[64,32,256]{2,1,0:T(8,128)(2,1)S(1)} %copy-done.1, bf16[32,32,256]{2,1,0:T(8,128)(2,1)S(1)} %collective-permute-done.2.b1.refs_1_, bf16[32,32,256]{2,1,0:T(8,128)(2,1)S(1)} %collective-permute-done.5.refs_2_.b1), custom_call_target="tpu_custom_call" | custom-call | flops 4000000000 | bytes 8000000 | tf_op jit(solution)/shard_map/left/pallas_call | solution.py:269
  76.5 0.0 copy-done.6
  76.5 0.0 copy-start.2
  76.5 0.0 collective-permute-done.10.o5
  76.5 0.0 collective-permute-done.9.b2
  76.6 0.0 copy-start.10
  76.6 0.8 copy-done.10
  77.3 12.9 %whiten.3.refs_3_ = bf16[2,256,64,128]{3,2,1,0:T(8,128)(2,1)} custom-call(s32[16]{0:T(128)S(1)} %get-tuple-element.29.right_ref, s32[1]{0:T(128)} %bitcast.1.odd_ref, bf16[512,256]{1,0:T(8,128)(2,1)S(1)} %copy-done.4, bf16[64,32,256]{2,1,0:T(8,128)(2,1)} %x0.3, bf16[64,32,256]{2,1,0:T(8,128)(2,1)} %copy-done, ...), custom_call_target="tpu_custom_call" | custom-call | flops 7680000000 | bytes 8000000 | tf_op jit(solution)/shard_map/whiten/pallas_call | solution.py:162
  90.2 0.0 copy-done.2
  90.2 11.5 %gram.3 = (bf16[4,416,256]{2,1,0:T(8,128)(2,1)S(1)}, bf16[4,416,256]{2,1,0:T(8,128)(2,1)S(1)}) custom-call(s32[16]{0:T(128)S(1)} %compare_convert_fusion.live_ref, s32[1,128]{1,0:T(1,128)S(1)} %get-tuple-element.33.first_ref, bf16[2,416,256]{2,1,0:T(8,128)(2,1)S(1)} %copy-done.2, bf16[256,64,128]{2,1,0:T(8,128)(2,1)} %copy-done.5, ...), custom_call_target="tpu_custom_call" | custom-call | flops 16000000000 | bytes 20000000 | tf_op jit(solution)/shard_map/gram/pallas_call | solution.py:389
  101.8 3.3 %collective-permute-start.11 = (bf16[4,416,256]{2,1,0:T(8,128)(2,1)S(1)}, bf16[4,416,256]{2,1,0:T(8,128)(2,1)S(1)}, u32[]{:S(2)}, u32[]{:S(2)}) collective-permute-start(bf16[4,416,256]{2,1,0:T(8,128)(2,1)S(1)} %get-tuple-element.25), channel_id=1, source_target_pairs={{0,192},{64,0},{128,64},{192,128},{1,193},{65,1},{129,65},{193,129... | collective-permute-start | bytes 2555912 | tf_op jit(solution)/shard_map/ppermute | solution.py:466
  105.1 0.0 collective-permute-start.12
  105.1 13.3 %gram.2 = (f32[2,416,256]{2,1,0:T(8,128)S(1)}, f32[2,416,256]{2,1,0:T(8,128)S(1)}, f32[4,416,256]{2,1,0:T(8,128)S(1)}) custom-call(s32[16]{0:T(128)S(1)} %compare_convert_fusion.live_ref, s32[1,128]{1,0:T(1,128)S(1)} %get-tuple-element.34.first_ref, bf16[2,416,256]{2,1,0:T(8,128)(2,1)S(1)} %copy-done.2, bf16[256,64,128]{2,1,0:T(8,128)(2,1)} %copy-done.5, ...), custom_call_target="tpu_custom_call" | custom-call | flops 16000000000 | bytes 20000000 | tf_op jit(solution)/shard_map/gram/pallas_call | solution.py:389
  118.4 2.0 %collective-permute-done.11 = bf16[4,416,256]{2,1,0:T(8,128)(2,1)S(1)} collective-permute-done((bf16[4,416,256]{2,1,0:T(8,128)(2,1)S(1)}, bf16[4,416,256]{2,1,0:T(8,128)(2,1)S(1)}, u32[]{:S(2)}, u32[]{:S(2)}) %collective-permute-start.11) | collective-permute-done | bytes 852000 | tf_op jit(solution)/shard_map/ppermute | solution.py:466
  120.4 0.1 add_convert_fusion
  120.5 3.7 %collective-permute-start.14 = (bf16[2,416,256]{2,1,0:T(8,128)(2,1)S(1)}, bf16[2,416,256]{2,1,0:T(8,128)(2,1)S(1)}, u32[]{:S(2)}, u32[]{:S(2)}) collective-permute-start(bf16[2,416,256]{2,1,0:T(8,128)(2,1)S(1)} %add_convert_fusion), channel_id=1, source_target_pairs={{0,192},{64,0},{128,64},{192,128},{1,193},{65,1},{129,65},{193,129... | collective-permute-start | bytes 1277960 | tf_op jit(solution)/shard_map/ppermute | solution.py:466
  124.2 0.0 collective-permute-done.12
  124.2 0.1 add_convert_fusion.1
  124.3 0.1 collective-permute-start.13
  124.5 0.2 convert_add_fusion.near_any
  124.7 5.1 %collective-permute-done.14.high_any = bf16[2,416,256]{2,1,0:T(8,128)(2,1)S(1)} collective-permute-done((bf16[2,416,256]{2,1,0:T(8,128)(2,1)S(1)}, bf16[2,416,256]{2,1,0:T(8,128)(2,1)S(1)}, u32[]{:S(2)}, u32[]{:S(2)}) %collective-permute-start.14) | collective-permute-done | bytes 426016 | tf_op jit(solution)/shard_map/ppermute | solution.py:466
  129.8 3.9 %collective-permute-done.13.low_any = bf16[2,416,256]{2,1,0:T(8,128)(2,1)S(1)} collective-permute-done((bf16[2,416,256]{2,1,0:T(8,128)(2,1)S(1)}, bf16[2,416,256]{2,1,0:T(8,128)(2,1)S(1)}, u32[]{:S(2)}, u32[]{:S(2)}) %collective-permute-start.13) | collective-permute-done | bytes 426016 | tf_op jit(solution)/shard_map/ppermute | solution.py:466
  133.7 2.6 %final.1 = f32[401,4,256]{2,1,0:T(4,128)} custom-call(f32[4,416,256]{2,1,0:T(8,128)S(1)} %convert_add_fusion.near_any, bf16[2,416,256]{2,1,0:T(8,128)(2,1)S(1)} %collective-permute-done.13.low_any, bf16[2,416,256]{2,1,0:T(8,128)(2,1)S(1)} %collective-permute-done.14.high_any), custom_call_target="tpu_custom_call" | custom-call | flops 10000000 | bytes 7000000 | tf_op jit(solution)/shard_map/final/pallas_call | solution.py:450
  (14 shorter events, 0.1 us)
Async XLA Ops:
  1.1 17.6 %collective-permute-start = (bf16[32,32,256]{2,1,0:T(8,128)(2,1)S(1)}, bf16[32,32,256]{2,1,0:T(8,128)(2,1)S(1)}, u32[]{:S(2)}, u32[]{:S(2)}) collective-permute-start(bf16[32,32,256]{2,1,0:T(8,128)(2,1)S(1)} %slice.38), channel_id=1, source_target_pairs={{0,62},{1,63},{2,0},{3,1},{4,2},{5,3},{6,4},{7,5},{8,6},{9,7},{10,... | collective-permute-start | bytes 1572872 | tf_op jit(solution)/shard_map/ppermute | solution.py:466
  7.5 0.9 copy-start.3
  8.4 17.9 %copy-start.7 = (s32[16,2]{0,1:T(2,128)S(1)}, s32[16,2]{0,1:T(2,128)}, u32[]{:S(2)}) copy-start(s32[16,2]{0,1:T(2,128)} %param.8) | copy-start | bytes 388
  8.4 18.0 %copy-start.8 = (s32[16]{0:T(128)S(1)}, s32[16]{0:T(128)}, u32[]{:S(2)}) copy-start(s32[16]{0:T(128)} %constant.53.clone) | copy-start | bytes 196
  8.4 18.0 %copy-start.9 = (s32[16]{0:T(128)S(1)}, s32[16]{0:T(128)}, u32[]{:S(2)}) copy-start(s32[16]{0:T(128)} %constant.52.clone) | copy-start | bytes 196
  14.0 1.9 %copy-start.5 = (bf16[256,64,128]{2,1,0:T(8,128)(2,1)}, bf16[256,64,128]{2,1,0:T(8,128)(2,1)S(1)}, u32[]{:S(2)}) copy-start(bf16[256,64,128]{2,1,0:T(8,128)(2,1)S(1)} %left.2.refs_0_) | copy-start | bytes 12582916
  15.9 36.0 %copy-start.4 = (bf16[512,256]{1,0:T(8,128)(2,1)S(1)}, bf16[512,256]{1,0:T(8,128)(2,1)}, u32[]{:S(2)}) copy-start(bf16[512,256]{1,0:T(8,128)(2,1)} %constant.54.clone.table_ref) | copy-start | bytes 786436
  18.7 18.2 %collective-permute-start.6 = (bf16[32,32,256]{2,1,0:T(8,128)(2,1)S(1)}, bf16[32,32,256]{2,1,0:T(8,128)(2,1)}, u32[]{:S(2)}, u32[]{:S(2)}) collective-permute-start(bf16[32,32,256]{2,1,0:T(8,128)(2,1)S(1)} %collective-permute-done.a1), channel_id=1, source_target_pairs={{0,62},{1,63},{2,0},{3,1},{4,2},{5,3},{6,4},{7,5},{8,6},{9,7},{10,... | collective-permute-start | bytes 1572872 | tf_op jit(solution)/shard_map/ppermute | solution.py:466
  24.5 21.7 %collective-permute-start.1 = (bf16[64,32,256]{2,1,0:T(8,128)(2,1)}, bf16[64,32,256]{2,1,0:T(8,128)(2,1)S(1)}, u32[]{:S(2)}, u32[]{:S(2)}) collective-permute-start(bf16[64,32,256]{2,1,0:T(8,128)(2,1)} %x0.3), channel_id=1, source_target_pairs={{0,1},{1,0},{2,3},{3,2},{4,5},{5,4},{6,7},{7,6},{8,9},{9,8},{10,11... | collective-permute-start | bytes 3145736 | tf_op jit(solution)/shard_map/ppermute | solution.py:466
  26.3 19.8 %collective-permute-start.3 = (bf16[32,32,256]{2,1,0:T(8,128)(2,1)}, bf16[32,32,256]{2,1,0:T(8,128)(2,1)S(1)}, u32[]{:S(2)}, u32[]{:S(2)}) collective-permute-start(bf16[32,32,256]{2,1,0:T(8,128)(2,1)} %slice.39), channel_id=1, source_target_pairs={{0,62},{1,63},{2,0},{3,1},{4,2},{5,3},{6,4},{7,5},{8,6},{9,7},{10,... | collective-permute-start | bytes 1572872 | tf_op jit(solution)/shard_map/ppermute | solution.py:466
  27.0 24.9 %collective-permute-start.2 = (bf16[32,32,256]{2,1,0:T(8,128)(2,1)S(1)}, bf16[32,32,256]{2,1,0:T(8,128)(2,1)S(1)}, u32[]{:S(2)}, u32[]{:S(2)}) collective-permute-start(bf16[32,32,256]{2,1,0:T(8,128)(2,1)S(1)} %collective-permute-done.a1), channel_id=1, source_target_pairs={{0,1},{1,0},{2,3},{3,2},{4,5},{5,4},{6,7},{7,6},{8,9},{9,8},{10,11... | collective-permute-start | bytes 1572872 | tf_op jit(solution)/shard_map/ppermute | solution.py:466
  36.8 15.1 %collective-permute-start.7 = (bf16[32,32,256]{2,1,0:T(8,128)(2,1)}, bf16[32,32,256]{2,1,0:T(8,128)(2,1)}, u32[]{:S(2)}, u32[]{:S(2)}) collective-permute-start(bf16[32,32,256]{2,1,0:T(8,128)(2,1)} %collective-permute-done.6.a2), channel_id=1, source_target_pairs={{0,1},{1,0},{2,3},{3,2},{4,5},{5,4},{6,7},{7,6},{8,9},{9,8},{10,11... | collective-permute-start | bytes 1572872 | tf_op jit(solution)/shard_map/ppermute | solution.py:466
  37.8 14.1 %collective-permute-start.8 = (bf16[32,16,256]{2,1,0:T(8,128)(2,1)S(1)}, bf16[32,16,256]{2,1,0:T(8,128)(2,1)S(1)}, u32[]{:S(2)}, u32[]{:S(2)}) collective-permute-start(bf16[32,16,256]{2,1,0:T(8,128)(2,1)S(1)} %slice.53), channel_id=1, source_target_pairs={{0,63},{1,0},{2,1},{3,2},{4,3},{5,4},{6,5},{7,6},{8,7},{9,8},{10,9... | collective-permute-start | bytes 786440 | tf_op jit(solution)/shard_map/ppermute | solution.py:466
  46.1 18.8 %collective-permute-start.5 = (bf16[32,32,256]{2,1,0:T(8,128)(2,1)S(1)}, bf16[32,32,256]{2,1,0:T(8,128)(2,1)S(1)}, u32[]{:S(2)}, u32[]{:S(2)}) collective-permute-start(bf16[32,32,256]{2,1,0:T(8,128)(2,1)S(1)} %collective-permute-done.3.a1), channel_id=1, source_target_pairs={{0,1},{1,0},{2,3},{3,2},{4,5},{5,4},{6,7},{7,6},{8,9},{9,8},{10,11... | collective-permute-start | bytes 1572872 | tf_op jit(solution)/shard_map/ppermute | solution.py:466
  46.1 5.8 %copy-start = (bf16[64,32,256]{2,1,0:T(8,128)(2,1)}, bf16[64,32,256]{2,1,0:T(8,128)(2,1)S(1)}, u32[]{:S(2)}) copy-start(bf16[64,32,256]{2,1,0:T(8,128)(2,1)S(1)} %collective-permute-done.1.b0.refs_0_) | copy-start | bytes 3145732
  46.1 18.8 %collective-permute-start.4 = (bf16[32,32,256]{2,1,0:T(8,128)(2,1)S(1)}, bf16[32,32,256]{2,1,0:T(8,128)(2,1)S(1)}, u32[]{:S(2)}, u32[]{:S(2)}) collective-permute-start(bf16[32,32,256]{2,1,0:T(8,128)(2,1)S(1)} %collective-permute-done.3.a1), channel_id=1, source_target_pairs={{0,62},{1,63},{2,0},{3,1},{4,2},{5,3},{6,4},{7,5},{8,6},{9,7},{10,... | collective-permute-start | bytes 1572872 | tf_op jit(solution)/shard_map/ppermute | solution.py:466
  64.9 11.6 %copy-start.6 = (bf16[32,32,256]{2,1,0:T(8,128)(2,1)}, bf16[32,32,256]{2,1,0:T(8,128)(2,1)S(1)}, u32[]{:S(2)}) copy-start(bf16[32,32,256]{2,1,0:T(8,128)(2,1)S(1)} %collective-permute-done.4.a2) | copy-start | bytes 1572868
  64.9 11.6 %collective-permute-start.9 = (bf16[32,32,256]{2,1,0:T(8,128)(2,1)S(1)}, bf16[32,32,256]{2,1,0:T(8,128)(2,1)S(1)}, u32[]{:S(2)}, u32[]{:S(2)}) collective-permute-start(bf16[32,32,256]{2,1,0:T(8,128)(2,1)S(1)} %collective-permute-done.4.a2), channel_id=1, source_target_pairs={{0,1},{1,0},{2,3},{3,2},{4,5},{5,4},{6,7},{7,6},{8,9},{9,8},{10,11... | collective-permute-start | bytes 1572872 | tf_op jit(solution)/shard_map/ppermute | solution.py:466
  65.1 11.4 %collective-permute-start.10 = (bf16[32,16,256]{2,1,0:T(8,128)(2,1)S(1)}, bf16[32,16,256]{2,1,0:T(8,128)(2,1)S(1)}, u32[]{:S(2)}, u32[]{:S(2)}) collective-permute-start(bf16[32,16,256]{2,1,0:T(8,128)(2,1)S(1)} %slice.42), channel_id=1, source_target_pairs={{0,63},{1,0},{2,1},{3,2},{4,3},{5,4},{6,5},{7,6},{8,7},{9,8},{10,9... | collective-permute-start | bytes 786440 | tf_op jit(solution)/shard_map/ppermute | solution.py:466
  69.7 1.2 copy-start.1
  76.5 13.7 %copy-start.2 = (bf16[2,416,256]{2,1,0:T(8,128)(2,1)S(1)}, bf16[2,416,256]{2,1,0:T(8,128)(2,1)}, u32[]{:S(2)}) copy-start(bf16[2,416,256]{2,1,0:T(8,128)(2,1)} %constant.55.clone.table_ref) | copy-start | bytes 1277956
  76.6 0.8 copy-start.10
  101.8 18.6 %collective-permute-start.11 = (bf16[4,416,256]{2,1,0:T(8,128)(2,1)S(1)}, bf16[4,416,256]{2,1,0:T(8,128)(2,1)S(1)}, u32[]{:S(2)}, u32[]{:S(2)}) collective-permute-start(bf16[4,416,256]{2,1,0:T(8,128)(2,1)S(1)} %get-tuple-element.25), channel_id=1, source_target_pairs={{0,192},{64,0},{128,64},{192,128},{1,193},{65,1},{129,65},{193,129... | collective-permute-start | bytes 2555912 | tf_op jit(solution)/shard_map/ppermute | solution.py:466
  105.1 19.1 %collective-permute-start.12 = (bf16[4,416,256]{2,1,0:T(8,128)(2,1)S(1)}, bf16[4,416,256]{2,1,0:T(8,128)(2,1)S(1)}, u32[]{:S(2)}, u32[]{:S(2)}) collective-permute-start(bf16[4,416,256]{2,1,0:T(8,128)(2,1)S(1)} %get-tuple-element.26), channel_id=1, source_target_pairs={{0,64},{64,128},{128,192},{192,0},{1,65},{65,129},{129,193},{193,1... | collective-permute-start | bytes 2555912 | tf_op jit(solution)/shard_map/ppermute | solution.py:466
  120.5 9.3 %collective-permute-start.14 = (bf16[2,416,256]{2,1,0:T(8,128)(2,1)S(1)}, bf16[2,416,256]{2,1,0:T(8,128)(2,1)S(1)}, u32[]{:S(2)}, u32[]{:S(2)}) collective-permute-start(bf16[2,416,256]{2,1,0:T(8,128)(2,1)S(1)} %add_convert_fusion), channel_id=1, source_target_pairs={{0,192},{64,0},{128,64},{192,128},{1,193},{65,1},{129,65},{193,129... | collective-permute-start | bytes 1277960 | tf_op jit(solution)/shard_map/ppermute | solution.py:466
  124.3 9.4 %collective-permute-start.13 = (bf16[2,416,256]{2,1,0:T(8,128)(2,1)S(1)}, bf16[2,416,256]{2,1,0:T(8,128)(2,1)S(1)}, u32[]{:S(2)}, u32[]{:S(2)}) collective-permute-start(bf16[2,416,256]{2,1,0:T(8,128)(2,1)S(1)} %add_convert_fusion.1), channel_id=1, source_target_pairs={{0,64},{64,128},{128,192},{192,0},{1,65},{65,129},{129,193},{193,1... | collective-permute-start | bytes 1277960 | tf_op jit(solution)/shard_map/ppermute | solution.py:466

commit v9 on v7

--- a/solution.py
+++ b/solution.py
@@ -277,7 +277,7 @@
             pltpu.SemaphoreType.DMA((len(pieces),)),
         ]
         + [pltpu.VMEM(p.shape, p.dtype) for p in pieces],
-        compiler_params=pltpu.CompilerParams(vmem_limit_bytes=48 * MIB),
+        compiler_params=pltpu.CompilerParams(vmem_limit_bytes=58 * MIB),
         cost_estimate=pl.CostEstimate(flops=4_000_000_000, bytes_accessed=8_000_000, transcendentals=0),
         name="left",
     )(odd, table, *pieces)

time: 137 us -> 140 us (1.022)
  Pallas kernels: 64 us -> 68.3 us
  local copies, waits for them, and re-layouts: 9.72 us -> 5.63 us
  waiting for transfers between devices: 24.2 us -> 26.2 us
    pallas_call x2, Pallas kernels: 10.9 us -> 15.2 us  [left_bins(): pl.pallas_call(left_kernel, out_shape=jax.ShapeDtypeStruct(shape, jnp.bfl...]
    unnamed x23 -> x25, local copies, waits for them, and re-layouts: 5.01 us -> 1.96 us
    ppermute x15, waiting for transfers between devices: 24.2 us -> 26.2 us  [moved(): return lax.ppermute(block, axis, [(i, to(i) % size) for i in range(size)])]
  transfers between devices with their start and end apart: 15 -> 15, of which waited for: 6 -> 6; matrix products, arithmetic and copies ran while one was open for 3% -> 2% of each run, Pallas kernels for 27% -> 30%
where the time goes in v9:
time: 140 us; the launch traced here: 138 us
  Pallas kernels  68.3 us (49%)
  starting transfers between devices  36.5 us (26%)
  waiting for transfers between devices  26.2 us (19%)
  local copies, waits for them, and re-layouts  5.63 us (4%)
    ppermute x15, starting transfers between devices, moved(): return lax.ppermute(block, axis, [(i, to(i) % size) for i in range(size)])  36.5 us
    ppermute x15, waiting for transfers between devices, moved(): return lax.ppermute(block, axis, [(i, to(i) % size) for i in range(size)])  26.2 us
    pallas_call x2, Pallas kernels, whiten_bins(): pl.pallas_call(functools.partial(whiten_kernel, chunk), out_shape=jax.Sha...  25.5 us
    pallas_call x2, Pallas kernels, gram(): pl.pallas_call(functools.partial(gram_kernel, tile), out_shape=[jax.Shape...  24.9 us
    pallas_call x2, Pallas kernels, left_bins(): pl.pallas_call(left_kernel, out_shape=jax.ShapeDtypeStruct(shape, jnp.bfl...  15.2 us
  transfers between devices with their start and end apart: 15, of which 6 were waited for; matrix products, arithmetic and copies ran while one was open for 2% of the time, Pallas kernels for 30%

profile of v9, /device:TPU:0, one launch (start us, length us, event | category | flops | bytes accessed | tf_op | source)
XLA Modules:
  0.0 138.4 jit_solution(16452170527398258890)
XLA Ops:
  0.0 1.1 slice.38
  1.1 6.4 %collective-permute-start = (bf16[32,32,256]{2,1,0:T(8,128)(2,1)S(1)}, bf16[32,32,256]{2,1,0:T(8,128)(2,1)S(1)}, u32[]{:S(2)}, u32[]{:S(2)}) collective-permute-start(bf16[32,32,256]{2,1,0:T(8,128)(2,1)S(1)} %slice.38), channel_id=1, source_target_pairs={{0,62},{1,63},{2,0},{3,1},{4,2},{5,3},{6,4},{7,5},{8,6},{9,7},{10,... | collective-permute-start | bytes 1572872 | tf_op jit(solution)/shard_map/ppermute | solution.py:462
  7.5 7.4 %left.2.refs_0_ = bf16[256,64,128]{2,1,0:T(8,128)(2,1)} custom-call(s32[1]{0:T(128)} %bitcast.1.odd_ref, bf16[512,256]{1,0:T(8,128)(2,1)} %constant.54.clone.table_ref, bf16[64,32,256]{2,1,0:T(8,128)(2,1)} %x0.3), custom_call_target="tpu_custom_call" | custom-call | flops 4000000000 | bytes 8000000 | tf_op jit(solution)/shard_map/left/pallas_call | solution.py:265
  14.9 0.0 copy-start.4
  14.9 3.8 %collective-permute-done.a1 = bf16[32,32,256]{2,1,0:T(8,128)(2,1)S(1)} collective-permute-done((bf16[32,32,256]{2,1,0:T(8,128)(2,1)S(1)}, bf16[32,32,256]{2,1,0:T(8,128)(2,1)S(1)}, u32[]{:S(2)}, u32[]{:S(2)}) %collective-permute-start) | collective-permute-done | bytes 524320 | tf_op jit(solution)/shard_map/ppermute | solution.py:462
  18.7 5.8 %collective-permute-start.6 = (bf16[32,32,256]{2,1,0:T(8,128)(2,1)S(1)}, bf16[32,32,256]{2,1,0:T(8,128)(2,1)}, u32[]{:S(2)}, u32[]{:S(2)}) collective-permute-start(bf16[32,32,256]{2,1,0:T(8,128)(2,1)S(1)} %collective-permute-done.a1), channel_id=1, source_target_pairs={{0,62},{1,63},{2,0},{3,1},{4,2},{5,3},{6,4},{7,5},{8,6},{9,7},{10,... | collective-permute-start | bytes 1572872 | tf_op jit(solution)/shard_map/ppermute | solution.py:462
  24.5 0.0 copy-done.6
  24.5 0.0 collective-permute-start.1
  24.5 0.8 slice.39
  25.3 0.0 collective-permute-start.3
  25.3 0.0 copy-done.8
  25.3 0.1 copy.9
  25.4 0.0 copy-done.9
  25.4 0.0 copy-done.10
  25.4 0.6 gather_fusion
  26.0 0.6 collective-permute-start.2
  26.6 10.3 %collective-permute-done.6.a2 = bf16[32,32,256]{2,1,0:T(8,128)(2,1)} collective-permute-done((bf16[32,32,256]{2,1,0:T(8,128)(2,1)S(1)}, bf16[32,32,256]{2,1,0:T(8,128)(2,1)}, u32[]{:S(2)}, u32[]{:S(2)}) %collective-permute-start.6) | collective-permute-done | bytes 524320 | tf_op jit(solution)/shard_map/ppermute | solution.py:462
  36.8 0.0 collective-permute-start.7
  36.8 1.0 slice.53
  37.8 6.1 %collective-permute-start.8 = (bf16[32,16,256]{2,1,0:T(8,128)(2,1)S(1)}, bf16[32,16,256]{2,1,0:T(8,128)(2,1)S(1)}, u32[]{:S(2)}, u32[]{:S(2)}) collective-permute-start(bf16[32,16,256]{2,1,0:T(8,128)(2,1)S(1)} %slice.53), channel_id=1, source_target_pairs={{0,63},{1,0},{2,1},{3,2},{4,3},{5,4},{6,5},{7,6},{8,7},{9,8},{10,9... | collective-permute-start | bytes 786440 | tf_op jit(solution)/shard_map/ppermute | solution.py:462
  43.9 0.2 fusion
  44.7 0.1 broadcast_in_dim.10
  44.8 0.1 broadcast_in_dim_reshape.3
  44.9 1.2 collective-permute-done.3.a1
  46.1 0.0 collective-permute-start.5
  46.1 0.0 collective-permute-done.1.b0.refs_0_
  46.1 5.7 %collective-permute-start.4 = (bf16[32,32,256]{2,1,0:T(8,128)(2,1)S(1)}, bf16[32,32,256]{2,1,0:T(8,128)(2,1)S(1)}, u32[]{:S(2)}, u32[]{:S(2)}) collective-permute-start(bf16[32,32,256]{2,1,0:T(8,128)(2,1)S(1)} %collective-permute-done.3.a1), channel_id=1, source_target_pairs={{0,62},{1,63},{2,0},{3,1},{4,2},{5,3},{6,4},{7,5},{8,6},{9,7},{10,... | collective-permute-start | bytes 1572872 | tf_op jit(solution)/shard_map/ppermute | solution.py:462
  51.8 0.0 collective-permute-done.2.b1.refs_1_
  51.8 0.0 collective-permute-done.8.o5
  51.8 0.0 collective-permute-done.7.b2
  51.8 0.0 copy-done.4
  51.8 12.8 %whiten.2.refs_2_ = bf16[2,256,64,128]{3,2,1,0:T(8,128)(2,1)} custom-call(s32[16]{0:T(128)S(1)} %get-tuple-element.29.right_ref, s32[1]{0:T(128)} %bitcast.1.odd_ref, bf16[512,256]{1,0:T(8,128)(2,1)S(1)} %copy-done.4, bf16[64,32,256]{2,1,0:T(8,128)(2,1)} %x0.3, bf16[64,32,256]{2,1,0:T(8,128)(2,1)} %collective-permute-done.1.b0.refs_0_, ...), custom_call_target="tpu_custom_call" | custom-call | flops 7680000000 | bytes 8000000 | tf_op jit(solution)/shard_map/whiten/pallas_call | solution.py:156
  64.7 0.0 copy-done
  64.7 0.0 collective-permute-done.5.refs_2_.b1
  64.7 0.0 copy-start.1
  64.7 0.0 collective-permute-done.4.a2
  64.7 0.0 copy-start.7
  64.7 0.3 collective-permute-start.9
  65.0 0.0 copy-start.5
  65.0 4.7 %collective-permute-start.10 = (bf16[32,16,256]{2,1,0:T(8,128)(2,1)S(1)}, bf16[32,16,256]{2,1,0:T(8,128)(2,1)S(1)}, u32[]{:S(2)}, u32[]{:S(2)}) collective-permute-start(bf16[32,16,256]{2,1,0:T(8,128)(2,1)S(1)} %slice.42), channel_id=1, source_target_pairs={{0,63},{1,0},{2,1},{3,2},{4,3},{5,4},{6,5},{7,6},{8,7},{9,8},{10,9... | collective-permute-start | bytes 786440 | tf_op jit(solution)/shard_map/ppermute | solution.py:462
  69.7 0.0 copy-done.1
  69.7 7.8 %left.3.refs_1_ = bf16[256,64,128]{2,1,0:T(8,128)(2,1)} custom-call(s32[1]{0:T(128)} %bitcast.1.odd_ref, bf16[512,256]{1,0:T(8,128)(2,1)} %constant.54.clone.table_ref, bf16[64,32,256]{2,1,0:T(8,128)(2,1)} %collective-permute-done.1.b0.refs_0_, bf16[32,32,256]{2,1,0:T(8,128)(2,1)} %copy-done, bf16[32,32,256]{2,1,0:T(8,128)(2,1)} %copy-done.1), custom_call_target="tpu_custom_call" | custom-call | flops 4000000000 | bytes 8000000 | tf_op jit(solution)/shard_map/left/pallas_call | solution.py:265
  77.5 0.0 copy-done.7
  77.5 0.0 collective-permute-done.10.o5
  77.6 0.0 collective-permute-done.9.b2
  77.6 0.0 copy-start.11
  77.6 0.8 copy-done.11
  78.4 0.0 copy-done.5
  78.4 1.0 copy-done.2
  79.4 12.7 %whiten.3.refs_3_ = bf16[2,256,64,128]{3,2,1,0:T(8,128)(2,1)} custom-call(s32[16]{0:T(128)S(1)} %get-tuple-element.29.right_ref, s32[1]{0:T(128)} %bitcast.1.odd_ref, bf16[512,256]{1,0:T(8,128)(2,1)S(1)} %copy-done.5, bf16[64,32,256]{2,1,0:T(8,128)(2,1)} %x0.3, bf16[64,32,256]{2,1,0:T(8,128)(2,1)} %collective-permute-done.1.b0.refs_0_, ...), custom_call_target="tpu_custom_call" | custom-call | flops 7680000000 | bytes 8000000 | tf_op jit(solution)/shard_map/whiten/pallas_call | solution.py:156
  92.1 11.6 %gram.3 = (bf16[4,416,256]{2,1,0:T(8,128)(2,1)S(1)}, bf16[4,416,256]{2,1,0:T(8,128)(2,1)S(1)}) custom-call(s32[16]{0:T(128)S(1)} %compare_convert_fusion.live_ref, s32[1,128]{1,0:T(1,128)S(1)} %get-tuple-element.33.first_ref, bf16[2,416,256]{2,1,0:T(8,128)(2,1)S(1)} %copy-done.3, bf16[256,64,128]{2,1,0:T(8,128)(2,1)} %left.2.refs_0_, ...), custom_call_target="tpu_custom_call" | custom-call | flops 16000000000 | bytes 20000000 | tf_op jit(solution)/shard_map/gram/pallas_call | solution.py:385
  103.7 3.3 %collective-permute-start.11 = (bf16[4,416,256]{2,1,0:T(8,128)(2,1)S(1)}, bf16[4,416,256]{2,1,0:T(8,128)(2,1)S(1)}, u32[]{:S(2)}, u32[]{:S(2)}) collective-permute-start(bf16[4,416,256]{2,1,0:T(8,128)(2,1)S(1)} %get-tuple-element.25), channel_id=1, source_target_pairs={{0,192},{64,0},{128,64},{192,128},{1,193},{65,1},{129,65},{193,129... | collective-permute-start | bytes 2555912 | tf_op jit(solution)/shard_map/ppermute | solution.py:462
  107.0 0.0 collective-permute-start.12
  107.0 13.4 %gram.2 = (f32[2,416,256]{2,1,0:T(8,128)S(1)}, f32[2,416,256]{2,1,0:T(8,128)S(1)}, f32[4,416,256]{2,1,0:T(8,128)S(1)}) custom-call(s32[16]{0:T(128)S(1)} %compare_convert_fusion.live_ref, s32[1,128]{1,0:T(1,128)S(1)} %get-tuple-element.34.first_ref, bf16[2,416,256]{2,1,0:T(8,128)(2,1)S(1)} %copy-done.3, bf16[256,64,128]{2,1,0:T(8,128)(2,1)} %left.2.refs_0_, ...), custom_call_target="tpu_custom_call" | custom-call | flops 16000000000 | bytes 20000000 | tf_op jit(solution)/shard_map/gram/pallas_call | solution.py:385
  120.4 2.0 %collective-permute-done.11 = bf16[4,416,256]{2,1,0:T(8,128)(2,1)S(1)} collective-permute-done((bf16[4,416,256]{2,1,0:T(8,128)(2,1)S(1)}, bf16[4,416,256]{2,1,0:T(8,128)(2,1)S(1)}, u32[]{:S(2)}, u32[]{:S(2)}) %collective-permute-start.11) | collective-permute-done | bytes 852000 | tf_op jit(solution)/shard_map/ppermute | solution.py:462
  122.3 0.1 add_convert_fusion
  122.5 3.6 %collective-permute-start.14 = (bf16[2,416,256]{2,1,0:T(8,128)(2,1)S(1)}, bf16[2,416,256]{2,1,0:T(8,128)(2,1)S(1)}, u32[]{:S(2)}, u32[]{:S(2)}) collective-permute-start(bf16[2,416,256]{2,1,0:T(8,128)(2,1)S(1)} %add_convert_fusion), channel_id=1, source_target_pairs={{0,192},{64,0},{128,64},{192,128},{1,193},{65,1},{129,65},{193,129... | collective-permute-start | bytes 1277960 | tf_op jit(solution)/shard_map/ppermute | solution.py:462
  126.1 0.0 collective-permute-done.12
  126.1 0.1 add_convert_fusion.1
  126.2 0.1 collective-permute-start.13
  126.4 0.2 convert_add_fusion.near_any
  126.6 5.1 %collective-permute-done.14.high_any = bf16[2,416,256]{2,1,0:T(8,128)(2,1)S(1)} collective-permute-done((bf16[2,416,256]{2,1,0:T(8,128)(2,1)S(1)}, bf16[2,416,256]{2,1,0:T(8,128)(2,1)S(1)}, u32[]{:S(2)}, u32[]{:S(2)}) %collective-permute-start.14) | collective-permute-done | bytes 426016 | tf_op jit(solution)/shard_map/ppermute | solution.py:462
  131.7 3.9 %collective-permute-done.13.low_any = bf16[2,416,256]{2,1,0:T(8,128)(2,1)S(1)} collective-permute-done((bf16[2,416,256]{2,1,0:T(8,128)(2,1)S(1)}, bf16[2,416,256]{2,1,0:T(8,128)(2,1)S(1)}, u32[]{:S(2)}, u32[]{:S(2)}) %collective-permute-start.13) | collective-permute-done | bytes 426016 | tf_op jit(solution)/shard_map/ppermute | solution.py:462
  135.6 2.6 %final.1 = f32[401,4,256]{2,1,0:T(4,128)} custom-call(f32[4,416,256]{2,1,0:T(8,128)S(1)} %convert_add_fusion.near_any, bf16[2,416,256]{2,1,0:T(8,128)(2,1)S(1)} %collective-permute-done.13.low_any, bf16[2,416,256]{2,1,0:T(8,128)(2,1)S(1)} %collective-permute-done.14.high_any), custom_call_target="tpu_custom_call" | custom-call | flops 10000000 | bytes 7000000 | tf_op jit(solution)/shard_map/final/pallas_call | solution.py:446
  (16 shorter events, 0.1 us)
Async XLA Ops:
  1.1 17.6 %collective-permute-start = (bf16[32,32,256]{2,1,0:T(8,128)(2,1)S(1)}, bf16[32,32,256]{2,1,0:T(8,128)(2,1)S(1)}, u32[]{:S(2)}, u32[]{:S(2)}) collective-permute-start(bf16[32,32,256]{2,1,0:T(8,128)(2,1)S(1)} %slice.38), channel_id=1, source_target_pairs={{0,62},{1,63},{2,0},{3,1},{4,2},{5,3},{6,4},{7,5},{8,6},{9,7},{10,... | collective-permute-start | bytes 1572872 | tf_op jit(solution)/shard_map/ppermute | solution.py:462
  7.5 17.0 %copy-start.6 = (bf16[64,32,256]{2,1,0:T(8,128)(2,1)S(1)}, bf16[64,32,256]{2,1,0:T(8,128)(2,1)}, u32[]{:S(2)}) copy-start(bf16[64,32,256]{2,1,0:T(8,128)(2,1)} %x0.3) | copy-start | bytes 3145732
  7.5 17.8 %copy-start.8 = (s32[16,2]{0,1:T(2,128)S(1)}, s32[16,2]{0,1:T(2,128)}, u32[]{:S(2)}) copy-start(s32[16,2]{0,1:T(2,128)} %param.8) | copy-start | bytes 388
  7.5 17.9 %copy-start.9 = (s32[16]{0:T(128)S(1)}, s32[16]{0:T(128)}, u32[]{:S(2)}) copy-start(s32[16]{0:T(128)} %constant.53.clone) | copy-start | bytes 196
  7.5 17.9 %copy-start.10 = (s32[16]{0:T(128)S(1)}, s32[16]{0:T(128)}, u32[]{:S(2)}) copy-start(s32[16]{0:T(128)} %constant.52.clone) | copy-start | bytes 196
  14.9 36.9 %copy-start.4 = (bf16[512,256]{1,0:T(8,128)(2,1)S(1)}, bf16[512,256]{1,0:T(8,128)(2,1)}, u32[]{:S(2)}) copy-start(bf16[512,256]{1,0:T(8,128)(2,1)} %constant.54.clone.table_ref) | copy-start | bytes 786436
  18.7 18.2 %collective-permute-start.6 = (bf16[32,32,256]{2,1,0:T(8,128)(2,1)S(1)}, bf16[32,32,256]{2,1,0:T(8,128)(2,1)}, u32[]{:S(2)}, u32[]{:S(2)}) collective-permute-start(bf16[32,32,256]{2,1,0:T(8,128)(2,1)S(1)} %collective-permute-done.a1), channel_id=1, source_target_pairs={{0,62},{1,63},{2,0},{3,1},{4,2},{5,3},{6,4},{7,5},{8,6},{9,7},{10,... | collective-permute-start | bytes 1572872 | tf_op jit(solution)/shard_map/ppermute | solution.py:462
  24.5 21.7 %collective-permute-start.1 = (bf16[64,32,256]{2,1,0:T(8,128)(2,1)S(1)}, bf16[64,32,256]{2,1,0:T(8,128)(2,1)}, u32[]{:S(2)}, u32[]{:S(2)}) collective-permute-start(bf16[64,32,256]{2,1,0:T(8,128)(2,1)S(1)} %copy-done.6), channel_id=1, source_target_pairs={{0,1},{1,0},{2,3},{3,2},{4,5},{5,4},{6,7},{7,6},{8,9},{9,8},{10,11... | collective-permute-start | bytes 3145736 | tf_op jit(solution)/shard_map/ppermute | solution.py:462
  25.3 20.8 %collective-permute-start.3 = (bf16[32,32,256]{2,1,0:T(8,128)(2,1)}, bf16[32,32,256]{2,1,0:T(8,128)(2,1)S(1)}, u32[]{:S(2)}, u32[]{:S(2)}) collective-permute-start(bf16[32,32,256]{2,1,0:T(8,128)(2,1)} %slice.39), channel_id=1, source_target_pairs={{0,62},{1,63},{2,0},{3,1},{4,2},{5,3},{6,4},{7,5},{8,6},{9,7},{10,... | collective-permute-start | bytes 1572872 | tf_op jit(solution)/shard_map/ppermute | solution.py:462
  26.0 25.8 %collective-permute-start.2 = (bf16[32,32,256]{2,1,0:T(8,128)(2,1)S(1)}, bf16[32,32,256]{2,1,0:T(8,128)(2,1)S(1)}, u32[]{:S(2)}, u32[]{:S(2)}) collective-permute-start(bf16[32,32,256]{2,1,0:T(8,128)(2,1)S(1)} %collective-permute-done.a1), channel_id=1, source_target_pairs={{0,1},{1,0},{2,3},{3,2},{4,5},{5,4},{6,7},{7,6},{8,9},{9,8},{10,11... | collective-permute-start | bytes 1572872 | tf_op jit(solution)/shard_map/ppermute | solution.py:462
  36.8 15.0 %collective-permute-start.7 = (bf16[32,32,256]{2,1,0:T(8,128)(2,1)}, bf16[32,32,256]{2,1,0:T(8,128)(2,1)}, u32[]{:S(2)}, u32[]{:S(2)}) collective-permute-start(bf16[32,32,256]{2,1,0:T(8,128)(2,1)} %collective-permute-done.6.a2), channel_id=1, source_target_pairs={{0,1},{1,0},{2,3},{3,2},{4,5},{5,4},{6,7},{7,6},{8,9},{9,8},{10,11... | collective-permute-start | bytes 1572872 | tf_op jit(solution)/shard_map/ppermute | solution.py:462
  37.8 14.0 %collective-permute-start.8 = (bf16[32,16,256]{2,1,0:T(8,128)(2,1)S(1)}, bf16[32,16,256]{2,1,0:T(8,128)(2,1)S(1)}, u32[]{:S(2)}, u32[]{:S(2)}) collective-permute-start(bf16[32,16,256]{2,1,0:T(8,128)(2,1)S(1)} %slice.53), channel_id=1, source_target_pairs={{0,63},{1,0},{2,1},{3,2},{4,3},{5,4},{6,5},{7,6},{8,7},{9,8},{10,9... | collective-permute-start | bytes 786440 | tf_op jit(solution)/shard_map/ppermute | solution.py:462
  46.1 18.6 %collective-permute-start.5 = (bf16[32,32,256]{2,1,0:T(8,128)(2,1)S(1)}, bf16[32,32,256]{2,1,0:T(8,128)(2,1)S(1)}, u32[]{:S(2)}, u32[]{:S(2)}) collective-permute-start(bf16[32,32,256]{2,1,0:T(8,128)(2,1)S(1)} %collective-permute-done.3.a1), channel_id=1, source_target_pairs={{0,1},{1,0},{2,3},{3,2},{4,5},{5,4},{6,7},{7,6},{8,9},{9,8},{10,11... | collective-permute-start | bytes 1572872 | tf_op jit(solution)/shard_map/ppermute | solution.py:462
  46.1 18.6 %collective-permute-start.4 = (bf16[32,32,256]{2,1,0:T(8,128)(2,1)S(1)}, bf16[32,32,256]{2,1,0:T(8,128)(2,1)S(1)}, u32[]{:S(2)}, u32[]{:S(2)}) collective-permute-start(bf16[32,32,256]{2,1,0:T(8,128)(2,1)S(1)} %collective-permute-done.3.a1), channel_id=1, source_target_pairs={{0,62},{1,63},{2,0},{3,1},{4,2},{5,3},{6,4},{7,5},{8,6},{9,7},{10,... | collective-permute-start | bytes 1572872 | tf_op jit(solution)/shard_map/ppermute | solution.py:462
  51.8 12.9 %copy-start = (bf16[32,32,256]{2,1,0:T(8,128)(2,1)}, bf16[32,32,256]{2,1,0:T(8,128)(2,1)S(1)}, u32[]{:S(2)}) copy-start(bf16[32,32,256]{2,1,0:T(8,128)(2,1)S(1)} %collective-permute-done.2.b1.refs_1_) | copy-start | bytes 1572868
  64.7 5.0 %copy-start.1 = (bf16[32,32,256]{2,1,0:T(8,128)(2,1)}, bf16[32,32,256]{2,1,0:T(8,128)(2,1)S(1)}, u32[]{:S(2)}) copy-start(bf16[32,32,256]{2,1,0:T(8,128)(2,1)S(1)} %collective-permute-done.5.refs_2_.b1) | copy-start | bytes 1572868
  64.7 12.8 %copy-start.7 = (bf16[32,32,256]{2,1,0:T(8,128)(2,1)}, bf16[32,32,256]{2,1,0:T(8,128)(2,1)S(1)}, u32[]{:S(2)}) copy-start(bf16[32,32,256]{2,1,0:T(8,128)(2,1)S(1)} %collective-permute-done.4.a2) | copy-start | bytes 1572868
  64.7 12.8 %collective-permute-start.9 = (bf16[32,32,256]{2,1,0:T(8,128)(2,1)S(1)}, bf16[32,32,256]{2,1,0:T(8,128)(2,1)S(1)}, u32[]{:S(2)}, u32[]{:S(2)}) collective-permute-start(bf16[32,32,256]{2,1,0:T(8,128)(2,1)S(1)} %collective-permute-done.4.a2), channel_id=1, source_target_pairs={{0,1},{1,0},{2,3},{3,2},{4,5},{5,4},{6,7},{7,6},{8,9},{9,8},{10,11... | collective-permute-start | bytes 1572872 | tf_op jit(solution)/shard_map/ppermute | solution.py:462
  65.0 13.4 %copy-start.5 = (bf16[512,256]{1,0:T(8,128)(2,1)S(1)}, bf16[512,256]{1,0:T(8,128)(2,1)}, u32[]{:S(2)}) copy-start(bf16[512,256]{1,0:T(8,128)(2,1)} %constant.54.clone.table_ref) | copy-start | bytes 786436
  65.0 12.5 %collective-permute-start.10 = (bf16[32,16,256]{2,1,0:T(8,128)(2,1)S(1)}, bf16[32,16,256]{2,1,0:T(8,128)(2,1)S(1)}, u32[]{:S(2)}, u32[]{:S(2)}) collective-permute-start(bf16[32,16,256]{2,1,0:T(8,128)(2,1)S(1)} %slice.42), channel_id=1, source_target_pairs={{0,63},{1,0},{2,1},{3,2},{4,3},{5,4},{6,5},{7,6},{8,7},{9,8},{10,9... | collective-permute-start | bytes 786440 | tf_op jit(solution)/shard_map/ppermute | solution.py:462
  69.7 22.4 %copy-start.3 = (bf16[2,416,256]{2,1,0:T(8,128)(2,1)S(1)}, bf16[2,416,256]{2,1,0:T(8,128)(2,1)}, u32[]{:S(2)}) copy-start(bf16[2,416,256]{2,1,0:T(8,128)(2,1)} %constant.55.clone.table_ref) | copy-start | bytes 1277956
  77.6 0.8 copy-start.11
  78.4 1.0 copy-start.2
  103.7 18.6 %collective-permute-start.11 = (bf16[4,416,256]{2,1,0:T(8,128)(2,1)S(1)}, bf16[4,416,256]{2,1,0:T(8,128)(2,1)S(1)}, u32[]{:S(2)}, u32[]{:S(2)}) collective-permute-start(bf16[4,416,256]{2,1,0:T(8,128)(2,1)S(1)} %get-tuple-element.25), channel_id=1, source_target_pairs={{0,192},{64,0},{128,64},{192,128},{1,193},{65,1},{129,65},{193,129... | collective-permute-start | bytes 2555912 | tf_op jit(solution)/shard_map/ppermute | solution.py:462
  107.0 19.1 %collective-permute-start.12 = (bf16[4,416,256]{2,1,0:T(8,128)(2,1)S(1)}, bf16[4,416,256]{2,1,0:T(8,128)(2,1)S(1)}, u32[]{:S(2)}, u32[]{:S(2)}) collective-permute-start(bf16[4,416,256]{2,1,0:T(8,128)(2,1)S(1)} %get-tuple-element.26), channel_id=1, source_target_pairs={{0,64},{64,128},{128,192},{192,0},{1,65},{65,129},{129,193},{193,1... | collective-permute-start | bytes 2555912 | tf_op jit(solution)/shard_map/ppermute | solution.py:462
  122.5 9.3 %collective-permute-start.14 = (bf16[2,416,256]{2,1,0:T(8,128)(2,1)S(1)}, bf16[2,416,256]{2,1,0:T(8,128)(2,1)S(1)}, u32[]{:S(2)}, u32[]{:S(2)}) collective-permute-start(bf16[2,416,256]{2,1,0:T(8,128)(2,1)S(1)} %add_convert_fusion), channel_id=1, source_target_pairs={{0,192},{64,0},{128,64},{192,128},{1,193},{65,1},{129,65},{193,129... | collective-permute-start | bytes 1277960 | tf_op jit(solution)/shard_map/ppermute | solution.py:462
  126.2 9.4 %collective-permute-start.13 = (bf16[2,416,256]{2,1,0:T(8,128)(2,1)S(1)}, bf16[2,416,256]{2,1,0:T(8,128)(2,1)S(1)}, u32[]{:S(2)}, u32[]{:S(2)}) collective-permute-start(bf16[2,416,256]{2,1,0:T(8,128)(2,1)S(1)} %add_convert_fusion.1), channel_id=1, source_target_pairs={{0,64},{64,128},{128,192},{192,0},{1,65},{65,129},{129,193},{193,1... | collective-permute-start | bytes 1277960 | tf_op jit(solution)/shard_map/ppermute | solution.py:462
